TPU v7x, 32 devices: a whole 2x2x4 slice. The times are simulated.
32 devices in a mesh: dp: 16 (over z, y, core), vocab: 2 (over x).
Axes of the slice: x: 2, y: 2, z: 4, core: 2. Of those that a mesh axis runs over, the one named last changes fastest.
Arguments:
- audio_codes: int32 [64, 4, 128], P('dp'), may hold values from 0 to 2047
- delay_offsets: int32 [64, 4], P('dp'), may hold values from 0 to 3
- clip_lengths: int32 [64], P('dp'), may hold values from 64 to 128
- loss_positions: int32 [64, 32], P('dp'), may hold values from 0 to 127
- teacher_ids: int32 [64, 4, 32, 64], P('dp'), may hold values from 0 to 2047
- text_states: bfloat16 [64, 64, 1024], P(('dp', 'vocab')), may hold values from -6 to 6
- step_count: int32 [], replicated, may hold values from 1 to 20
- in_proj: float32 [6, 1024, 1024], P(None, ('dp', 'vocab')), may hold values from -0.1875 to 0.1875
- in_proj_mean: float32 [6, 1024, 1024], P(None, ('dp', 'vocab')), may hold values from -0.0008544922 to 0.0008544922
- in_proj_sq: float32 [6, 1024, 1024], P(None, ('dp', 'vocab')), may hold values from 5e-09 to 3e-08
- out_proj: float32 [2, 1024, 1024], P(None, ('dp', 'vocab')), may hold values from -1 to 1
- out_proj_mean: float32 [2, 1024, 1024], P(None, ('dp', 'vocab')), may hold values from -0.0008544922 to 0.0008544922
- out_proj_sq: float32 [2, 1024, 1024], P(None, ('dp', 'vocab')), may hold values from 5e-09 to 3e-08
- ffn_proj: float32 [2, 1024, 4096], P(None, ('dp', 'vocab')), may hold values from -0.1875 to 0.1875
- ffn_proj_mean: float32 [2, 1024, 4096], P(None, ('dp', 'vocab')), may hold values from -0.0008544922 to 0.0008544922
- ffn_proj_sq: float32 [2, 1024, 4096], P(None, ('dp', 'vocab')), may hold values from 5e-09 to 3e-08
- embed_table: float32 [4, 2049, 1024], P(None, None, ('dp', 'vocab')), may hold values from -3 to 3
- embed_table_mean: float32 [4, 2049, 1024], P(None, None, ('dp', 'vocab')), may hold values from -0.00015258789 to 0.00015258789
- embed_table_sq: float32 [4, 2049, 1024], P(None, None, ('dp', 'vocab')), may hold values from 1.5e-10 to 9e-10
- head_table: float32 [4, 1024, 2048], P(None, 'dp', 'vocab'), may hold values from -0.1875 to 0.1875
- head_table_mean: float32 [4, 1024, 2048], P(None, 'dp', 'vocab'), may hold values from -0.0008544922 to 0.0008544922
- head_table_sq: float32 [4, 1024, 2048], P(None, 'dp', 'vocab'), may hold values from 5e-09 to 3e-08
- norm_gain: float32 [4, 1024], P(None, ('dp', 'vocab')), may hold values from -0.4 to 0.4
- norm_gain_mean: float32 [4, 1024], P(None, ('dp', 'vocab')), may hold values from -0.0008544922 to 0.0008544922
- norm_gain_sq: float32 [4, 1024], P(None, ('dp', 'vocab')), may hold values from 5e-09 to 3e-08
- norm_bias: float32 [4, 1024], P(None, ('dp', 'vocab')), may hold values from -3 to 3
- norm_bias_mean: float32 [4, 1024], P(None, ('dp', 'vocab')), may hold values from -0.0008544922 to 0.0008544922
- norm_bias_sq: float32 [4, 1024], P(None, ('dp', 'vocab')), may hold values from 5e-09 to 3e-08
Outputs:
- loss_value: float32 [], replicated
- grad_norm: float32 [], replicated
- in_proj_next: float32 [6, 1024, 1024], P(None, ('dp', 'vocab'))
- in_proj_mean_next: float32 [6, 1024, 1024], P(None, ('dp', 'vocab'))
- in_proj_sq_next: float32 [6, 1024, 1024], P(None, ('dp', 'vocab'))
- out_proj_next: float32 [2, 1024, 1024], P(None, ('dp', 'vocab'))
- out_proj_mean_next: float32 [2, 1024, 1024], P(None, ('dp', 'vocab'))
- out_proj_sq_next: float32 [2, 1024, 1024], P(None, ('dp', 'vocab'))
- ffn_proj_next: float32 [2, 1024, 4096], P(None, ('dp', 'vocab'))
- ffn_proj_mean_next: float32 [2, 1024, 4096], P(None, ('dp', 'vocab'))
- ffn_proj_sq_next: float32 [2, 1024, 4096], P(None, ('dp', 'vocab'))
- embed_table_next: float32 [4, 2049, 1024], P(None, None, ('dp', 'vocab'))
- embed_table_mean_next: float32 [4, 2049, 1024], P(None, None, ('dp', 'vocab'))
- embed_table_sq_next: float32 [4, 2049, 1024], P(None, None, ('dp', 'vocab'))
- head_table_next: float32 [4, 1024, 2048], P(None, 'dp', 'vocab')
- head_table_mean_next: float32 [4, 1024, 2048], P(None, 'dp', 'vocab')
- head_table_sq_next: float32 [4, 1024, 2048], P(None, 'dp', 'vocab')
- norm_gain_next: float32 [4, 1024], P(None, ('dp', 'vocab'))
- norm_gain_mean_next: float32 [4, 1024], P(None, ('dp', 'vocab'))
- norm_gain_sq_next: float32 [4, 1024], P(None, ('dp', 'vocab'))
- norm_bias_next: float32 [4, 1024], P(None, ('dp', 'vocab'))
- norm_bias_mean_next: float32 [4, 1024], P(None, ('dp', 'vocab'))
- norm_bias_sq_next: float32 [4, 1024], P(None, ('dp', 'vocab'))
All inputs are finite; a program needn't handle non-finite values.
Results may differ from a plain program's by a relative error of at most 0.0064.
Values may be sent and summed in bfloat16 or wider, within the bound.
A program may use at most 448 MiB of HBM per device.

v0:
```python
import math

import jax
import jax.numpy as jnp
from jax import lax
from jax.sharding import PartitionSpec as P

HEADS = 16


NORM_EPS = 1e-05
SCORE_SCALE = 0.125
NEG_FILL = -1e30
CLIP_LIMIT = 3.0
BETA_ONE = 0.9
BETA_TWO = 0.95
LEARN_RATE = 0.05
DECAY_RATE = 0.1
ADAM_EPS = 1e-08


def merged(value, axis, join):
    pieces = jax.tree.map(lambda part: lax.all_gather(part, axis), value)
    head = jax.tree.map(lambda part: part[0], pieces)
    tail = jax.tree.map(lambda part: part[1:], pieces)
    so_far, _ = lax.scan(lambda so_far, section: (join(so_far, section), None), head, tail)
    return so_far


def layer_norm(values, gain, bias):
    average = jnp.mean(values, axis=-1, keepdims=True)
    centred = values - average
    spread = jnp.mean(centred * centred, axis=-1, keepdims=True)
    return centred * lax.rsqrt(spread + NORM_EPS) * (1.0 + gain) + bias


def norm_back(values, gain, bias, cotangent):
    unused, pull_back = jax.vjp(layer_norm, values, gain, bias)
    return pull_back(cotangent)


def gelu_exact(values):
    return jax.nn.gelu(values, approximate=False)


def sinusoid(frames, model_width):
    half_width = model_width // 2
    freq_rates = jnp.exp(
        jnp.arange(half_width, dtype=jnp.float32) * (-math.log(10000.0) / (half_width - 1))
    )
    angles = jnp.arange(frames, dtype=jnp.float32)[:, None] * freq_rates[None, :]
    return jnp.concatenate([jnp.sin(angles), jnp.cos(angles)], axis=1)


def delay_ids(codes_clip, offsets_clip, special):
    frames = codes_clip.shape[1]
    frame_shift = jnp.arange(frames, dtype=jnp.int32)[None, :] - offsets_clip[:, None]
    picked = jnp.take_along_axis(codes_clip, jnp.clip(frame_shift, 0, frames - 1), axis=1)
    targets = jnp.where(frame_shift >= 0, picked, special)
    before = frame_shift - 1
    picked_before = jnp.take_along_axis(codes_clip, jnp.clip(before, 0, frames - 1), axis=1)
    inputs = jnp.where(before >= 0, picked_before, special)
    return (inputs, targets)


def to_low(values):
    return values.astype(jnp.bfloat16)


def dense(left, right):
    return jnp.dot(left, right, preferred_element_type=jnp.float32)


def dense_trans(left, right):
    return lax.dot_general(
        left, right, (((1,), (1,)), ((), ())), preferred_element_type=jnp.float32
    )


def outer_sum(left, right):
    return lax.dot_general(
        left, right, (((0,), (0,)), ((), ())), preferred_element_type=jnp.float32
    )


def split_heads(matrix):
    row_count = matrix.shape[0]
    return matrix.reshape(row_count, HEADS, -1).transpose(1, 0, 2)


def join_heads(tensor):
    return tensor.transpose(1, 0, 2).reshape(tensor.shape[1], -1)


def raw_scores(queries, keyset, causal):
    scores = (
        jnp.einsum("hqe,hke->hqk", queries, keyset, preferred_element_type=jnp.float32)
        * SCORE_SCALE
    )
    if causal:
        length_q = scores.shape[1]
        allowed = jnp.arange(length_q)[:, None] >= jnp.arange(length_q)[None, :]
        scores = jnp.where(allowed[None], scores, NEG_FILL)
    return scores


def attend_forward(queries, keyset, valset, causal):
    scores = raw_scores(queries, keyset, causal)
    highest = jnp.max(scores, axis=-1, keepdims=True)
    exponents = jnp.exp(scores - highest)
    denominator = jnp.sum(exponents, axis=-1, keepdims=True)
    attn_probs = to_low(exponents / denominator)
    mixed_heads = jnp.einsum("hqk,hke->hqe", attn_probs, valset, preferred_element_type=jnp.float32)
    return (mixed_heads, highest + jnp.log(denominator))


def attend_backward(queries, keyset, valset, log_total, grad_mixed, causal):
    attn_probs = jnp.exp(raw_scores(queries, keyset, causal) - log_total)
    grad_probs = jnp.einsum("hqe,hke->hqk", grad_mixed, valset, preferred_element_type=jnp.float32)
    grad_values = to_low(
        jnp.einsum(
            "hqk,hqe->hke", to_low(attn_probs), grad_mixed, preferred_element_type=jnp.float32
        )
    )
    grad_scores = to_low(
        attn_probs * (grad_probs - jnp.sum(attn_probs * grad_probs, axis=-1, keepdims=True))
    )
    grad_queries = to_low(
        jnp.einsum("hqk,hke->hqe", grad_scores, keyset, preferred_element_type=jnp.float32)
        * SCORE_SCALE
    )
    grad_keys = to_low(
        jnp.einsum("hqk,hqe->hke", grad_scores, queries, preferred_element_type=jnp.float32)
        * SCORE_SCALE
    )
    return (grad_queries, grad_keys, grad_values)


def clip_forward(layer_low, embedded, text_clip, positions_clip):
    in_weight, out_weight, ffn_weight, gain_low, bias_low = layer_low
    gain_rows = gain_low.astype(jnp.float32)
    biases = bias_low.astype(jnp.float32)
    frames = embedded.shape[0]
    model_width = embedded.shape[1]
    start_rows = embedded + sinusoid(frames, model_width)
    normed_self = to_low(layer_norm(start_rows, gain_rows[0], biases[0]))
    self_proj = to_low(
        jnp.einsum("sd,kde->kse", normed_self, in_weight[0:3], preferred_element_type=jnp.float32)
    )
    mixed_heads, self_lse = attend_forward(
        split_heads(self_proj[0]), split_heads(self_proj[1]), split_heads(self_proj[2]), True
    )
    self_out = to_low(join_heads(mixed_heads))
    after_self = start_rows + dense(self_out, out_weight[0])
    normed_cross = to_low(layer_norm(after_self, gain_rows[1], biases[1]))
    cross_query = to_low(dense(normed_cross, in_weight[3]))
    cross_text = to_low(
        jnp.einsum("td,kde->kte", text_clip, in_weight[4:6], preferred_element_type=jnp.float32)
    )
    mixed_heads, cross_lse = attend_forward(
        split_heads(cross_query), split_heads(cross_text[0]), split_heads(cross_text[1]), False
    )
    cross_out = to_low(join_heads(mixed_heads))
    after_cross = after_self + dense(cross_out, out_weight[1])
    normed_ffn = to_low(layer_norm(after_cross, gain_rows[2], biases[2]))
    up_values = dense(normed_ffn, ffn_weight[0])
    active = to_low(gelu_exact(up_values))
    after_ffn = after_cross + dense_trans(active, ffn_weight[1])
    final_norm = layer_norm(after_ffn, gain_rows[3], biases[3])
    chosen = to_low(jnp.take(final_norm, positions_clip, axis=0))
    kept_state = (
        start_rows,
        after_self,
        after_cross,
        after_ffn,
        normed_self,
        self_proj,
        self_lse,
        self_out,
        normed_cross,
        cross_query,
        cross_text,
        cross_lse,
        cross_out,
        normed_ffn,
        up_values,
        active,
    )
    return (chosen, kept_state)


def clip_backward(layer_low, kept_state, text_clip, positions_clip, grad_chosen):
    in_weight, out_weight, ffn_weight, gain_low, bias_low = layer_low
    (
        start_rows,
        after_self,
        after_cross,
        after_ffn,
        normed_self,
        self_proj,
        self_lse,
        self_out,
        normed_cross,
        cross_query,
        cross_text,
        cross_lse,
        cross_out,
        normed_ffn,
        up_values,
        active,
    ) = kept_state
    gain_rows = gain_low.astype(jnp.float32)
    biases = bias_low.astype(jnp.float32)
    grad_final = jnp.zeros(after_ffn.shape, jnp.float32).at[positions_clip].add(grad_chosen)
    grad_ffn_res, gain_three, bias_three = norm_back(after_ffn, gain_rows[3], biases[3], grad_final)
    low_ffn = to_low(grad_ffn_res)
    grad_down = outer_sum(low_ffn, active)
    grad_active = dense(low_ffn, ffn_weight[1])
    unused, gelu_pull = jax.vjp(gelu_exact, up_values)
    grad_upper = to_low(gelu_pull(grad_active)[0])
    grad_up = outer_sum(normed_ffn, grad_upper)
    grad_normed = dense_trans(grad_upper, ffn_weight[0])
    grad_inner, gain_two, bias_two = norm_back(after_cross, gain_rows[2], biases[2], grad_normed)
    grad_cross_res = grad_ffn_res + grad_inner
    low_cross = to_low(grad_cross_res)
    grad_out_cross = outer_sum(cross_out, low_cross)
    grad_mixed = to_low(dense_trans(low_cross, out_weight[1]))
    grad_query, grad_key, grad_value = attend_backward(
        split_heads(cross_query),
        split_heads(cross_text[0]),
        split_heads(cross_text[1]),
        cross_lse,
        split_heads(grad_mixed),
        False,
    )
    grad_cross_query = join_heads(grad_query)
    grad_cross_text = jnp.stack([join_heads(grad_key), join_heads(grad_value)])
    grad_in_query = outer_sum(normed_cross, grad_cross_query)
    grad_in_text = jnp.einsum(
        "td,kte->kde", text_clip, grad_cross_text, preferred_element_type=jnp.float32
    )
    grad_normed = dense_trans(grad_cross_query, in_weight[3])
    grad_inner, gain_one, bias_one = norm_back(after_self, gain_rows[1], biases[1], grad_normed)
    grad_self_res = grad_cross_res + grad_inner
    low_self = to_low(grad_self_res)
    grad_out_self = outer_sum(self_out, low_self)
    grad_mixed = to_low(dense_trans(low_self, out_weight[0]))
    grad_query, grad_key, grad_value = attend_backward(
        split_heads(self_proj[0]),
        split_heads(self_proj[1]),
        split_heads(self_proj[2]),
        self_lse,
        split_heads(grad_mixed),
        True,
    )
    grad_proj = jnp.stack([join_heads(grad_query), join_heads(grad_key), join_heads(grad_value)])
    grad_in_self = jnp.einsum(
        "sd,kse->kde", normed_self, grad_proj, preferred_element_type=jnp.float32
    )
    grad_normed = jnp.einsum(
        "kse,kde->sd", grad_proj, in_weight[0:3], preferred_element_type=jnp.float32
    )
    grad_inner, gain_zero, bias_zero = norm_back(start_rows, gain_rows[0], biases[0], grad_normed)
    grad_start = grad_self_res + grad_inner
    grad_in = jnp.concatenate([grad_in_self, grad_in_query[None], grad_in_text], axis=0)
    grad_out = jnp.stack([grad_out_self, grad_out_cross])
    grad_ffn = jnp.stack([grad_up, grad_down])
    grad_gain = jnp.stack([gain_zero, gain_one, gain_two, gain_three])
    grad_bias = jnp.stack([bias_zero, bias_one, bias_two, bias_three])
    return ((grad_in, grad_out, grad_ffn, grad_gain, grad_bias), grad_start)


def table_segments(rows, ids_by_book, table_rows):
    return jnp.stack(
        [
            jax.ops.segment_sum(rows, ids_by_book[codebook], num_segments=table_rows)
            for codebook in range(ids_by_book.shape[0])
        ]
    )


def head_terms(pair_rows, head_low, targets, teach_pair, vocab_base, special):
    logits = jnp.einsum("rd,kdv->krv", pair_rows, head_low, preferred_element_type=jnp.float32)
    half_vocab = head_low.shape[2]
    local_ids = vocab_base + jnp.arange(half_vocab, dtype=jnp.int32)
    highest = jnp.max(logits, axis=-1)
    exp_sum = jnp.sum(jnp.exp(logits - highest[:, :, None]), axis=-1)
    target_valid = (targets != special).astype(jnp.float32)
    target_hit = (targets[:, :, None] == local_ids[None, None, :]).astype(jnp.float32)
    teach_local = teach_pair - vocab_base
    inside = (teach_local >= 0) & (teach_local < half_vocab)
    slot_index = jnp.where(inside, teach_local, half_vocab)
    book_index = jnp.broadcast_to(
        jnp.arange(teach_pair.shape[0], dtype=jnp.int32)[:, None, None], teach_pair.shape
    )
    row_index = jnp.broadcast_to(
        jnp.arange(teach_pair.shape[1], dtype=jnp.int32)[None, :, None], teach_pair.shape
    )
    counts = (
        jnp.zeros(logits.shape, jnp.float32)
        .at[book_index, row_index, slot_index]
        .add(1.0, mode="drop")
    )
    teach_count = teach_pair.shape[2]
    target_sum = (
        target_valid * jnp.sum(target_hit * logits, axis=-1)
        + jnp.sum(counts * logits, axis=-1) / teach_count
    )
    return (logits, highest, exp_sum, target_sum, target_valid, target_hit, counts / teach_count)


def combine_stats(left_stats, right_stats):
    highest = jnp.maximum(left_stats[0], right_stats[0])
    exp_sum = left_stats[1] * jnp.exp(left_stats[0] - highest) + right_stats[1] * jnp.exp(
        right_stats[0] - highest
    )
    return (highest, exp_sum)


def adam_step(weight, first_moment, second_moment, gradient, factor, corr_one, corr_two):
    clipped = gradient * factor
    first_next = BETA_ONE * first_moment + (1.0 - BETA_ONE) * clipped
    second_next = BETA_TWO * second_moment + (1.0 - BETA_TWO) * clipped * clipped
    update = (
        first_next / corr_one / (jnp.sqrt(second_next / corr_two) + ADAM_EPS) + DECAY_RATE * weight
    )
    return (weight - LEARN_RATE * update, first_next, second_next)


def local(
    audio_codes,
    delay_offsets,
    clip_lengths,
    loss_positions,
    teacher_ids,
    text_states,
    step_count,
    in_proj,
    in_proj_mean,
    in_proj_sq,
    out_proj,
    out_proj_mean,
    out_proj_sq,
    ffn_proj,
    ffn_proj_mean,
    ffn_proj_sq,
    embed_table,
    embed_table_mean,
    embed_table_sq,
    head_table,
    head_table_mean,
    head_table_sq,
    norm_gain,
    norm_gain_mean,
    norm_gain_sq,
    norm_bias,
    norm_bias_mean,
    norm_bias_sq,
):
    micro_count = text_states.shape[0]
    vocab_count = lax.axis_size("vocab")
    vocab_index = lax.axis_index("vocab")
    book_count = head_table.shape[0]
    pos_count = loss_positions.shape[1]
    frames = audio_codes.shape[2]
    table_rows = embed_table.shape[1]
    special = table_rows - 1
    half_vocab = head_table.shape[2]
    vocab_base = vocab_index * half_vocab
    denominator = float(micro_count * lax.axis_size("dp") * vocab_count * pos_count * book_count)
    own_inputs_list = []
    for micro_step in range(micro_count):
        own_clip = vocab_index * micro_count + micro_step
        own_codes = lax.dynamic_index_in_dim(audio_codes, own_clip, 0, False)
        own_offsets = lax.dynamic_index_in_dim(delay_offsets, own_clip, 0, False)
        own_inputs_list.append(delay_ids(own_codes, own_offsets, special)[0])
    kept_layer = (
        lax.all_gather(to_low(in_proj), ("dp", "vocab"), axis=1, tiled=True),
        lax.all_gather(to_low(out_proj), ("dp", "vocab"), axis=1, tiled=True),
        lax.all_gather(to_low(ffn_proj), ("dp", "vocab"), axis=1, tiled=True),
        lax.all_gather(to_low(norm_gain), ("dp", "vocab"), axis=1, tiled=True),
        lax.all_gather(to_low(norm_bias), ("dp", "vocab"), axis=1, tiled=True),
    )
    kept_head = lax.all_gather(to_low(head_table), "dp", axis=1, tiled=True)
    kept_table = lax.all_gather(to_low(embed_table), ("dp", "vocab"), axis=2, tiled=True)
    layer_sum = None
    head_sum = None
    embed_sum = None
    loss_sum = jnp.zeros((), jnp.float32)
    for micro_step in range(micro_count):
        own_positions = lax.dynamic_index_in_dim(
            loss_positions, vocab_index * micro_count + micro_step, 0, False
        )
        own_inputs = own_inputs_list[micro_step]
        embedded = jnp.zeros((frames, kept_table.shape[2]), jnp.float32)
        for codebook in range(book_count):
            embedded = embedded + jnp.take(
                kept_table[codebook], own_inputs[codebook], axis=0
            ).astype(jnp.float32)
        chosen, kept_state = clip_forward(
            kept_layer, embedded, text_states[micro_step], own_positions
        )
        pair_rows = lax.all_gather(chosen, "vocab", axis=0, tiled=True)
        target_parts = []
        teach_parts = []
        weight_parts = []
        for member in range(vocab_count):
            pair_clip = member * micro_count + micro_step
            unused, clip_targets = delay_ids(
                audio_codes[pair_clip], delay_offsets[pair_clip], special
            )
            target_parts.append(jnp.take(clip_targets, loss_positions[pair_clip], axis=1))
            teach_parts.append(teacher_ids[pair_clip])
            weight_parts.append(
                (loss_positions[pair_clip] < clip_lengths[pair_clip]).astype(jnp.float32)
            )
        targets = jnp.concatenate(target_parts, axis=1)
        teach_pair = jnp.concatenate(teach_parts, axis=1)
        row_weight = jnp.concatenate(weight_parts, axis=0)
        logits, highest, exp_sum, target_sum, target_valid, target_hit, teach_share = head_terms(
            pair_rows, kept_head, targets, teach_pair, vocab_base, special
        )
        top_all, sum_all = merged((highest, exp_sum), "vocab", combine_stats)
        log_total = top_all + jnp.log(sum_all)
        row_loss = row_weight[None, :] * (target_valid + 1.0) * log_total
        loss_sum = loss_sum + jnp.sum(
            lax.dynamic_slice_in_dim(row_loss, vocab_index * pos_count, pos_count, 1)
        )
        loss_sum = loss_sum - jnp.sum(row_weight[None, :] * target_sum)
        scaled = (row_weight / denominator)[None, :, None]
        grad_logits = to_low(
            scaled
            * (
                (target_valid + 1.0)[:, :, None] * jnp.exp(logits - log_total[:, :, None])
                - target_valid[:, :, None] * target_hit
                - teach_share
            )
        )
        head_grad = jnp.einsum(
            "rd,krv->kdv", pair_rows, grad_logits, preferred_element_type=jnp.float32
        )
        grad_rows = jnp.einsum(
            "krv,kdv->rd", grad_logits, kept_head, preferred_element_type=jnp.float32
        )
        grad_chosen = lax.psum_scatter(
            grad_rows.astype(jnp.bfloat16), "vocab", scatter_dimension=0, tiled=True
        ).astype(jnp.float32)
        layer_grads, grad_start = clip_backward(
            kept_layer, kept_state, text_states[micro_step], own_positions, grad_chosen
        )
        embed_part = table_segments(grad_start, own_inputs, table_rows)
        layer_sum = (
            layer_grads if layer_sum is None else jax.tree.map(jnp.add, layer_sum, layer_grads)
        )
        head_sum = head_grad if head_sum is None else head_sum + head_grad
        embed_sum = embed_part if embed_sum is None else embed_sum + embed_part
    head_shard = lax.psum_scatter(head_sum, "dp", scatter_dimension=1, tiled=True)
    embed_shard = lax.psum_scatter(embed_sum, ("dp", "vocab"), scatter_dimension=2, tiled=True)
    gradients = (
        lax.psum_scatter(layer_sum[0], ("dp", "vocab"), scatter_dimension=1, tiled=True),
        lax.psum_scatter(layer_sum[1], ("dp", "vocab"), scatter_dimension=1, tiled=True),
        lax.psum_scatter(layer_sum[2], ("dp", "vocab"), scatter_dimension=1, tiled=True),
        embed_shard,
        head_shard,
        lax.psum_scatter(layer_sum[3], ("dp", "vocab"), scatter_dimension=1, tiled=True),
        lax.psum_scatter(layer_sum[4], ("dp", "vocab"), scatter_dimension=1, tiled=True),
    )
    square_sum = jnp.zeros((), jnp.float32)
    for shard_grad in gradients:
        square_sum = square_sum + jnp.sum(shard_grad * shard_grad)
    square_total, loss_total = lax.psum((square_sum, loss_sum), ("dp", "vocab"))
    loss_value = loss_total / denominator
    grad_norm = jnp.sqrt(square_total)
    factor = CLIP_LIMIT / jnp.maximum(grad_norm, CLIP_LIMIT)
    steps_float = step_count.astype(jnp.float32)
    corr_one = 1.0 - jnp.power(BETA_ONE, steps_float)
    corr_two = 1.0 - jnp.power(BETA_TWO, steps_float)
    masters = (in_proj, out_proj, ffn_proj, embed_table, head_table, norm_gain, norm_bias)
    mean_list = (
        in_proj_mean,
        out_proj_mean,
        ffn_proj_mean,
        embed_table_mean,
        head_table_mean,
        norm_gain_mean,
        norm_bias_mean,
    )
    square_list = (
        in_proj_sq,
        out_proj_sq,
        ffn_proj_sq,
        embed_table_sq,
        head_table_sq,
        norm_gain_sq,
        norm_bias_sq,
    )
    results = [
        adam_step(
            masters[index],
            mean_list[index],
            square_list[index],
            gradients[index],
            factor,
            corr_one,
            corr_two,
        )
        for index in range(7)
    ]
    return (
        loss_value,
        grad_norm,
        results[0][0],
        results[0][1],
        results[0][2],
        results[1][0],
        results[1][1],
        results[1][2],
        results[2][0],
        results[2][1],
        results[2][2],
        results[3][0],
        results[3][1],
        results[3][2],
        results[4][0],
        results[4][1],
        results[4][2],
        results[5][0],
        results[5][1],
        results[5][2],
        results[6][0],
        results[6][1],
        results[6][2],
    )


def solution(mesh):
    placed = (
        P("dp", None, None),
        P("dp", None),
        P("dp"),
        P("dp", None),
        P("dp", None, None, None),
        P(("dp", "vocab"), None, None),
        P(),
        P(None, ("dp", "vocab"), None),
        P(None, ("dp", "vocab"), None),
        P(None, ("dp", "vocab"), None),
        P(None, ("dp", "vocab"), None),
        P(None, ("dp", "vocab"), None),
        P(None, ("dp", "vocab"), None),
        P(None, ("dp", "vocab"), None),
        P(None, ("dp", "vocab"), None),
        P(None, ("dp", "vocab"), None),
        P(None, None, ("dp", "vocab")),
        P(None, None, ("dp", "vocab")),
        P(None, None, ("dp", "vocab")),
        P(None, "dp", "vocab"),
        P(None, "dp", "vocab"),
        P(None, "dp", "vocab"),
        P(None, ("dp", "vocab")),
        P(None, ("dp", "vocab")),
        P(None, ("dp", "vocab")),
        P(None, ("dp", "vocab")),
        P(None, ("dp", "vocab")),
        P(None, ("dp", "vocab")),
    )
    return jax.shard_map(
        local,
        mesh=mesh,
        in_specs=placed,
        out_specs=(
            P(),
            P(),
            P(None, ("dp", "vocab"), None),
            P(None, ("dp", "vocab"), None),
            P(None, ("dp", "vocab"), None),
            P(None, ("dp", "vocab"), None),
            P(None, ("dp", "vocab"), None),
            P(None, ("dp", "vocab"), None),
            P(None, ("dp", "vocab"), None),
            P(None, ("dp", "vocab"), None),
            P(None, ("dp", "vocab"), None),
            P(None, None, ("dp", "vocab")),
            P(None, None, ("dp", "vocab")),
            P(None, None, ("dp", "vocab")),
            P(None, "dp", "vocab"),
            P(None, "dp", "vocab"),
            P(None, "dp", "vocab"),
            P(None, ("dp", "vocab")),
            P(None, ("dp", "vocab")),
            P(None, ("dp", "vocab")),
            P(None, ("dp", "vocab")),
            P(None, ("dp", "vocab")),
            P(None, ("dp", "vocab")),
        ),
        check_vma=False,
    )
```

profile of v0, /device:TPU:0, one launch (start us, length us, event | category | flops | bytes accessed | tf_op | source)
XLA Modules:
  0.0 3514.9 jit_solution(15226518380875218854)
XLA Ops:
  24.9 4.7 gather_fusion
  42.5 70.5 %all-gather.5 = bf16[32,32,4]{1,2,0:T(4,128)(2,1)S(1)} all-gather(bf16[1,32,4]{1,2,0:T(4,128)(2,1)S(1)} %convert_bitcast_fusion), channel_id=1, replica_groups=mesh['dp'=16,'vocab'=2] {'dp','vocab'}, dimensions={0}, use_global_device_ids=true | all-gather | bytes 8448 | tf_op jit(solution)/shard_map/all_gather | solution.py:382
  113.7 63.9 %all-gather.4 = bf16[32,32,4]{1,2,0:T(4,128)(2,1)S(1)} all-gather(bf16[1,32,4]{1,2,0:T(4,128)(2,1)S(1)} %convert_bitcast_fusion.1), channel_id=1, replica_groups=mesh['dp'=16,'vocab'=2] {'dp','vocab'}, dimensions={0}, use_global_device_ids=true | all-gather | bytes 8448 | tf_op jit(solution)/shard_map/all_gather | solution.py:381
  193.9 86.4 %scatter_custom_fusion.11 = f32[262144]{0:T(1024)S(1)} fusion(s32[16384]{0:T(1024)S(1)} %reshape.1033, f32[16384]{0:T(1024)S(1)} %broadcast.888, f32[]{:T(128)} %constant.100.clone.1), kind=kCustom, calls=%fused_computation.267 | custom fusion | flops 16384 | bytes 1048580
  282.1 86.6 %scatter_custom_fusion.10 = f32[262144]{0:T(1024)S(1)} fusion(s32[16384]{0:T(1024)S(1)} %reshape.1027, f32[16384]{0:T(1024)S(1)} %broadcast.888, f32[]{:T(128)} %constant.100.clone.1), kind=kCustom, calls=%fused_computation.269 | custom fusion | flops 16384 | bytes 1048580
  382.1 39.1 %fusion.275 = (bf16[1,2049,1024]{1,0,2:T(2,128)(2,1)}, bf16[1,2049,1024]{1,0,2:T(2,128)(2,1)}, bf16[1,2049,1024]{1,0,2:T(2,128)(2,1)}, bf16[1,2049,1024]{1,0,2:T(2,128)(2,1)}) fusion(bf16[4,2049,1024]{1,0,2:T(4,128)(2,1)} %all-gather.16.cloned.1.call-done), kind=kLoop, calls=%fused_computation.649 | loop fusion | bytes 33570816 | tf_op jit(solution)/shard_map/slice | solution.py:398
  421.2 20.7 copy.359
  441.9 20.8 copy.358
  462.7 20.7 copy.357
  483.4 20.6 copy.356
  564.8 5.0 fusion.3
  569.9 10.2 fusion.286
  584.0 6.3 fusion.291
  594.8 4.9 all_gather.63
  600.7 5.2 all_gather.57
  605.9 5.2 fusion.292
  640.0 9.3 fusion.181
  649.4 6.7 fusion.116
  660.0 5.6 reduce-scatter.12.cloned.1.call-done
  672.6 8.7 add_convert_fusion.1
  684.4 6.4 add_convert_fusion
  731.7 5.3 fusion.74
  744.4 14.0 add_bitcast_fusion
  758.4 20.2 copy.326
  791.7 6.4 scatter_custom_fusion.5
  798.1 5.9 scatter_custom_fusion.4
  804.1 5.9 scatter_custom_fusion.3
  810.0 5.9 scatter_custom_fusion.2
  817.8 5.8 scatter_custom_fusion.9
  823.7 6.0 scatter_custom_fusion.8
  829.7 5.8 scatter_custom_fusion.7
  835.5 5.9 scatter_custom_fusion.6
  841.3 34.6 maximum_add_fusion
  876.0 37.4 %copy.325 = f32[4,2049,1024]{1,0,2:T(4,128)} copy(f32[4,2049,1024]{2,1,0:T(8,128)} %maximum_add_fusion) | data formatting | bytes 67141632 | tf_op jit(solution)/shard_map/add | solution.py:456
  935.4 6.5 convolution_bitcast_fusion.4
  941.9 20.9 maximum_add_fusion.2
  962.8 29.8 copy.322
  994.0 8.2 convolution_bitcast_fusion.3
  1002.3 8.3 convolution_bitcast_fusion.1
  1010.6 9.3 convolution_bitcast_fusion.2
  1019.9 9.0 convolution_bitcast_fusion
  1028.9 34.5 maximum_add_fusion.1
  1072.9 234.7 %all-reduce.8.cloned.1.call-done = f32[4,1024,1024]{2,0,1:T(4,128)} async-done(((f32[4,1024,1024]{2,0,1:T(4,128)}), f32[4,1024,1024]{2,0,1:T(4,128)}) %all-reduce.8.cloned.1.call-update) | async-done | bytes 16777232
  1310.0 182.8 %reduce-scatter.18.cloned.1.call-done = f32[2,32,1024]{2,1,0:T(8,128)} async-done(((f32[2,1024,1024]{2,1,0:T(8,128)}), f32[2,32,1024]{2,1,0:T(8,128)}) %reduce-scatter.18.cloned.1.call-update) | async-done | bytes 262160 | tf_op jit(solution)/shard_map/reduce_scatter | solution.py:461
  1494.4 528.9 %all-reduce.6.cloned.1.call-done = f32[4,2049,1024]{1,0,2:T(4,128)} async-done(((f32[4,2049,1024]{1,0,2:T(4,128)}), f32[4,2049,1024]{1,0,2:T(4,128)}) %all-reduce.6.cloned.1.call-update) | async-done | bytes 33570832
  2025.8 705.7 %reduce-scatter.16.cloned.1.call-done = f32[6,32,1024]{2,0,1:T(8,128)} async-done(((f32[6,1024,1024]{2,0,1:T(8,128)}), f32[6,32,1024]{2,0,1:T(8,128)}) %reduce-scatter.16.cloned.1.call-update) | async-done | bytes 786448 | tf_op jit(solution)/shard_map/reduce_scatter | solution.py:460
  2734.9 707.5 %reduce-scatter.20.cloned.1.call-done = f32[2,32,4096]{2,1,0:T(8,128)} async-done(((f32[2,1024,4096]{2,1,0:T(8,128)}), f32[2,32,4096]{2,1,0:T(8,128)}) %reduce-scatter.20.cloned.1.call-update) | async-done | bytes 1048592 | tf_op jit(solution)/shard_map/reduce_scatter | solution.py:462
  3447.7 42.2 %all-reduce.2 = (f32[]{:T(128)}, f32[]{:T(128)}) all-reduce(f32[]{:T(128)S(6)} %sub.483, f32[]{:T(128)S(6)} %add.709), channel_id=1, replica_groups=mesh['dp'=16,'vocab'=2] {'dp','vocab'}, use_global_device_ids=true, to_apply=%region_38.43 | all-reduce | flops 2 | bytes 16 | tf_op jit(solution)/shard_map/psum | solution.py:471
  (905 shorter events, 289.1 us)
Async XLA Ops:
  7.2 365.1 %all-gather.18.cloned.1.call-start = ((), (), s32[]{:S(2)}) async-start(), calls=%async_computation.8 | async-start | bytes 12976128 | tf_op jit(solution)/shard_map/all_gather | solution.py:378
  9.4 372.7 %all-gather.16.cloned.1.call-start = ((), (), s32[]{:S(2)}) async-start(), calls=%async_computation.7 | async-start | bytes 18382848 | tf_op jit(solution)/shard_map/all_gather | solution.py:385
  11.0 514.4 %all-gather.20.cloned.1.call-start = ((), (), s32[]{:S(2)}) async-start(), calls=%async_computation.9 | async-start | bytes 4325376 | tf_op jit(solution)/shard_map/all_gather | solution.py:379
  11.8 552.9 %all-gather.22.cloned.1.call-start = ((), (), s32[]{:S(2)}) async-start(), calls=%async_computation.10 | async-start | bytes 17301504 | tf_op jit(solution)/shard_map/all_gather | solution.py:380
  12.7 593.1 %all-gather.24.cloned.1.call-start = ((), (), s32[]{:S(2)}) async-start(), calls=%async_computation.11 | async-start | bytes 8912896 | tf_op jit(solution)/shard_map/all_gather | solution.py:384
  13.7 644.4 %reduce-scatter.14.cloned.1.call-start = ((), (), s32[]{:S(2)}) async-start(), calls=%async_computation.13 | async-start | bytes 196608 | tf_op jit(solution)/shard_map/reduce_scatter | solution.py:445
  32.5 81.2 %copy-start.179 = (f32[4,32]{1,0:T(4,128)S(1)}, f32[4,32]{1,0:T(4,128)}, u32[]{:S(2)}) copy-start(f32[4,32]{1,0:T(4,128)} %param.58) | copy-start | bytes 1540
  113.7 434.0 %copy-start.146 = (f32[1,1024]{1,0:T(1,128)}, f32[1,1024]{1,0:T(1,128)S(1)}, u32[]{:S(2)}) copy-start(f32[1,1024]{1,0:T(1,128)S(1)} %get-tuple-element.273) | copy-start | bytes 12292
  113.7 468.5 %copy-start.125 = (f32[1,1024]{1,0:T(1,128)}, f32[1,1024]{1,0:T(1,128)S(1)}, u32[]{:S(2)}) copy-start(f32[1,1024]{1,0:T(1,128)S(1)} %get-tuple-element.271) | copy-start | bytes 12292
  177.7 379.3 %copy-start.144 = (f32[1,1024]{1,0:T(1,128)}, f32[1,1024]{1,0:T(1,128)S(1)}, u32[]{:S(2)}) copy-start(f32[1,1024]{1,0:T(1,128)S(1)} %get-tuple-element.268) | copy-start | bytes 12292
  177.7 412.9 %copy-start.142 = (f32[1,1024]{1,0:T(1,128)}, f32[1,1024]{1,0:T(1,128)S(1)}, u32[]{:S(2)}) copy-start(f32[1,1024]{1,0:T(1,128)S(1)} %get-tuple-element.266) | copy-start | bytes 12292
  177.7 516.8 %copy-start.123 = (f32[1,1024]{1,0:T(1,128)}, f32[1,1024]{1,0:T(1,128)S(1)}, u32[]{:S(2)}) copy-start(f32[1,1024]{1,0:T(1,128)S(1)} %get-tuple-element.267) | copy-start | bytes 12292
  187.3 93.0 %copy-start.164 = (s32[4,128]{1,0:T(4,128)}, s32[4,128]{1,0:T(4,128)S(1)}, u32[]{:S(2)}) copy-start(s32[4,128]{1,0:T(4,128)S(1)} %get-tuple-element.391) | copy-start | bytes 6148
  281.4 91.0 %copy-start.127 = (bf16[2,64,1024]{2,1,0:T(8,128)(2,1)S(1)}, bf16[2,64,1024]{2,1,0:T(8,128)(2,1)}, u32[]{:S(2)}) copy-start(bf16[2,64,1024]{2,1,0:T(8,128)(2,1)} %param.41) | copy-start | bytes 786436
  530.8 29.7 copy-start.58
  562.3 18.1 copy-start.140
  613.4 18.3 copy-start.207
  613.4 18.3 copy-start.257
  613.4 19.5 copy-start.205
  613.4 19.5 copy-start.256
  613.4 20.7 copy-start.171
  613.4 20.7 copy-start.172
  613.4 20.7 copy-start.173
  613.4 20.7 copy-start.174
  613.5 20.7 copy-start.235
  613.5 20.7 copy-start.236
  639.9 25.7 reduce-scatter.12.cloned.1.call-start
  649.3 18.6 copy-start.143
  649.3 18.6 copy-start.190
  649.3 18.6 copy-start.192
  649.4 18.6 copy-start.200
  649.4 18.6 copy-start.202
  657.4 412.7 %reduce-scatter.22.cloned.1.call-start = ((), (), s32[]{:S(2)}) async-start(), calls=%async_computation.17 | async-start | bytes 540672
  671.2 25.0 copy-start.77
  671.2 25.0 copy-start.253
  743.1 327.7 %reduce-scatter.24.cloned.1.call-start = ((), (), s32[]{:S(2)}) async-start(), calls=%async_computation.18 | async-start | bytes 540672
  744.4 563.2 %all-reduce.8.cloned.1.call-start = ((), (), s32[]{:S(2)}) async-start(), calls=%async_computation.20 | async-start | bytes 33554432
  778.7 714.1 %reduce-scatter.18.cloned.1.call-start = ((), (), s32[]{:S(2)}) async-start(), calls=%async_computation.15 | async-start | bytes 8650752 | tf_op jit(solution)/shard_map/reduce_scatter | solution.py:461
  787.7 1235.6 %all-reduce.6.cloned.1.call-start = ((), (), s32[]{:S(2)}) async-start(), calls=%async_computation.19 | async-start | bytes 71303168
  913.4 1818.1 %reduce-scatter.16.cloned.1.call-start = ((), (), s32[]{:S(2)}) async-start(), calls=%async_computation.14 | async-start | bytes 34603008 | tf_op jit(solution)/shard_map/reduce_scatter | solution.py:460
  992.7 2449.7 %reduce-scatter.20.cloned.1.call-start = ((), (), s32[]{:S(2)}) async-start(), calls=%async_computation.16 | async-start | bytes 34603008 | tf_op jit(solution)/shard_map/reduce_scatter | solution.py:462
  1494.4 1997.0 %copy-start.180 = (f32[4,32]{1,0:T(4,128)S(1)}, f32[4,32]{1,0:T(4,128)}, u32[]{:S(2)}) copy-start(f32[4,32]{1,0:T(4,128)} %param.58) | copy-start | bytes 1540
  1494.4 1997.0 %copy-start.237 = (f32[4,32]{1,0:T(4,128)S(1)}, f32[4,32]{1,0:T(4,128)}, u32[]{:S(2)}) copy-start(f32[4,32]{1,0:T(4,128)} %param.60) | copy-start | bytes 1540
  1494.4 1997.0 %copy-start.238 = (f32[4,32]{1,0:T(4,128)S(1)}, f32[4,32]{1,0:T(4,128)}, u32[]{:S(2)}) copy-start(f32[4,32]{1,0:T(4,128)} %param.59) | copy-start | bytes 1540
  1494.4 1997.6 %copy-start.182 = (f32[4,32]{1,0:T(4,128)S(1)}, f32[4,32]{1,0:T(4,128)}, u32[]{:S(2)}) copy-start(f32[4,32]{1,0:T(4,128)} %param.61) | copy-start | bytes 1540
  1494.4 1997.6 %copy-start.239 = (f32[4,32]{1,0:T(4,128)S(1)}, f32[4,32]{1,0:T(4,128)}, u32[]{:S(2)}) copy-start(f32[4,32]{1,0:T(4,128)} %param.63) | copy-start | bytes 1540
  1494.4 1997.6 %copy-start.240 = (f32[4,32]{1,0:T(4,128)S(1)}, f32[4,32]{1,0:T(4,128)}, u32[]{:S(2)}) copy-start(f32[4,32]{1,0:T(4,128)} %param.62) | copy-start | bytes 1540
  1494.4 1998.2 %copy-start.48 = (f32[4,2049,32]{1,2,0:T(8,128)S(1)}, f32[4,2049,32]{1,2,0:T(8,128)}, u32[]{:S(2)}) copy-start(f32[4,2049,32]{1,2,0:T(8,128)} %param.52) | copy-start | bytes 3147268
  (258 other events, 1110.6 us)
Sparse Core Ops, SparseCore 0:
  11.7 99.0 all-gather.17
  114.2 118.4 all-gather.15
  236.3 60.1 all-gather.19
  300.0 113.3 all-gather.21
  416.0 73.0 all-gather.23
  640.0 8.0 reduce-scatter.13
  657.5 8.0 reduce-scatter.11
  743.3 133.9 reduce-scatter.21
  879.6 129.9 reduce-scatter.23
  1013.4 294.1 all-reduce.7
  1309.9 182.8 reduce-scatter.17
  1499.1 524.2 all-reduce.5
  2025.7 705.7 reduce-scatter.15
  2733.6 708.7 reduce-scatter.19
where the time goes:
time: 3530 us; the launch traced here: 3510 us
  waiting for transfers between devices  2370 us (67%)
  other arithmetic  393 us (11%)
  local copies, waits for them, and re-layouts  318 us (9%)
  blocking collectives  204 us (6%)
  matrix products  203 us (6%)
    unnamed x18, waiting for transfers between devices  764 us
    reduce_scatter x1, waiting for transfers between devices, local(): lax.psum_scatter(layer_sum[2], ('dp', 'vocab'), scatter_dimension=1, tile...  708 us
    reduce_scatter x1, waiting for transfers between devices, local(): lax.psum_scatter(layer_sum[0], ('dp', 'vocab'), scatter_dimension=1, tile...  706 us
    reduce_scatter x1, waiting for transfers between devices, local(): lax.psum_scatter(layer_sum[1], ('dp', 'vocab'), scatter_dimension=1, tile...  183 us
    unnamed x10, other arithmetic  173 us
    unnamed x597, local copies, waits for them, and re-layouts  109 us
  transfers between devices with their start and end apart: 14, of which 6 were waited for; matrix products, arithmetic and copies ran while one was open for 23% of the time, Pallas kernels for 0%

commit v1 on v0

v1 whole, which is shorter than its diff:
```python
import functools
import math

import jax
import jax.numpy as jnp
from jax import lax
from jax.experimental import pallas as pl
from jax.experimental.pallas import tpu as pltpu
from jax.sharding import PartitionSpec as P

HEADS = 16
NORM_EPS = 1e-05
SCORE_SCALE = 0.125
NEG_FILL = -1e30
CLIP_LIMIT = 3.0
BETA_ONE = 0.9
BETA_TWO = 0.95
LEARN_RATE = 0.05
DECAY_RATE = 0.1
ADAM_EPS = 1e-08
BOTH = ("dp", "vocab")
MESH = pl.DeviceIdType.MESH
BF = jnp.bfloat16
F32 = jnp.float32
GROUPS = (3, 1, 1, 2, 1, 4, 4)
UNITS = tuple((group, index) for group, size in enumerate(GROUPS) for index in range(size))


def place():
    dp, x = lax.axis_index("dp"), lax.axis_index("vocab")
    return lax.div(dp, 4), lax.rem(lax.div(dp, 2), 2), lax.rem(dp, 2), x


def device(z, y, c, x):
    return ((z * 2 + y) * 2 + c, x)


def partners():
    z, y, c, x = place()
    line = [lax.rem(z + step, 4) for step in (1, 2, 3)]
    return (
        line,
        [device(other, y, c, x) for other in line],
        device(z, 1 - y, c, x),
        device(z, y, c, 1 - x),
        device(z, y, 1 - c, x),
    )


def greet(targets):
    barrier = pltpu.get_barrier_semaphore()
    for target in targets:
        pl.semaphore_signal(barrier, inc=1, device_id=target, device_id_type=MESH)
    pl.semaphore_wait(barrier, len(targets))


def transfer_order(heads):
    order, head = [], 0
    for unit in range(len(UNITS)):
        order.append(("b" if unit % 4 == 3 else "a", unit))
        if unit % 4 == 1 and head < heads:
            order.append(("h", head))
            head += 1
    return tuple(order)


def gather_kernel(order, delays, *refs):
    layer_ref, head_ref = refs[:2]
    outs, head_out = refs[2:9], refs[9]
    send_sem, recv_sem, local_sem = refs[10:]
    z, y, c, x = place()
    line, z_dev, y_dev, x_dev, c_dev = partners()
    greet(z_dev + [y_dev, x_dev, c_dev])

    def copy(src, dst, item, slot, target):
        return pltpu.make_async_remote_copy(
            src_ref=src,
            dst_ref=dst,
            send_sem=send_sem.at[item, slot],
            recv_sem=recv_sem.at[item, slot],
            device_id=target,
            device_id_type=MESH,
        )

    def whole(unit):
        group, index = UNITS[unit]
        return outs[group].at[index]

    own = []
    for unit in range(len(UNITS)):
        own.append(
            pltpu.make_async_copy(
                layer_ref.at[unit], whole(unit).at[z, y, c, x], local_sem.at[unit]
            )
        )
    own.append(
        pltpu.make_async_copy(head_ref, head_out.at[:, z, y, c], local_sem.at[len(UNITS)])
    )
    for piece in own:
        piece.start()
    count = len(order)

    def first(item):
        kind, unit = order[item]
        if kind == "h":
            src, dst = head_ref.at[unit], head_out.at[unit, z, y, c]
        else:
            src, dst = layer_ref.at[unit], whole(unit).at[z, y, c, x]
        return [copy(src, dst, item, slot, target) for slot, target in enumerate(z_dev)]

    def second(item):
        kind, unit = order[item]
        block = head_out.at[unit, :, y, c] if kind == "h" else whole(unit).at[:, y, c, x]
        return copy(block, block, item, 3, x_dev if kind == "b" else y_dev)

    def third(item):
        kind, unit = order[item]
        if kind == "h":
            return None
        block = whole(unit).at[:, :, c, x] if kind == "a" else whole(unit).at[:, y, c]
        return copy(block, block, item, 4, x_dev if kind == "a" else y_dev)

    def fourth(item):
        kind, unit = order[item]
        block = head_out.at[unit, :, :, c] if kind == "h" else whole(unit).at[:, :, c]
        return copy(block, block, item, 5, c_dev)

    for piece in own:
        piece.wait()
    late_two, late_three, late_four = delays
    for tick in range(count + late_four):
        if tick < count:
            for part in first(tick):
                part.start()
        item = tick - late_two
        if 0 <= item < count:
            for part in first(item):
                part.wait_recv()
            second(item).start()
        item = tick - late_three
        if 0 <= item < count:
            second(item).wait_recv()
            part = third(item)
            if part is not None:
                part.start()
        item = tick - late_four
        if 0 <= item < count:
            part = third(item)
            if part is not None:
                part.wait_recv()
            fourth(item).start()
    for item in range(count):
        fourth(item).wait_recv()
        for part in first(item) + [second(item), third(item), fourth(item)]:
            if part is not None:
                part.wait_send()


def gather_fast(layer, head):
    order = transfer_order(head.shape[0])
    count = len(order)
    shapes = [jax.ShapeDtypeStruct((size, 4, 2, 2, 2) + layer.shape[1:], BF) for size in GROUPS]
    shapes.append(jax.ShapeDtypeStruct((head.shape[0], 4, 2, 2) + head.shape[1:], BF))
    results = pl.pallas_call(
        functools.partial(gather_kernel, order, (1, 2, 3)),
        out_shape=tuple(shapes),
        in_specs=[pl.BlockSpec(memory_space=pltpu.VMEM)] * 2,
        out_specs=(pl.BlockSpec(memory_space=pl.ANY),) * len(shapes),
        scratch_shapes=[
            pltpu.SemaphoreType.DMA((count, 6)),
            pltpu.SemaphoreType.DMA((count, 6)),
            pltpu.SemaphoreType.DMA((len(UNITS) + 1,)),
        ],
        compiler_params=pltpu.CompilerParams(
            collective_id=1, has_side_effects=True, vmem_limit_bytes=32 * 2**20
        ),
    )(layer, head)
    weights = [
        part.reshape(size, -1, part.shape[-1]) for size, part in zip(GROUPS, results[:7])
    ]
    return weights, results[7].reshape(head.shape[0], -1, head.shape[2])


def reduce_kernel(order, delays, *refs):
    grads, head_grad = refs[:7], refs[7]
    out, head_out = refs[8:10]
    core_in, first_in, second_in, line_in, head_core, head_y, head_line, own, send_sem, recv_sem, local_sem = refs[10:]
    z, y, c, x = place()
    line, z_dev, y_dev, x_dev, c_dev = partners()
    greet(z_dev + [y_dev, x_dev, c_dev])
    count, slots = len(order), own.shape[0]

    def copy(src, dst, item, slot, target):
        return pltpu.make_async_remote_copy(
            src_ref=src,
            dst_ref=dst,
            send_sem=send_sem.at[item, slot],
            recv_sem=recv_sem.at[item, slot],
            device_id=target,
            device_id_type=MESH,
        )

    def whole(kind, unit):
        if kind == "h":
            return head_grad.at[unit]
        group, index = UNITS[unit]
        return grads[group].at[index]

    def to_core(item):
        kind, unit = order[item]
        target = head_core.at[unit] if kind == "h" else core_in.at[unit]
        return copy(whole(kind, unit).at[:, :, 1 - c], target, item, 0, c_dev)

    def own_half(item):
        kind, unit = order[item]
        slot = own.at[item % slots]
        if kind == "h":
            slot = slot.reshape(head_core.shape[1:])
        return pltpu.make_async_copy(whole(kind, unit).at[:, :, c], slot, local_sem.at[item % slots])

    def first(item):
        kind, unit = order[item]
        if kind == "h":
            return None
        if kind == "a":
            return copy(core_in.at[unit, :, :, 1 - x], first_in.at[unit], item, 1, x_dev)
        return copy(core_in.at[unit, :, 1 - y], first_in.at[unit], item, 1, y_dev)

    def second(item):
        kind, unit = order[item]
        if kind == "h":
            return copy(head_core.at[unit, :, 1 - y], head_y.at[unit], item, 2, y_dev)
        if kind == "a":
            return copy(first_in.at[unit, :, 1 - y], second_in.at[unit], item, 2, y_dev)
        return copy(first_in.at[unit, :, 1 - x], second_in.at[unit], item, 2, x_dev)

    def third(item):
        kind, unit = order[item]
        parts = []
        for slot, other in enumerate(line):
            if kind == "h":
                src, dst = head_y.at[unit, other], head_line.at[unit, slot]
            else:
                src, dst = second_in.at[unit, other], line_in.at[unit, slot]
            parts.append(copy(src, dst, item, 3 + slot, z_dev[slot]))
        return parts

    def wide(value):
        return value.astype(F32)

    late_one, late_two, late_three, late_four = delays
    for tick in range(count + late_four):
        if tick < count:
            to_core(tick).start()
            own_half(tick).start()
        item = tick - late_one
        if 0 <= item < count:
            kind, unit = order[item]
            own_half(item).wait()
            to_core(item).wait_recv()

            def join_core(k, carry):
                kept = own[item % slots, k]
                if kind == "h":
                    kept = kept.reshape(head_core.shape[2:])
                    head_core[unit, k] = (wide(head_core[unit, k]) + wide(kept)).astype(BF)
                else:
                    core_in[unit, k] = (wide(core_in[unit, k]) + wide(kept)).astype(BF)
                return carry

            lax.fori_loop(0, 4, join_core, 0)
            if kind != "h":
                first(item).start()
        item = tick - late_two
        if 0 <= item < count:
            kind, unit = order[item]
            if kind != "h":
                first(item).wait_recv()

                def join_first(k, carry):
                    kept = core_in[unit, k, :, x] if kind == "a" else core_in[unit, k, y]
                    first_in[unit, k] = (wide(first_in[unit, k]) + wide(kept)).astype(BF)
                    return carry

                lax.fori_loop(0, 4, join_first, 0)
            second(item).start()
        item = tick - late_three
        if 0 <= item < count:
            kind, unit = order[item]
            second(item).wait_recv()

            def join_second(k, carry):
                if kind == "h":
                    head_y[unit, k] = (wide(head_y[unit, k]) + wide(head_core[unit, k, y])).astype(BF)
                else:
                    kept = first_in[unit, k, y if kind == "a" else x]
                    second_in[unit, k] = (wide(second_in[unit, k]) + wide(kept)).astype(BF)
                return carry

            lax.fori_loop(0, 4, join_second, 0)
            for part in third(item):
                part.start()
        item = tick - late_four
        if 0 <= item < count:
            kind, unit = order[item]
            for part in third(item):
                part.wait_recv()
            held, landed = (head_y, head_line) if kind == "h" else (second_in, line_in)
            total = wide(held[unit, z])
            for slot in range(3):
                total = total + wide(landed[unit, slot])
            if kind == "h":
                head_out[unit] = total
            else:
                out[unit] = total
    for item in range(count):
        for part in [to_core(item), first(item), second(item)] + third(item):
            if part is not None:
                part.wait_send()


def reduce_fast(grads, head_grad):
    books, rows, width = head_grad.shape
    order = transfer_order(books)
    count = len(order)
    deep, head_deep = grads[0].shape[1] // 32, rows // 16
    split = [g.reshape(g.shape[0], 4, 2, 2, 2, deep, g.shape[2]) for g in grads]
    head_split = head_grad.reshape(books, 4, 2, 2, head_deep, width)
    tile, head_tile = (deep, grads[0].shape[2]), (head_deep, width)
    units = len(UNITS)
    vmem = pltpu.VMEM
    return pl.pallas_call(
        functools.partial(reduce_kernel, order, (2, 5, 8, 10)),
        out_shape=(
            jax.ShapeDtypeStruct((units,) + tile, F32),
            jax.ShapeDtypeStruct((books,) + head_tile, F32),
        ),
        in_specs=[pl.BlockSpec(memory_space=pl.ANY)] * 8,
        out_specs=(pl.BlockSpec(memory_space=vmem),) * 2,
        scratch_shapes=[
            vmem((units, 4, 2, 2) + tile, BF),
            vmem((units, 4, 2) + tile, BF),
            vmem((units, 4) + tile, BF),
            vmem((units, 3) + tile, BF),
            vmem((books, 4, 2) + head_tile, BF),
            vmem((books, 4) + head_tile, BF),
            vmem((books, 3) + head_tile, BF),
            vmem((4, 4, 2, 2) + tile, BF),
            pltpu.SemaphoreType.DMA((count, 6)),
            pltpu.SemaphoreType.DMA((count, 6)),
            pltpu.SemaphoreType.DMA((4,)),
        ],
        compiler_params=pltpu.CompilerParams(
            collective_id=2, has_side_effects=True, vmem_limit_bytes=58 * 2**20
        ),
    )(*split, head_split)


def lookup_kernel(ids_ref, table_ref, out_ref, stacked):
    books, columns, lanes = stacked.shape[0], out_ref.shape[1], stacked.shape[2]
    width = out_ref.shape[2]
    high_count = stacked.shape[1] // columns

    @pl.when(pl.program_id(0) == 0)
    def _():
        for book in range(books):
            for high in range(high_count):
                stacked[book, high * columns : (high + 1) * columns, :] = table_ref[
                    book, :, high * lanes : (high + 1) * lanes
                ].astype(BF)

    total = jnp.zeros((columns, width), F32)
    spread = lax.broadcasted_iota(jnp.int32, (lanes, width), 0)
    for book in range(books):
        ids = ids_ref[0, book : book + 1, :]
        low = ids % lanes
        high_ids = ids // lanes
        hot = jnp.where(spread == low, 1.0, 0.0).astype(BF)
        found = jnp.dot(stacked[book], hot, preferred_element_type=F32)
        for high in range(high_count):
            total = total + jnp.where(
                high_ids == high, found[high * columns : (high + 1) * columns], 0.0
            )
    out_ref[0] = total


def lookup(ids, table_t):
    blocks, books, width = ids.shape
    columns, rows = table_t.shape[1:]
    lanes = 256
    high_count = -(-rows // lanes)
    padded = jnp.pad(table_t, ((0, 0), (0, 0), (0, high_count * lanes - rows)))
    return pl.pallas_call(
        lookup_kernel,
        grid=(blocks,),
        out_shape=jax.ShapeDtypeStruct((blocks, columns, width), F32),
        in_specs=[
            pl.BlockSpec((1, books, width), lambda i: (i, 0, 0)),
            pl.BlockSpec(padded.shape, lambda i: (0, 0, 0)),
        ],
        out_specs=pl.BlockSpec((1, columns, width), lambda i: (i, 0, 0)),
        scratch_shapes=[pltpu.VMEM((books, high_count * columns, lanes), BF)],
        compiler_params=pltpu.CompilerParams(vmem_limit_bytes=40 * 2**20),
    )(ids, padded)


def spread_kernel(ids_ref, rows_ref, out_ref, total):
    books, columns, rows = out_ref.shape
    width = rows_ref.shape[2]
    lanes = total.shape[2]
    high_count = total.shape[1] // columns
    step = pl.program_id(0)

    @pl.when(step == 0)
    def _():
        total[...] = jnp.zeros_like(total)

    values = rows_ref[0].astype(F32)
    spread = lax.broadcasted_iota(jnp.int32, (lanes, width), 0)
    for book in range(books):
        ids = ids_ref[0, book : book + 1, :]
        low = ids % lanes
        high_ids = ids // lanes
        hot = jnp.where(spread == low, 1.0, 0.0).astype(BF)
        parted = jnp.concatenate(
            [jnp.where(high_ids == high, values, 0.0) for high in range(high_count)], axis=0
        ).astype(BF)
        total[book] += lax.dot_general(
            parted, hot, (((1,), (1,)), ((), ())), preferred_element_type=F32
        )

    @pl.when(step == pl.num_programs(0) - 1)
    def _():
        for book in range(books):
            for high in range(high_count):
                first = high * lanes
                last = min(rows, first + lanes)
                out_ref[book, :, first:last] = total[
                    book, high * columns : (high + 1) * columns, : last - first
                ]


def spread_rows(ids, values, rows):
    blocks, books, width = ids.shape
    columns = values.shape[1]
    lanes = 256
    high_count = -(-rows // lanes)
    return pl.pallas_call(
        spread_kernel,
        grid=(blocks,),
        out_shape=jax.ShapeDtypeStruct((books, columns, rows), F32),
        in_specs=[
            pl.BlockSpec((1, books, width), lambda i: (i, 0, 0)),
            pl.BlockSpec((1, columns, width), lambda i: (i, 0, 0)),
        ],
        out_specs=pl.BlockSpec((books, columns, rows), lambda i: (0, 0, 0)),
        scratch_shapes=[pltpu.VMEM((books, high_count * columns, lanes), F32)],
        compiler_params=pltpu.CompilerParams(vmem_limit_bytes=40 * 2**20),
    )(ids, values)


def low(values):
    return values.astype(BF)


def ein(formula, left, right):
    return jnp.einsum(formula, left, right, preferred_element_type=F32)


def norm_stats(values):
    average = jnp.mean(values, axis=-1, keepdims=True)
    centred = values - average
    spread = jnp.mean(centred * centred, axis=-1, keepdims=True)
    scale = lax.rsqrt(spread + NORM_EPS)
    return centred * scale, scale


def norm_forward(values, gain, bias):
    hat, scale = norm_stats(values)
    return hat * (1.0 + gain) + bias


def norm_backward(values, gain, cotangent):
    hat, scale = norm_stats(values)
    scaled = cotangent * (1.0 + gain)
    mean_one = jnp.mean(scaled, axis=-1, keepdims=True)
    mean_two = jnp.mean(scaled * hat, axis=-1, keepdims=True)
    return (
        (scaled - mean_one - hat * mean_two) * scale,
        jnp.sum(cotangent * hat, axis=0),
        jnp.sum(cotangent, axis=0),
    )


def sinusoid(frames, model_width):
    half_width = model_width // 2
    freq_rates = jnp.exp(
        jnp.arange(half_width, dtype=F32) * (-math.log(10000.0) / (half_width - 1))
    )
    angles = jnp.arange(frames, dtype=F32)[:, None] * freq_rates[None, :]
    return jnp.concatenate([jnp.sin(angles), jnp.cos(angles)], axis=1)


def delay_ids(codes, offsets, special):
    frames = codes.shape[2]
    frame = jnp.arange(frames, dtype=jnp.int32)[None, None, :]
    inputs = jnp.full_like(codes, special)
    targets = jnp.full_like(codes, special)
    padded = jnp.pad(codes, ((0, 0), (0, 0), (4, 0)), constant_values=special)
    for shift in range(4):
        is_shift = (offsets == shift)[:, :, None]
        targets = jnp.where(is_shift, padded[:, :, 4 - shift : 4 - shift + frames], targets)
        inputs = jnp.where(is_shift, padded[:, :, 3 - shift : 3 - shift + frames], inputs)
    return inputs, targets


def split_heads(matrix, clips):
    return matrix.reshape(clips, matrix.shape[0] // clips, HEADS, -1)


def raw_scores(queries, keyset, causal):
    scores = ein("bqhe,bkhe->bhqk", queries, keyset) * SCORE_SCALE
    if causal:
        length = scores.shape[2]
        allowed = jnp.arange(length)[:, None] >= jnp.arange(length)[None, :]
        scores = jnp.where(allowed[None, None], scores, NEG_FILL)
    return scores


def attend_forward(queries, keyset, valset, clips, causal):
    queries, keyset, valset = (split_heads(m, clips) for m in (queries, keyset, valset))
    scores = raw_scores(queries, keyset, causal)
    highest = jnp.max(scores, axis=-1, keepdims=True)
    exponents = jnp.exp(scores - highest)
    denominator = jnp.sum(exponents, axis=-1, keepdims=True)
    probs = exponents / denominator
    mixed = ein("bhqk,bkhe->bqhe", low(probs), valset)
    return low(mixed).reshape(mixed.shape[0] * mixed.shape[1], -1), probs


def attend_backward(queries, keyset, valset, probs, grad_mixed, clips):
    queries, keyset, valset, grad_mixed = (
        split_heads(m, clips) for m in (queries, keyset, valset, grad_mixed)
    )
    grad_probs = ein("bqhe,bkhe->bhqk", grad_mixed, valset)
    grad_values = low(ein("bhqk,bqhe->bkhe", low(probs), grad_mixed))
    grad_scores = low(
        probs * (grad_probs - jnp.sum(probs * grad_probs, axis=-1, keepdims=True))
    )
    grad_queries = low(ein("bhqk,bkhe->bqhe", grad_scores, keyset) * SCORE_SCALE)
    grad_keys = low(ein("bhqk,bqhe->bkhe", grad_scores, queries) * SCORE_SCALE)
    return tuple(
        m.reshape(m.shape[0] * m.shape[1], -1) for m in (grad_queries, grad_keys, grad_values)
    )


def normal_cdf(values):
    return 0.5 * (1.0 + lax.erf(values * math.sqrt(0.5)))


def adam_step(weight, first_moment, second_moment, gradient, factor, corr_one, corr_two):
    clipped = gradient * factor
    first_next = BETA_ONE * first_moment + (1.0 - BETA_ONE) * clipped
    second_next = BETA_TWO * second_moment + (1.0 - BETA_TWO) * clipped * clipped
    update = (
        first_next / corr_one / (jnp.sqrt(second_next / corr_two) + ADAM_EPS) + DECAY_RATE * weight
    )
    return (weight - LEARN_RATE * update, first_next, second_next)


def columns_apart(matrix, pieces):
    count, rows, width = matrix.shape
    parts = matrix.reshape(count, rows, pieces, width // pieces).transpose(0, 2, 1, 3)
    return parts.reshape(count * pieces, rows, width // pieces)


def columns_together(parts, pieces):
    total, rows, width = parts.shape
    matrix = parts.reshape(total // pieces, pieces, rows, width).transpose(0, 2, 1, 3)
    return matrix.reshape(total // pieces, rows, pieces * width)


def local(
    fast,
    audio_codes,
    delay_offsets,
    clip_lengths,
    loss_positions,
    teacher_ids,
    text_states,
    step_count,
    in_proj,
    in_proj_mean,
    in_proj_sq,
    out_proj,
    out_proj_mean,
    out_proj_sq,
    ffn_proj,
    ffn_proj_mean,
    ffn_proj_sq,
    embed_table,
    embed_table_mean,
    embed_table_sq,
    head_table,
    head_table_mean,
    head_table_sq,
    norm_gain,
    norm_gain_mean,
    norm_gain_sq,
    norm_bias,
    norm_bias_mean,
    norm_bias_sq,
):
    clips = text_states.shape[0]
    vocab_count = lax.axis_size("vocab")
    device_count = lax.axis_size("dp") * vocab_count
    vocab_index = lax.axis_index("vocab")
    book_count = head_table.shape[0]
    pos_count = loss_positions.shape[1]
    frames = audio_codes.shape[2]
    table_rows = embed_table.shape[1]
    special = table_rows - 1
    half_vocab = head_table.shape[2]
    vocab_base = vocab_index * half_vocab
    model_width = text_states.shape[2]
    rows = clips * frames
    ffn_pieces = ffn_proj.shape[2] // model_width
    denominator = float(clips * device_count * pos_count * book_count)

    inputs, targets = delay_ids(audio_codes, delay_offsets, special)
    own_first = vocab_index * clips
    own_inputs = lax.dynamic_slice_in_dim(inputs, own_first, clips, 0)
    own_positions = lax.dynamic_slice_in_dim(loss_positions, own_first, clips, 0)

    layer_local = jnp.concatenate(
        [
            low(in_proj[0:3]),
            low(out_proj[0:1]),
            low(in_proj[3:6]),
            low(out_proj[1:2]),
            columns_apart(low(ffn_proj), ffn_pieces),
        ],
        axis=0,
    )
    head_local = low(head_table)
    norms = lax.all_gather(
        low(jnp.concatenate([norm_gain, norm_bias], axis=0)), BOTH, axis=1, tiled=True
    ).astype(F32)
    gains, biases = norms[:4], norms[4:]
    if fast:
        all_inputs = lax.all_gather(inputs, "dp", axis=0, tiled=True)
        block_ids = (
            all_inputs.reshape(device_count, clips, book_count, frames)
            .transpose(0, 2, 1, 3)
            .reshape(device_count, book_count, rows)
        )
        table_t = jnp.swapaxes(embed_table, 1, 2)
        looked = lookup(block_ids, table_t)
        looked = lax.all_to_all(looked, BOTH, 0, 0, tiled=True)
        embedded = looked.reshape(model_width, rows).T
        layer_parts, head_all = gather_fast(layer_local, head_local)
    else:
        table = lax.all_gather(low(embed_table), BOTH, axis=2, tiled=True)
        embedded = jnp.zeros((rows, model_width), F32)
        for book in range(book_count):
            embedded = embedded + jnp.take(
                table[book], own_inputs[:, book].reshape(-1), axis=0
            ).astype(F32)
        layer_all = lax.all_gather(layer_local, BOTH, axis=1, tiled=True)
        starts = [sum(GROUPS[:g]) for g in range(len(GROUPS))]
        layer_parts = [layer_all[s : s + g] for s, g in zip(starts, GROUPS)]
        head_all = lax.all_gather(head_local, "dp", axis=1, tiled=True)
    w_self, w_self_out, w_query, w_text, w_cross_out, w_up, w_down = layer_parts

    start = embedded + jnp.tile(sinusoid(frames, model_width), (clips, 1))
    normed_self = low(norm_forward(start, gains[0], biases[0]))
    proj = low(ein("rd,kde->kre", normed_self, w_self))
    self_out, self_probs = attend_forward(proj[0], proj[1], proj[2], clips, True)
    after_self = start + ein("rd,de->re", self_out, w_self_out[0])
    normed_cross = low(norm_forward(after_self, gains[1], biases[1]))
    cross_query = low(ein("rd,de->re", normed_cross, w_query[0]))
    text = text_states.reshape(-1, model_width)
    cross_text = low(ein("td,kde->kte", text, w_text))
    cross_out, cross_probs = attend_forward(cross_query, cross_text[0], cross_text[1], clips, False)
    after_cross = after_self + ein("rd,de->re", cross_out, w_cross_out[0])
    normed_ffn = low(norm_forward(after_cross, gains[2], biases[2]))
    upper = ein("rd,jdf->jrf", normed_ffn, w_up)
    cdf = normal_cdf(upper)
    active = low(upper * cdf)
    after_ffn = after_cross + ein("jrf,jdf->rd", active, w_down)
    final_norm = low(norm_forward(after_ffn, gains[3], biases[3]))
    flat_positions = (own_positions + jnp.arange(clips, dtype=jnp.int32)[:, None] * frames).reshape(-1)
    pick = flat_positions[:, None] == jnp.arange(rows, dtype=jnp.int32)[None, :]
    chosen = low(ein("pr,rd->pd", pick.astype(BF), final_norm))

    pair_rows = lax.all_gather(chosen, "vocab", axis=0, tiled=True)
    pair_count = pair_rows.shape[0]
    target_at = jnp.take_along_axis(targets, loss_positions[:, None, :], axis=2)
    target_at = target_at.transpose(1, 0, 2).reshape(book_count, pair_count)
    teach = teacher_ids.transpose(1, 0, 2, 3).reshape(book_count, pair_count, -1)
    row_weight = (loss_positions < clip_lengths[:, None]).astype(F32).reshape(pair_count)
    local_ids = vocab_base + jnp.arange(half_vocab, dtype=jnp.int32)
    counts = jnp.sum(
        (teach[:, :, :, None] == local_ids[None, None, None, :]).astype(F32), axis=2
    )
    valid = (target_at != special).astype(F32)
    wanted = counts / teach.shape[2] + valid[:, :, None] * (
        target_at[:, :, None] == local_ids[None, None, :]
    ).astype(F32)
    logits = ein("rd,kdv->krv", pair_rows, head_all)
    highest = jnp.max(logits, axis=-1)
    exp_sum = jnp.sum(jnp.exp(logits - highest[:, :, None]), axis=-1)
    stats = lax.all_gather(jnp.stack([highest, exp_sum]), "vocab")
    top_all = jnp.max(stats[:, 0], axis=0)
    sum_all = jnp.sum(stats[:, 1] * jnp.exp(stats[:, 0] - top_all[None]), axis=0)
    log_total = top_all + jnp.log(sum_all)
    row_loss = row_weight[None, :] * (valid + 1.0) * log_total
    own_rows = clips * pos_count
    loss_sum = jnp.sum(
        lax.dynamic_slice_in_dim(row_loss, vocab_index * own_rows, own_rows, 1)
    ) - jnp.sum(row_weight[None, :] * jnp.sum(wanted * logits, axis=-1))
    scaled = (row_weight / denominator)[None, :, None]
    grad_logits = low(
        scaled * ((valid + 1.0)[:, :, None] * jnp.exp(logits - log_total[:, :, None]) - wanted)
    )
    grad_head = ein("rd,krv->kdv", pair_rows, grad_logits)
    grad_rows = ein("krv,kdv->rd", grad_logits, head_all)
    grad_chosen = lax.psum_scatter(low(grad_rows), "vocab", scatter_dimension=0, tiled=True).astype(F32)

    grad_final = jnp.einsum(
        "pr,pd->rd", pick.astype(F32), grad_chosen, precision=lax.Precision.HIGHEST
    )
    grad_ffn_res, gain_three, bias_three = norm_backward(after_ffn, gains[3], grad_final)
    low_ffn = low(grad_ffn_res)
    grad_down = ein("rd,jrf->jdf", low_ffn, active)
    grad_active = ein("rd,jdf->jrf", low_ffn, w_down)
    slope = cdf + upper * jnp.exp(-0.5 * upper * upper) * (1.0 / math.sqrt(2.0 * math.pi))
    grad_upper = low(grad_active * slope)
    grad_up = ein("rd,jrf->jdf", normed_ffn, grad_upper)
    grad_normed = ein("jrf,jdf->rd", grad_upper, w_up)
    grad_inner, gain_two, bias_two = norm_backward(after_cross, gains[2], grad_normed)
    grad_cross_res = grad_ffn_res + grad_inner
    low_cross = low(grad_cross_res)
    grad_cross_out = ein("rd,re->de", cross_out, low_cross)[None]
    grad_mixed = low(ein("re,de->rd", low_cross, w_cross_out[0]))
    grad_query, grad_key, grad_value = attend_backward(
        cross_query, cross_text[0], cross_text[1], cross_probs, grad_mixed, clips
    )
    grad_w_query = ein("rd,re->de", normed_cross, grad_query)[None]
    grad_w_text = ein("td,kte->kde", text, jnp.stack([grad_key, grad_value]))
    grad_normed = ein("re,de->rd", grad_query, w_query[0])
    grad_inner, gain_one, bias_one = norm_backward(after_self, gains[1], grad_normed)
    grad_self_res = grad_cross_res + grad_inner
    low_self = low(grad_self_res)
    grad_self_out = ein("rd,re->de", self_out, low_self)[None]
    grad_mixed = low(ein("re,de->rd", low_self, w_self_out[0]))
    grad_proj = jnp.stack(
        attend_backward(proj[0], proj[1], proj[2], self_probs, grad_mixed, clips)
    )
    grad_w_self = ein("rd,kre->kde", normed_self, grad_proj)
    grad_normed = ein("kre,kde->rd", grad_proj, w_self)
    grad_inner, gain_zero, bias_zero = norm_backward(start, gains[0], grad_normed)
    grad_start = grad_self_res + grad_inner

    layer_grads = (
        grad_w_self, grad_self_out, grad_w_query, grad_w_text, grad_cross_out, grad_up, grad_down
    )
    norm_grads = jnp.stack(
        [gain_zero, gain_one, gain_two, gain_three, bias_zero, bias_one, bias_two, bias_three]
    )
    norm_shard = lax.psum_scatter(norm_grads, BOTH, scatter_dimension=1, tiled=True)
    if fast:
        parted = low(grad_start).T.reshape(device_count, -1, rows)
        parted = lax.all_to_all(parted, BOTH, 0, 0, tiled=True)
        embed_shard = jnp.swapaxes(spread_rows(block_ids, parted, table_rows), 1, 2)
        layer_shard, head_shard = reduce_fast([low(g) for g in layer_grads], low(grad_head))
    else:
        embed_sum = jnp.stack(
            [
                jax.ops.segment_sum(
                    grad_start, own_inputs[:, book].reshape(-1), num_segments=table_rows
                )
                for book in range(book_count)
            ]
        )
        embed_shard = lax.psum_scatter(embed_sum, BOTH, scatter_dimension=2, tiled=True)
        layer_shard = lax.psum_scatter(
            jnp.concatenate(layer_grads, axis=0), BOTH, scatter_dimension=1, tiled=True
        )
        head_shard = lax.psum_scatter(grad_head, "dp", scatter_dimension=1, tiled=True)
    gradients = (
        jnp.concatenate([layer_shard[0:3], layer_shard[4:7]], axis=0),
        jnp.concatenate([layer_shard[3:4], layer_shard[7:8]], axis=0),
        columns_together(layer_shard[8:], ffn_pieces),
        embed_shard,
        head_shard,
        norm_shard[:4],
        norm_shard[4:],
    )
    square_sum = jnp.zeros((), F32)
    for shard_grad in gradients:
        square_sum = square_sum + jnp.sum(shard_grad * shard_grad)
    square_total, loss_total = lax.psum((square_sum, loss_sum), BOTH)
    loss_value = loss_total / denominator
    grad_norm = jnp.sqrt(square_total)
    factor = CLIP_LIMIT / jnp.maximum(grad_norm, CLIP_LIMIT)
    steps_float = step_count.astype(F32)
    corr_one = 1.0 - jnp.power(BETA_ONE, steps_float)
    corr_two = 1.0 - jnp.power(BETA_TWO, steps_float)
    masters = (in_proj, out_proj, ffn_proj, embed_table, head_table, norm_gain, norm_bias)
    mean_list = (
        in_proj_mean,
        out_proj_mean,
        ffn_proj_mean,
        embed_table_mean,
        head_table_mean,
        norm_gain_mean,
        norm_bias_mean,
    )
    square_list = (
        in_proj_sq,
        out_proj_sq,
        ffn_proj_sq,
        embed_table_sq,
        head_table_sq,
        norm_gain_sq,
        norm_bias_sq,
    )
    outputs = [loss_value, grad_norm]
    for index in range(7):
        outputs.extend(
            adam_step(
                masters[index],
                mean_list[index],
                square_list[index],
                gradients[index],
                factor,
                corr_one,
                corr_two,
            )
        )
    return tuple(outputs)


def solution(mesh):
    by_row = P(None, BOTH, None)
    by_column = P(None, None, BOTH)
    by_head = P(None, "dp", "vocab")
    by_feature = P(None, BOTH)
    weights = (
        (by_row,) * 9 + (by_column,) * 3 + (by_head,) * 3 + (by_feature,) * 6
    )
    placed = (
        P("dp", None, None),
        P("dp", None),
        P("dp"),
        P("dp", None),
        P("dp", None, None, None),
        P(BOTH, None, None),
        P(),
    ) + weights
    fast = dict(mesh.shape) == {"dp": 16, "vocab": 2}
    return jax.shard_map(
        functools.partial(local, fast),
        mesh=mesh,
        in_specs=placed,
        out_specs=(P(), P()) + weights,
        check_vma=False,
    )
```

time: 3530 us -> 857 us (0.24)
  waiting for transfers between devices: 2370 us -> 2.23 us
  Pallas kernels: 0 us -> 430 us
  other arithmetic: 393 us -> 61.5 us
  local copies, waits for them, and re-layouts: 318 us -> 72.9 us
  matrix products: 203 us -> 108 us
  blocking collectives: 204 us -> 143 us
    reduce_scatter x5 -> x1, waiting for transfers between devices: 1600 us -> 2.17 us  [local(): lax.psum_scatter(low(grad_rows), 'vocab', scatter_dimension=0, tiled=True)]
    unnamed x18 -> x3, waiting for transfers between devices: 764 us -> 0.05 us
    pallas_call x0 -> x4, Pallas kernels: none -> 430 us  [the longest x1 211 us: reduce_fast(): pl.pallas_call(functools.partial(reduce_kernel, order, (2, 5, 8, 10)), ou...]
    unnamed x10 -> x4, other arithmetic: 173 us -> 0.01 us
    dot_general x70 -> x35, matrix products: 203 us -> 100 us  [the longest x34 97.5 us: ein(): return jnp.einsum(formula, left, right, preferred_element_type=F32)]
    add x21 -> x5, other arithmetic: 104 us -> 2.05 us  [the longest x1 0.64 us: local(): own_positions + jnp.arange(clips, dtype=jnp.int32)[:, None] * frames]
    unnamed x597 -> x290, local copies, waits for them, and re-layouts: 109 us -> 16.7 us
    add x3 -> x0, local copies, waits for them, and re-layouts: 87.3 us -> none  [the longest x1 37.4 us: local(): embed_sum = embed_part if embed_sum is None else embed_sum + embed_part]
  transfers between devices with their start and end apart: 14 -> 4, of which waited for: 6 -> 1; matrix products, arithmetic and copies ran while one was open for 23% -> 7% of each run, Pallas kernels for 0% -> 47%
where the time goes in v1:
time: 857 us; the launch traced here: 852 us
  Pallas kernels  430 us (50%)
  blocking collectives  143 us (17%)
  matrix products  108 us (13%)
  local copies, waits for them, and re-layouts  72.9 us (9%)
  other arithmetic  61.5 us (7%)
  between operations  26.4 us (3%)
    pallas_call x1, Pallas kernels, reduce_fast(): pl.pallas_call(functools.partial(reduce_kernel, order, (2, 5, 8, 10)), ou...  211 us
    pallas_call x1, Pallas kernels, gather_fast(): pl.pallas_call(functools.partial(gather_kernel, order, (1, 2, 3)), out_sh...  190 us
    dot_general x34, matrix products, ein(): return jnp.einsum(formula, left, right, preferred_element_type=F32)  97.5 us
    all_gather x1, blocking collectives, local(): lax.all_gather(low(jnp.concatenate([norm_gain, norm_bias], axis=0)), BOTH...  68.9 us
    psum x1, blocking collectives, local(): square_total, loss_total = lax.psum((square_sum, loss_sum), BOTH)  39.6 us
    all_gather x1, blocking collectives, local(): all_inputs = lax.all_gather(inputs, 'dp', axis=0, tiled=True)  23.4 us
    reduce_sum x1, other arithmetic, local(): jnp.sum((teach[:, :, :, None] == local_ids[None, None, None, :]).astype(F...  20.3 us
  transfers between devices with their start and end apart: 4, of which 1 were waited for; matrix products, arithmetic and copies ran while one was open for 7% of the time, Pallas kernels for 47%

profile of v1, /device:TPU:0, one launch (start us, length us, event | category | flops | bytes accessed | tf_op | source)
XLA Modules:
  0.0 851.8 jit_solution(14950351031013607720)
XLA Ops:
  10.1 23.4 %all_gather.15 = s32[64,4,128]{2,1,0:T(4,128)S(1)} all-gather(s32[4,4,128]{2,1,0:T(4,128)S(1)} %copy.222), channel_id=1, replica_groups=mesh['dp'=16,'vocab'=2] {'dp'}, dimensions={0}, use_global_device_ids=true | all-gather | bytes 139264 | tf_op jit(solution)/shard_map/all_gather | solution.py:651
  33.9 16.0 %shard_map.444 = f32[32,32,256]{2,1,0:T(8,128)} custom-call(s32[32,4,256]{2,1,0:T(4,128)S(1)} %reshape.317.ids_ref, f32[4,32,2304]{2,1,0:T(8,128)S(1)} %pad.9.table_ref), custom_call_target="tpu_custom_call" | custom-call | tf_op jit(solution)/shard_map/pallas_call | solution.py:393
  49.8 3.5 all-to-all-start
  57.8 20.3 %convert_reduce_fusion = f32[4,128,1024]{2,1,0:T(8,128)} fusion(s32[1024]{0:T(1024)S(1)} %iota_add_fusion, s32[4,128,64]{2,1,0:T(8,128)S(1)} %bitcast.332), kind=kLoop, calls=%fused_computation.3 | loop fusion | flops 100139008 | bytes 2232320 | tf_op jit(solution)/shard_map/reduce_sum | solution.py:703
  81.3 68.9 %all-gather.1 = bf16[32,32,8]{1,2,0:T(8,128)(2,1)S(1)} all-gather(bf16[1,32,8]{1,2,0:T(8,128)(2,1)S(1)} %maximum_bitcast_fusion), channel_id=1, replica_groups=mesh['dp'=16,'vocab'=2] {'dp','vocab'}, dimensions={0}, use_global_device_ids=true | all-gather | bytes 16896 | tf_op jit(solution)/shard_map/all_gather | solution.py:646
  152.0 3.0 copy.243
  157.2 190.1 %shard_map.443 = (bf16[3,4,2,2,2,32,1024]{6,5,4,3,2,1,0:T(8,128)(2,1)S(1)}, bf16[1,4,2,2,2,32,1024]{6,5,4,3,2,1,0:T(8,128)(2,1)S(1)}, bf16[1,4,2,2,2,32,1024]{6,...) custom-call(bf16[16,32,1024]{2,1,0:T(8,128)(2,1)S(1)} %copy-done.5, ...), custom_call_target="tpu_custom_call" | custom-call | tf_op jit(solution)/shard_map/pallas_call | solution.py:164
  347.3 2.7 copy-done.6
  358.1 2.5 copy.224
  362.5 4.8 fusion.21
  374.3 4.0 fusion.147
  378.4 2.1 fusion.31
  384.4 2.7 reshape.376
  387.1 2.8 copy.234
  389.9 3.3 fusion.153
  396.8 8.8 %fusion.11 = (bf16[4,256,1024]{1,2,0:T(8,128)(2,1)S(1)}, f32[4,1024,256]{2,1,0:T(8,128)}) fusion(bf16[4,1024,1024]{2,1,0:T(8,128)(2,1)} %bitcast.374, f32[256,1024]{1,0:T(8,128)S(1)} %get-tuple-element.130, f32[1024]{0:T(1024)S(1)} %bitcast.358, f32[1024]{0:T(1024)S(1)} %bitcast.349, f32[256]{0:T(256)S(1)} %add_rsqrt_fusion.1, ...), kind=kOutput, calls=%fused_computation.19 | convolution fusion | flops 2154037248 | bytes 15738880 | tf_op jit(solution)/shard_map/rd,jdf->jrf/dot_general | solution.py:467
  405.6 2.5 fusion.157
  408.9 7.0 all_gather.17
  415.9 2.4 bitcast_reduce_fusion
  419.1 4.3 all-gather
  426.4 4.8 fusion.38
  434.0 7.0 convolution_convert_fusion
  441.0 2.2 reduce-scatter.5.cloned.1.call-done
  443.1 2.7 multiply_reduce_fusion.2
  446.3 6.6 fusion.7
  453.0 3.2 multiply_reduce_fusion.3
  459.8 2.5 reshape.377
  462.3 2.8 copy.248
  465.0 2.7 fusion.37
  472.8 2.2 convolution_convert_fusion.6
  475.1 2.1 convolution_convert_fusion.5
  482.9 3.4 fusion.33
  490.8 2.1 convolution_convert_fusion.7
  505.2 6.4 multiply_reduce_fusion.5
  511.7 5.1 convolution_convert_fusion.3
  516.8 5.8 convolution_convert_fusion.2
  522.6 5.7 convolution_convert_fusion.1
  536.5 4.6 all-to-all-start.1
  542.3 3.3 convolution_convert_fusion.4
  545.6 210.8 %shard_map.445 = (f32[16,32,1024]{2,1,0:T(8,128)}, f32[4,64,1024]{2,1,0:T(8,128)}) custom-call(bf16[3,4,2,2,2,32,1024]{6,5,4,3,2,1,0:T(8,128)(2,1)} %bitcast.309, bf16[1,4,2,2,2,32,1024]{6,5,4,3,2,1,0:T(8,128)(2,1)} %bitcast.319, bf16[1,4,2,2,2,32,1024]{6,5,4,3,2,1,0:T(8,128)(2,1)} %bitcast.320, bf16[2,4,2,2,2,32,1024]{6,5,4,3,2,1,0:T(8,128)(2,1)} %bitcast.317, ...), custom_call_target="tpu_custom_call" | custom-call | tf_op jit(solution)/shard_map/pallas_call | solution.py:332
  757.5 2.2 multiply_reduce_fusion.8
  767.4 12.9 %shard_map.446 = f32[4,32,2049]{2,1,0:T(8,128)S(1)} custom-call(s32[32,4,256]{2,1,0:T(4,128)S(1)} %reshape.317.ids_ref, bf16[32,32,256]{2,1,0:T(8,128)(2,1)S(1)} %all-to-all-done.1.rows_ref), custom_call_target="tpu_custom_call" | custom-call | tf_op jit(solution)/shard_map/pallas_call | solution.py:448
  783.9 39.6 %all-reduce.2 = (f32[]{:T(128)}, f32[]{:T(128)}) all-reduce(f32[]{:T(128)S(6)} %sub.197, f32[]{:T(128)S(6)} %add.356), channel_id=1, replica_groups=mesh['dp'=16,'vocab'=2] {'dp','vocab'}, use_global_device_ids=true, to_apply=%region_20.21 | all-reduce | flops 2 | bytes 16 | tf_op jit(solution)/shard_map/psum | solution.py:803
  828.7 2.1 multiply_subtract_fusion.4
  830.8 3.1 multiply_subtract_fusion.3
  834.0 2.2 multiply_subtract_fusion.1
  837.0 2.3 multiply_subtract_fusion
  840.4 2.2 multiply_subtract_fusion.2
  (427 shorter events, 97.9 us)
Async XLA Ops:
  7.2 342.8 %copy-start = (bf16[2,64,1024]{2,1,0:T(8,128)(2,1)S(1)}, bf16[2,64,1024]{2,1,0:T(8,128)(2,1)}, u32[]{:S(2)}) copy-start(bf16[2,64,1024]{2,1,0:T(8,128)(2,1)} %param.33) | copy-start | bytes 786436
  7.2 26.5 %copy-start.29 = (f32[4,2049,32]{1,2,0:T(8,128)S(1)}, f32[4,2049,32]{1,2,0:T(8,128)}, u32[]{:S(2)}) copy-start(f32[4,2049,32]{1,2,0:T(8,128)} %param.44) | copy-start | bytes 3147268
  33.8 19.6 %copy-start.81 = (s32[4,32]{1,0:T(4,128)S(1)}, s32[4,32]{1,0:T(4,128)}, u32[]{:S(2)}) copy-start(s32[4,32]{1,0:T(4,128)} %param.31) | copy-start | bytes 1540
  33.8 19.6 %copy-start.115 = (f32[4,32]{1,0:T(4,128)S(1)}, f32[4,32]{1,0:T(4,128)}, u32[]{:S(2)}) copy-start(f32[4,32]{1,0:T(4,128)} %param.50) | copy-start | bytes 1540
  33.8 19.7 %copy-start.113 = (f32[4,32]{1,0:T(4,128)S(1)}, f32[4,32]{1,0:T(4,128)}, u32[]{:S(2)}) copy-start(f32[4,32]{1,0:T(4,128)} %param.53) | copy-start | bytes 1540
  33.8 19.8 %copy-start.132 = (s32[4]{0:T(128)S(1)}, s32[4]{0:T(128)}, u32[]{:S(2)}) copy-start(s32[4]{0:T(128)} %param.30) | copy-start | bytes 52
  33.9 20.3 %copy-start.66 = (f32[2,32,1024]{2,1,0:T(8,128)S(1)}, f32[2,32,1024]{2,1,0:T(8,128)}, u32[]{:S(2)}) copy-start(f32[2,32,1024]{2,1,0:T(8,128)} %param.38) | copy-start | bytes 786436
  33.9 20.4 %copy-start.75 = (s32[4,4,32,64]{3,2,1,0:T(8,128)S(1)}, s32[4,4,32,64]{3,2,1,0:T(8,128)}, u32[]{:S(2)}) copy-start(s32[4,4,32,64]{3,2,1,0:T(8,128)} %param.32) | copy-start | bytes 393220
  49.8 308.2 %all-to-all-start = ((f32[32,32,256]{2,1,0:T(8,128)}), f32[32,32,256]{2,1,0:T(8,128)}, u32[]{:S(2)}, u32[]{:S(2)}) async-start(f32[32,32,256]{2,1,0:T(8,128)} %shard_map.444), calls=%async_computation | async-start | bytes 2097152 | tf_op jit(solution)/shard_map/all_to_all | solution.py:659
  53.4 389.8 %reduce-scatter.5.cloned.1.call-start = ((), (), s32[]{:S(2)}) async-start(), calls=%async_computation.4 | async-start | bytes 393216 | tf_op jit(solution)/shard_map/reduce_scatter | solution.py:728
  57.1 21.0 %copy-start.73 = (bf16[2,32,1024]{2,1,0:T(8,128)(2,1)S(1)}, bf16[2,32,1024]{2,1,0:T(8,128)(2,1)}, u32[]{:S(2)}) copy-start(bf16[2,32,1024]{2,1,0:T(8,128)(2,1)} %get-tuple-element.101) | copy-start | bytes 393220
  57.1 21.0 %copy-start.74 = (bf16[2,32,1024]{2,1,0:T(8,128)(2,1)S(1)}, bf16[2,32,1024]{2,1,0:T(8,128)(2,1)}, u32[]{:S(2)}) copy-start(bf16[2,32,1024]{2,1,0:T(8,128)(2,1)} %get-tuple-element.102) | copy-start | bytes 393220
  57.1 94.8 %copy-start.31 = (f32[4,64,1024]{2,1,0:T(8,128)S(1)}, f32[4,64,1024]{2,1,0:T(8,128)}, u32[]{:S(2)}) copy-start(f32[4,64,1024]{2,1,0:T(8,128)} %param.47) | copy-start | bytes 3145732
  396.4 9.1 %copy-start.18 = (f32[256,1024]{1,0:T(8,128)}, f32[256,1024]{1,0:T(8,128)S(1)}, u32[]{:S(2)}) copy-start(f32[256,1024]{1,0:T(8,128)S(1)} %get-tuple-element.130) | copy-start | bytes 3145732
  396.4 9.1 %copy-start.96 = (f32[256]{0:T(256)}, f32[256]{0:T(256)S(1)}, u32[]{:S(2)}) copy-start(f32[256]{0:T(256)S(1)} %broadcast_multiply_fusion.9) | copy-start | bytes 3076
  396.4 9.1 %slice-start.4 = ((s8[8388608]{0:T(1024)(128)(4,1)}), s8[4194304]{0:T(1024)(128)(4,1)S(1)}, s32[]{:S(2)}) async-start(s8[8388608]{0:T(1024)(128)(4,1)} %bitcast.379), calls=%async_computation.10 | async-start | bytes 8388608
  396.7 8.8 %copy-start.107 = (f32[256]{0:T(256)}, f32[256]{0:T(256)S(1)}, u32[]{:S(2)}) copy-start(f32[256]{0:T(256)S(1)} %add_rsqrt_fusion.1) | copy-start | bytes 3076
  396.7 8.8 %slice-start.5 = ((s8[8388608]{0:T(1024)(128)(4,1)}), s8[4194304]{0:T(1024)(128)(4,1)S(1)}, s32[]{:S(2)}) async-start(s8[8388608]{0:T(1024)(128)(4,1)} %bitcast.379), calls=%async_computation.11 | async-start | bytes 8388608
  405.5 10.3 %slice-start = ((s8[8388608]{0:T(1024)(128)(4,1)}), s8[4194304]{0:T(1024)(128)(4,1)S(1)}, s32[]{:S(2)}) async-start(s8[8388608]{0:T(1024)(128)(4,1)} %bitcast.313), calls=%async_computation.6 | async-start | bytes 8388608
  405.6 10.3 %slice-start.1 = ((s8[8388608]{0:T(1024)(128)(4,1)}), s8[4194304]{0:T(1024)(128)(4,1)S(1)}, s32[]{:S(2)}) async-start(s8[8388608]{0:T(1024)(128)(4,1)} %bitcast.313), calls=%async_computation.7 | async-start | bytes 8388608
  408.2 7.7 copy-start.21
  408.2 7.7 copy-start.94
  408.5 7.4 copy-start.105
  418.4 6.3 copy-start.125
  434.0 9.2 %copy-start.95 = (f32[256]{0:T(256)S(1)}, f32[256]{0:T(256)}, u32[]{:S(2)}) copy-start(f32[256]{0:T(256)} %copy-done.94) | copy-start | bytes 3076
  434.0 9.1 %copy-start.106 = (f32[256]{0:T(256)S(1)}, f32[256]{0:T(256)}, u32[]{:S(2)}) copy-start(f32[256]{0:T(256)} %copy-done.105) | copy-start | bytes 3076
  445.9 7.1 slice-start.2
  446.2 10.0 %copy-start.23 = (f32[256,1024]{1,0:T(8,128)}, f32[256,1024]{1,0:T(8,128)S(1)}, u32[]{:S(2)}) copy-start(f32[256,1024]{1,0:T(8,128)S(1)} %subtract_multiply_fusion) | copy-start | bytes 3145732
  446.3 6.7 copy-start.19
  446.3 6.7 copy-start.78
  446.3 6.7 copy-start.97
  446.3 6.7 copy-start.108
  446.3 6.7 slice-start.3
  505.2 6.4 copy-start.87
  505.2 6.4 copy-start.103
  533.7 7.4 copy-start.117
  533.7 7.4 copy-start.118
  533.8 7.4 copy-start.119
  533.8 7.4 copy-start.120
  533.8 7.4 copy-start.121
  533.8 7.4 copy-start.122
  533.8 7.4 copy-start.123
  533.8 7.4 copy-start.124
  535.4 6.9 copy-start.59
  535.4 6.9 copy-start.60
  536.5 231.0 %all-to-all-start.1 = ((bf16[32,32,256]{2,1,0:T(8,128)(2,1)}), bf16[32,32,256]{2,1,0:T(8,128)(2,1)S(1)}, u32[]{:S(2)}, u32[]{:S(2)}) async-start(bf16[32,32,256]{2,1,0:T(8,128)(2,1)} %bitcast.79), calls=%async_computation.2 | async-start | bytes 1048576 | tf_op jit(solution)/shard_map/all_to_all | solution.py:774
  541.1 224.1 %reduce-scatter.7.cloned.1.call-start = ((), (), s32[]{:S(2)}) async-start(), calls=%async_computation.5 | async-start | bytes 540672
  760.9 6.6 copy-start.37
  (96 other events, 285.4 us)
Sparse Core Ops, SparseCore 0:
  431.4 11.7 reduce-scatter.4
  544.8 139.6 reduce-scatter.6

commit v2 on v1

v2 whole, which is shorter than its diff:
```python
import functools
import math
from typing import Any, NamedTuple

import jax
import jax.numpy as jnp
from jax import lax
from jax.experimental import pallas as pl
from jax.experimental.pallas import tpu as pltpu
from jax.sharding import PartitionSpec as P

HEADS = 16
NORM_EPS = 1e-05
SCORE_SCALE = 0.125
NEG_FILL = -1e30
CLIP_LIMIT = 3.0
BETA_ONE = 0.9
BETA_TWO = 0.95
LEARN_RATE = 0.05
DECAY_RATE = 0.1
ADAM_EPS = 1e-08
BOTH = ("dp", "vocab")
MESH = pl.DeviceIdType.MESH
BF = jnp.bfloat16
F32 = jnp.float32
GROUPS = (3, 1, 1, 2, 1, 4, 4)
UNITS = tuple((group, index) for group, size in enumerate(GROUPS) for index in range(size))


def place():
    dp, x = lax.axis_index("dp"), lax.axis_index("vocab")
    return lax.div(dp, 4), lax.rem(lax.div(dp, 2), 2), lax.rem(dp, 2), x


def device(z, y, c, x):
    return ((z * 2 + y) * 2 + c, x)


def partners():
    z, y, c, x = place()
    line = [lax.rem(z + step, 4) for step in (1, 2, 3)]
    return (
        line,
        [device(other, y, c, x) for other in line],
        device(z, 1 - y, c, x),
        device(z, y, c, 1 - x),
        device(z, y, 1 - c, x),
    )


def greet(targets):
    barrier = pltpu.get_barrier_semaphore()
    for target in targets:
        pl.semaphore_signal(barrier, inc=1, device_id=target, device_id_type=MESH)
    pl.semaphore_wait(barrier, len(targets))


def transfer_order(heads):
    order, head = [], 0
    for unit in range(len(UNITS)):
        order.append(("b" if unit % 4 == 3 else "a", unit))
        if unit % 4 == 1 and head < heads:
            order.append(("h", head))
            head += 1
    return tuple(order)


def total_kernel(value_ref, out_ref, landed, send_sem, recv_sem):
    z, y, c, x = place()
    line, z_dev, y_dev, x_dev, c_dev = partners()
    greet(z_dev + [y_dev, x_dev, c_dev])

    def copy(src, dst, slot, target):
        return pltpu.make_async_remote_copy(
            src_ref=src,
            dst_ref=dst,
            send_sem=send_sem.at[slot],
            recv_sem=recv_sem.at[slot],
            device_id=target,
            device_id_type=MESH,
        )

    landed[z] = value_ref[...]
    parts = [copy(value_ref, landed.at[z], k, z_dev[k]) for k in range(3)]
    for part in parts:
        part.start()
    for part in parts:
        part.wait()
    landed[4] = landed[0] + landed[1] + landed[2] + landed[3]
    for step, target in enumerate((y_dev, x_dev, c_dev)):
        part = copy(landed.at[4 + 2 * step], landed.at[5 + 2 * step], 3 + step, target)
        part.start()
        part.wait()
        summed = landed[4 + 2 * step] + landed[5 + 2 * step]
        if step == 2:
            out_ref[...] = summed
        else:
            landed[6 + 2 * step] = summed


def total_over_all(value):
    return pl.pallas_call(
        total_kernel,
        out_shape=jax.ShapeDtypeStruct(value.shape, F32),
        in_specs=[pl.BlockSpec(memory_space=pltpu.VMEM)],
        out_specs=pl.BlockSpec(memory_space=pltpu.VMEM),
        scratch_shapes=[
            pltpu.VMEM((10,) + value.shape, F32),
            pltpu.SemaphoreType.DMA((6,)),
            pltpu.SemaphoreType.DMA((6,)),
        ],
        compiler_params=pltpu.CompilerParams(collective_id=4, has_side_effects=True),
    )(value)


def spread_kernel(ids_ref, rows_ref, out_ref, total):
    books, columns, rows = out_ref.shape
    width = rows_ref.shape[2]
    lanes = total.shape[2]
    high_count = total.shape[1] // columns
    step = pl.program_id(0)

    @pl.when(step == 0)
    def _():
        total[...] = jnp.zeros_like(total)

    values = rows_ref[0].astype(F32)
    spread = lax.broadcasted_iota(jnp.int32, (lanes, width), 0)
    for book in range(books):
        ids = ids_ref[0, book : book + 1, :]
        low = ids % lanes
        high_ids = ids // lanes
        hot = jnp.where(spread == low, 1.0, 0.0).astype(BF)
        parted = jnp.concatenate(
            [jnp.where(high_ids == high, values, 0.0) for high in range(high_count)], axis=0
        ).astype(BF)
        total[book] += lax.dot_general(
            parted, hot, (((1,), (1,)), ((), ())), preferred_element_type=F32
        )

    @pl.when(step == pl.num_programs(0) - 1)
    def _():
        for book in range(books):
            for high in range(high_count):
                first = high * lanes
                last = min(rows, first + lanes)
                out_ref[book, :, first:last] = total[
                    book, high * columns : (high + 1) * columns, : last - first
                ]


def spread_rows(ids, values, rows):
    blocks, books, width = ids.shape
    columns = values.shape[1]
    lanes = 256
    high_count = -(-rows // lanes)
    return pl.pallas_call(
        spread_kernel,
        grid=(blocks,),
        out_shape=jax.ShapeDtypeStruct((books, columns, rows), F32),
        in_specs=[
            pl.BlockSpec((1, books, width), lambda i: (i, 0, 0)),
            pl.BlockSpec((1, columns, width), lambda i: (i, 0, 0)),
        ],
        out_specs=pl.BlockSpec((books, columns, rows), lambda i: (0, 0, 0)),
        scratch_shapes=[pltpu.VMEM((books, high_count * columns, lanes), F32)],
        compiler_params=pltpu.CompilerParams(vmem_limit_bytes=40 * 2**20),
    )(ids, values)


PAIR, RES3, FFN, MIX2, CROSS, TEXT, MIX1, SELF = range(8)
LOGIT, ACT, UP = 0, 4, 8
RES2, QUERY2, KEY2, VALUE2, RES1, QUERY1, KEY1, VALUE1 = range(12, 20)
PLAN = (
    ("h", 0, PAIR, LOGIT + 0),
    ("a", 12, RES3, ACT + 0),
    ("a", 13, RES3, ACT + 1),
    ("h", 1, PAIR, LOGIT + 1),
    ("a", 8, FFN, UP + 0),
    ("a", 14, RES3, ACT + 2),
    ("b", 9, FFN, UP + 1),
    ("a", 15, RES3, ACT + 3),
    ("a", 10, FFN, UP + 2),
    ("h", 2, PAIR, LOGIT + 2),
    ("b", 11, FFN, UP + 3),
    ("a", 7, MIX2, RES2),
    ("a", 4, CROSS, QUERY2),
    ("b", 5, TEXT, KEY2),
    ("a", 6, TEXT, VALUE2),
    ("h", 3, PAIR, LOGIT + 3),
    ("a", 3, MIX1, RES1),
    ("a", 0, SELF, QUERY1),
    ("b", 1, SELF, KEY1),
    ("a", 2, SELF, VALUE1),
)
LATE = (2, 4, 6, 8)


def dot_nn(left, right):
    return jnp.dot(left, right, preferred_element_type=F32)


def dot_nt(left, right):
    return lax.dot_general(left, right, (((1,), (1,)), ((), ())), preferred_element_type=F32)


def dot_tn(left, right):
    return lax.dot_general(left, right, (((0,), (0,)), ((), ())), preferred_element_type=F32)


def chunk(index, size):
    return pl.ds(pl.multiple_of(index * size, size), size)


def norm_back_rows(values_ref, gain_ref, grad_ref, add_ref, out_ref, low_ref, gain_out, bias_out):
    size = 32
    one_gain = 1.0 + gain_ref[...]

    def block(index, carry):
        gain_sum, bias_sum = carry
        rows = chunk(index, size)
        values, cotangent = values_ref[rows, :], grad_ref[rows, :]
        average = jnp.mean(values, axis=-1, keepdims=True)
        centred = values - average
        scale = lax.rsqrt(jnp.mean(centred * centred, axis=-1, keepdims=True) + NORM_EPS)
        hat = centred * scale
        scaled = cotangent * one_gain
        mean_one = jnp.mean(scaled, axis=-1, keepdims=True)
        mean_two = jnp.mean(scaled * hat, axis=-1, keepdims=True)
        result = (scaled - mean_one - hat * mean_two) * scale
        if add_ref is not None:
            result = result + add_ref[rows, :]
        out_ref[rows, :] = result
        if low_ref is not None:
            low_ref[rows, :] = result.astype(BF)
        return (
            gain_sum + jnp.sum(cotangent * hat, axis=0, keepdims=True),
            bias_sum + jnp.sum(cotangent, axis=0, keepdims=True),
        )

    zero = jnp.zeros((1, values_ref.shape[1]), F32)
    gain_sum, bias_sum = lax.fori_loop(0, values_ref.shape[0] // size, block, (zero, zero))
    gain_out[...] = gain_sum
    bias_out[...] = bias_sum


def attend_back_rows(query, key, value, grad, query_out, key_out, value_out, clips, causal):
    rows, keys = query.shape[0] // clips, key.shape[0] // clips
    pairs = query.shape[1] // 128
    lane = lax.broadcasted_iota(jnp.int32, (1, 128), 1)
    halves = [(lane < 64).astype(F32).astype(BF), (lane >= 64).astype(F32).astype(BF)]

    def pair(index, carry):
        at_q = chunk(lax.div(index, pairs), rows)
        at_k = chunk(lax.div(index, pairs), keys)
        lanes = chunk(lax.rem(index, pairs), 128)
        q, k, v, g = query[at_q, lanes], key[at_k, lanes], value[at_k, lanes], grad[at_q, lanes]
        dq = jnp.zeros((rows, 128), F32)
        dk = jnp.zeros((keys, 128), F32)
        dv = jnp.zeros((keys, 128), F32)
        for half in halves:
            qh, kh, gh = q * half, k * half, g * half
            scores = dot_nt(qh, k) * SCORE_SCALE
            if causal:
                allowed = lax.broadcasted_iota(jnp.int32, (rows, keys), 0) >= lax.broadcasted_iota(
                    jnp.int32, (rows, keys), 1
                )
                scores = jnp.where(allowed, scores, NEG_FILL)
            exponents = jnp.exp(scores - jnp.max(scores, axis=-1, keepdims=True))
            probs = exponents / jnp.sum(exponents, axis=-1, keepdims=True)
            grad_probs = dot_nt(gh, v)
            dv = dv + dot_tn(probs.astype(BF), gh)
            inner = jnp.sum(probs * grad_probs, axis=-1, keepdims=True)
            grad_scores = (probs * (grad_probs - inner)).astype(BF)
            dq = dq + dot_nn(grad_scores, kh)
            dk = dk + dot_tn(grad_scores, qh)
        query_out[at_q, lanes] = (dq * SCORE_SCALE).astype(BF)
        key_out[at_k, lanes] = (dk * SCORE_SCALE).astype(BF)
        value_out[at_k, lanes] = dv.astype(BF)
        return carry

    lax.fori_loop(0, clips * pairs, pair, 0)


class BackwardRefs(NamedTuple):
    grad_logits: Any
    pair_rows: Any
    pick: Any
    x0: Any
    x1: Any
    x2: Any
    x3: Any
    h1: Any
    h2: Any
    h3: Any
    q1: Any
    k1: Any
    v1: Any
    o1: Any
    q2: Any
    k2: Any
    v2: Any
    o2: Any
    upper: Any
    act: Any
    text: Any
    gains: Any
    head: Any
    w0: Any
    w1: Any
    w2: Any
    w3: Any
    w4: Any
    w5: Any
    w6: Any
    layer_out: Any
    head_out: Any
    norm_out: Any
    start_out: Any
    core_in: Any
    first_in: Any
    second_in: Any
    line_in: Any
    head_y: Any
    head_line: Any
    core_slot: Any
    send_slot: Any
    held: Any
    acts: Any
    ups: Any
    logit: Any
    upper_slot: Any
    qkv: Any
    query2: Any
    kv2: Any
    left: Any
    left_pair: Any
    left_text: Any
    weight: Any
    lows: Any
    query2_grad: Any
    kv2_grad: Any
    grad_x: Any
    grad_h: Any
    values: Any
    rows_in: Any
    pair_in: Any
    pick_in: Any
    gain_in: Any
    pair_grad: Any
    pair_send: Any
    pair_land: Any
    send_sem: Any
    recv_sem: Any
    weight_sem: Any
    load_sem: Any
    core_sem: Any
    upper_sem: Any
    pair_sem: Any


def backward_kernel(clips, *refs):
    r = BackwardRefs(*refs)
    z, y, c, x = place()
    line, z_dev, y_dev, x_dev, c_dev = partners()
    items = PLAN
    count = len(items)
    frames_all = r.x0.shape[0]
    pieces = 4

    load_count = [0]

    def load(src, dst):
        piece = pltpu.make_async_copy(src, dst, r.load_sem.at[load_count[0]])
        load_count[0] += 1
        piece.start()
        return piece

    load_logit = load(r.grad_logits, r.logit)
    load_pair = load(r.pair_rows, r.pair_in)
    load_pick = load(r.pick, r.pick_in)
    load_gains = load(r.gains, r.gain_in)
    load_x3 = load(r.x3, r.values)
    load_act = load(r.act, r.acts)
    load_h3 = load(r.h3, r.rows_in.at[0])
    load_q1 = load(r.q1, r.qkv.at[0])
    load_k1 = load(r.k1, r.qkv.at[1])
    load_v1 = load(r.v1, r.qkv.at[2])
    load_q2 = load(r.q2, r.query2)
    load_k2 = load(r.k2, r.kv2.at[0])
    load_v2 = load(r.v2, r.kv2.at[1])

    sequence = [(r.head, k) for k in range(pieces)]
    sequence += [(ref, j) for j in range(pieces) for ref in (r.w6, r.w5)]
    sequence += [(r.w4, 0), (r.w2, 0), (r.w1, 0)] + [(r.w0, k) for k in range(3)]
    slots = r.weight.shape[0]
    taken = [0]

    def weight_copy(index):
        ref, at = sequence[index]
        return pltpu.make_async_copy(
            ref.at[at], r.weight.at[index % slots], r.weight_sem.at[index % slots]
        )

    for index in range(slots - 1):
        weight_copy(index).start()

    def next_weight():
        index = taken[0]
        taken[0] += 1
        if index + slots - 1 < len(sequence):
            weight_copy(index + slots - 1).start()
        weight_copy(index).wait()
        return r.weight.at[index % slots]

    def upper_copy(j):
        return pltpu.make_async_copy(
            r.upper.at[j], r.upper_slot.at[j % 2], r.upper_sem.at[j % 2]
        )

    upper_copy(0).start()
    upper_copy(1).start()
    greet(z_dev + [y_dev, x_dev, c_dev])

    left = (
        r.left_pair, r.left.at[0], r.left.at[1], r.left.at[2],
        r.left.at[3], r.left_text, r.left.at[0], r.left.at[1],
    )
    right = [r.logit.at[k] for k in range(pieces)]
    right += [r.acts.at[j] for j in range(pieces)] + [r.ups.at[j] for j in range(pieces)]
    right += [r.lows.at[1], r.query2_grad, r.kv2_grad.at[0], r.kv2_grad.at[1]]
    right += [r.acts.at[3], r.acts.at[0], r.acts.at[1], r.acts.at[2]]

    def copy(src, dst, item, slot, target):
        return pltpu.make_async_remote_copy(
            src_ref=src,
            dst_ref=dst,
            send_sem=r.send_sem.at[item, slot],
            recv_sem=r.recv_sem.at[item, slot],
            device_id=target,
            device_id_type=MESH,
        )

    held_slots = r.held.shape[0]

    def to_core(item):
        return copy(r.send_slot.at[item % 2], r.core_in.at[item], item, 0, c_dev)

    def core_load(item):
        return pltpu.make_async_copy(
            r.core_in.at[item], r.core_slot.at[item % 2], r.core_sem.at[item % 2]
        )

    def first(item):
        kind, unit = items[item][:2]
        held = r.held.at[item % held_slots]
        if kind == "a":
            return copy(held.at[:, :, 1 - x], r.first_in.at[unit], item, 1, x_dev)
        target = r.head_y if kind == "h" else r.first_in
        return copy(held.at[:, 1 - y], target.at[unit], item, 1, y_dev)

    def second(item):
        kind, unit = items[item][:2]
        if kind == "h":
            return None
        if kind == "a":
            return copy(r.first_in.at[unit, :, 1 - y], r.second_in.at[unit], item, 2, y_dev)
        return copy(r.first_in.at[unit, :, 1 - x], r.second_in.at[unit], item, 2, x_dev)

    def third(item):
        kind, unit = items[item][:2]
        ready, landed = (
            (r.head_y, r.head_line) if kind == "h" else (r.second_in, r.line_in)
        )
        return [
            copy(ready.at[unit, other], landed.at[unit, slot], item, 3 + slot, z_dev[slot])
            for slot, other in enumerate(line)
        ]

    def left_rows(name, core):
        ref = left[name]
        return jnp.concatenate(
            [ref[pl.ds(pl.multiple_of(k * 128 + core * 64, 64), 64), :] for k in range(8)], axis=0
        )

    def wide(value):
        return value.astype(F32)

    def make(item):
        kind, unit, left_name, right_name = items[item]
        if item >= 2:
            to_core(item - 2).wait_send()
        slot = r.send_slot.at[item % 2]

        def columns(n, carry):
            cols = chunk(n, 256)
            value = dot_nn(left_rows(left_name, 1 - c), right[right_name][:, cols]).astype(BF)
            slot[:, :, :, :, cols] = value.reshape(4, 2, 2, 32, 256)
            return carry

        lax.fori_loop(0, 4, columns, 0)
        to_core(item).start()

    def join_core(item):
        kind, unit, left_name, right_name = items[item]
        core_load(item).wait()
        if item >= held_slots:
            first(item - held_slots).wait_send()
        held, landed = r.held.at[item % held_slots], r.core_slot.at[item % 2]

        def columns(n, carry):
            cols = chunk(n, 256)
            value = dot_nn(left_rows(left_name, c), right[right_name][:, cols])
            value = value.reshape(4, 2, 2, 32, 256) + wide(landed[:, :, :, :, cols])
            held[:, :, :, :, cols] = value.astype(BF)
            return carry

        lax.fori_loop(0, 4, columns, 0)
        first(item).start()

    def join_first(item):
        kind, unit = items[item][:2]
        first(item).wait_recv()
        held = r.held.at[item % held_slots]
        target = r.head_y.at[unit] if kind == "h" else r.first_in.at[unit]

        def planes(k, carry):
            kept = held[k, :, x] if kind == "a" else held[k, y]
            target[k] = (wide(target[k]) + wide(kept)).astype(BF)
            return carry

        lax.fori_loop(0, 4, planes, 0)
        parts = third(item) if kind == "h" else [second(item)]
        for part in parts:
            part.start()

    def join_second(item):
        kind, unit = items[item][:2]
        if kind == "h":
            return
        second(item).wait_recv()

        def planes(k, carry):
            kept = r.first_in[unit, k, y if kind == "a" else x]
            r.second_in[unit, k] = (wide(r.second_in[unit, k]) + wide(kept)).astype(BF)
            return carry

        lax.fori_loop(0, 4, planes, 0)
        for part in third(item):
            part.start()

    def finish(item):
        kind, unit = items[item][:2]
        for part in third(item):
            part.wait_recv()
        if kind == "h":
            total = wide(r.head_y[unit, z])
            for slot in range(3):
                total = total + wide(r.head_line[unit, slot])
            r.head_out[unit] = total
        else:
            total = wide(r.second_in[unit, z])
            for slot in range(3):
                total = total + wide(r.line_in[unit, slot])
            r.layer_out[unit] = total

    ticks = [0]

    def pump():
        tick = ticks[0]
        ticks[0] += 1
        item = tick - 1
        if 0 <= item < count:
            to_core(item).wait_recv()
            core_load(item).start()
        for late, stage in zip(LATE, (join_core, join_first, join_second, finish)):
            item = tick - late
            if 0 <= item < count:
                stage(item)

    def unit(right_name):
        item = ticks[0]
        assert items[item][3] == right_name
        make(item)
        pump()

    load_logit.wait()
    load_pair.wait()
    r.left_pair[...] = r.pair_in[...].T
    unit(LOGIT + 0)

    def pair_rows_of(k, w):
        def columns(n, carry):
            cols = chunk(n, 256)
            value = dot_nt(r.logit[k], w[cols, :])
            r.pair_grad[:, cols] = value if k == 0 else r.pair_grad[:, cols] + value
            return carry

        lax.fori_loop(0, 4, columns, 0)

    for k in range(pieces):
        pair_rows_of(k, next_weight())
    half = r.pair_send.shape[0]
    r.pair_send[...] = r.pair_grad[chunk(1 - x, half), :].astype(BF)
    exchange = pltpu.make_async_remote_copy(
        src_ref=r.pair_send,
        dst_ref=r.pair_land,
        send_sem=r.pair_sem.at[0],
        recv_sem=r.pair_sem.at[1],
        device_id=x_dev,
        device_id_type=MESH,
    )
    exchange.start()
    load_h3.wait()
    r.left[1] = r.rows_in[0].T
    load_pick.wait()
    load_gains.wait()
    load_x3.wait()
    load_act.wait()
    exchange.wait()
    chosen = r.pair_grad[chunk(x, half), :].astype(BF).astype(F32) + wide(r.pair_land[...])
    chosen_top = chosen.astype(BF)
    chosen_rest = (chosen - wide(chosen_top)).astype(BF)
    r.grad_h[...] = dot_nn(r.pick_in[...], chosen_top) + dot_nn(r.pick_in[...], chosen_rest)

    def norm_back(index, add, low_ref):
        norm_back_rows(
            r.values,
            r.gain_in.at[index : index + 1],
            r.grad_h,
            add,
            r.grad_x,
            low_ref,
            r.norm_out.at[index : index + 1],
            r.norm_out.at[4 + index : 5 + index],
        )

    norm_back(3, None, r.lows.at[0])
    load_x2 = load(r.x2, r.values)
    r.left[0] = r.lows[0].T
    load_o2 = load(r.o2, r.rows_in.at[1])
    load_h2 = load(r.h2, r.rows_in.at[0])

    def down_back(j):
        w = next_weight()
        upper_copy(j).wait()

        def columns(n, carry):
            cols = chunk(n, 256)
            grad = dot_nn(r.lows[0], w[:, cols])
            upper = r.upper_slot[j % 2, :, cols]
            slope = 0.5 * (1.0 + lax.erf(upper * math.sqrt(0.5))) + upper * jnp.exp(
                -0.5 * upper * upper
            ) * (1.0 / math.sqrt(2.0 * math.pi))
            r.ups[j, :, cols] = (grad * slope).astype(BF)
            return carry

        lax.fori_loop(0, 4, columns, 0)
        if j + 2 < pieces:
            upper_copy(j + 2).start()

    def into_grad_h(value_ref, w, fresh):
        def columns(n, carry):
            cols = chunk(n, 256)
            value = dot_nt(value_ref[...], w[cols, :])
            r.grad_h[:, cols] = value if fresh else r.grad_h[:, cols] + value
            return carry

        lax.fori_loop(0, 4, columns, 0)

    def up_back(j):
        into_grad_h(r.ups.at[j], next_weight(), j == 0)

    unit(ACT + 0)
    down_back(0)
    unit(ACT + 1)
    up_back(0)
    unit(LOGIT + 1)
    unit(UP + 0)
    down_back(1)
    unit(ACT + 2)
    up_back(1)
    unit(UP + 1)
    down_back(2)
    unit(ACT + 3)
    up_back(2)
    unit(UP + 2)
    down_back(3)
    unit(LOGIT + 2)
    up_back(3)
    unit(UP + 3)
    load_x2.wait()
    norm_back(2, r.grad_x, r.lows.at[1])
    load_x1 = load(r.x1, r.values)

    load_o2.wait()
    r.left[2] = r.rows_in[1].T
    load_o1 = load(r.o1, r.rows_in.at[1])
    unit(RES2)
    for piece in (load_q2, load_k2, load_v2):
        piece.wait()

    def into_mixed(low_ref):
        w = next_weight()

        def columns(n, carry):
            cols = chunk(n, 256)
            r.lows[0, :, cols] = dot_nt(low_ref[...], w[cols, :]).astype(BF)
            return carry

        lax.fori_loop(0, 4, columns, 0)

    into_mixed(r.lows.at[1])
    attend_back_rows(
        r.query2, r.kv2.at[0], r.kv2.at[1], r.lows.at[0],
        r.query2_grad, r.kv2_grad.at[0], r.kv2_grad.at[1], clips, False,
    )
    load_h2.wait()
    r.left[3] = r.rows_in[0].T
    load_text = load(r.text, r.pair_in)
    unit(QUERY2)
    load_text.wait()
    r.left_text[...] = r.pair_in[...].T
    load_h1 = load(r.h1, r.rows_in.at[0])
    unit(KEY2)
    into_grad_h(r.query2_grad, next_weight(), True)
    unit(VALUE2)
    load_x1.wait()
    norm_back(1, r.grad_x, r.acts.at[3])
    load_x0 = load(r.x0, r.values)

    load_o1.wait()
    r.left[0] = r.rows_in[1].T
    unit(LOGIT + 3)
    unit(RES1)
    for piece in (load_q1, load_k1, load_v1):
        piece.wait()
    into_mixed(r.acts.at[3])
    attend_back_rows(
        r.qkv.at[0], r.qkv.at[1], r.qkv.at[2], r.lows.at[0],
        r.acts.at[0], r.acts.at[1], r.acts.at[2], clips, True,
    )
    load_h1.wait()
    r.left[1] = r.rows_in[0].T
    unit(QUERY1)
    into_grad_h(r.acts.at[0], next_weight(), True)
    unit(KEY1)
    into_grad_h(r.acts.at[1], next_weight(), False)
    unit(VALUE1)
    into_grad_h(r.acts.at[2], next_weight(), False)
    load_x0.wait()
    norm_back(0, r.grad_x, r.lows.at[1])
    r.start_out[...] = r.lows[1].T
    while ticks[0] < count + LATE[-1]:
        pump()
    for item in range(count):
        if item >= count - 2:
            to_core(item).wait_send()
        if item >= count - held_slots:
            first(item).wait_send()
        if items[item][0] != "h":
            second(item).wait_send()
        for part in third(item):
            part.wait_send()


def backward_fast(clips, operands):
    named = BackwardRefs(*operands, *(None,) * (len(BackwardRefs._fields) - len(operands)))
    rows, width = named.x0.shape
    pair_count = named.pair_rows.shape[0]
    text_rows = named.text.shape[0]
    books = named.head.shape[0]
    units, count = len(UNITS), len(PLAN)
    block = (32, width)
    vmem, dma = pltpu.VMEM, pltpu.SemaphoreType.DMA
    any_spec, vmem_spec = pl.BlockSpec(memory_space=pl.ANY), pl.BlockSpec(memory_space=vmem)
    held_slots = LATE[1] - LATE[0] + 1
    results = pl.pallas_call(
        functools.partial(backward_kernel, clips),
        out_shape=(
            jax.ShapeDtypeStruct((units,) + block, F32),
            jax.ShapeDtypeStruct((books, 2) + block, F32),
            jax.ShapeDtypeStruct((8, width), F32),
            jax.ShapeDtypeStruct((width, rows), BF),
            jax.ShapeDtypeStruct((count, 4, 2, 2) + block, BF),
        ),
        in_specs=[any_spec] * len(operands),
        out_specs=(vmem_spec,) * 4 + (any_spec,),
        scratch_shapes=[
            vmem((units, 4, 2) + block, BF),
            vmem((units, 4) + block, BF),
            vmem((units, 3) + block, BF),
            vmem((books, 4, 2) + block, BF),
            vmem((books, 3, 2) + block, BF),
            vmem((2, 4, 2, 2) + block, BF),
            vmem((2, 4, 2, 2) + block, BF),
            vmem((held_slots, 4, 2, 2) + block, BF),
            vmem((4, rows, width), BF),
            vmem((4, rows, width), BF),
            vmem((books, pair_count, width), BF),
            vmem((2, rows, width), F32),
            vmem((3, rows, width), BF),
            vmem((rows, width), BF),
            vmem((2, text_rows, width), BF),
            vmem((4, width, rows), BF),
            vmem((width, pair_count), BF),
            vmem((width, text_rows), BF),
            vmem((2, width, width), BF),
            vmem((2, rows, width), BF),
            vmem((rows, width), BF),
            vmem((2, text_rows, width), BF),
            vmem((rows, width), F32),
            vmem((rows, width), F32),
            vmem((rows, width), F32),
            vmem((2, rows, width), BF),
            vmem((pair_count, width), BF),
            vmem(named.pick.shape, BF),
            vmem(named.gains.shape, F32),
            vmem((pair_count, width), F32),
            vmem((pair_count // 2, width), BF),
            vmem((pair_count // 2, width), BF),
            dma((count, 6)),
            dma((count, 6)),
            dma((2,)),
            dma((24,)),
            dma((2,)),
            dma((2,)),
            dma((2,)),
        ],
        compiler_params=pltpu.CompilerParams(
            collective_id=2, has_side_effects=True, vmem_limit_bytes=60 * 2**20
        ),
    )(*operands)
    layer_shard, head_shard, norm_grads, start_grad = results[:4]
    return layer_shard, head_shard.reshape(books, -1, width), norm_grads, start_grad


class ForwardRefs(NamedTuple):
    ids: Any
    norms: Any
    table: Any
    layer: Any
    head_own: Any
    angles: Any
    text: Any
    pick: Any
    teach: Any
    row_info: Any
    ids_all: Any
    gains: Any
    loss: Any
    head: Any
    w0: Any
    w1: Any
    w2: Any
    w3: Any
    w4: Any
    w5: Any
    w6: Any
    grad_logits: Any
    pair_rows: Any
    x0: Any
    x1: Any
    x2: Any
    x3: Any
    h1: Any
    h2: Any
    h3: Any
    q1: Any
    k1: Any
    v1: Any
    o1: Any
    q2: Any
    k2: Any
    v2: Any
    o2: Any
    upper: Any
    act: Any
    norms_all: Any
    norm_rows: Any
    stacked: Any
    looked: Any
    landed: Any
    xs: Any
    hs: Any
    qkv: Any
    mixed: Any
    query2: Any
    kv2: Any
    uppers: Any
    acts: Any
    final: Any
    pair: Any
    wanted: Any
    logits: Any
    logit_grads: Any
    stats: Any
    weight: Any
    send_sem: Any
    recv_sem: Any
    local_sem: Any
    small_send: Any
    small_recv: Any
    look_send: Any
    look_recv: Any
    weight_sem: Any
    store_sem: Any
    pair_send: Any
    pair_recv: Any


GATHER_LATE = (2, 4, 6, 7)


def norm_rows_low(values_ref, gain_ref, bias_ref, low_ref):
    size = 32
    one_gain, bias = 1.0 + gain_ref[...], bias_ref[...]

    def block(index, carry):
        rows = chunk(index, size)
        values = values_ref[rows, :]
        average = jnp.mean(values, axis=-1, keepdims=True)
        centred = values - average
        spread = jnp.mean(centred * centred, axis=-1, keepdims=True)
        low_ref[rows, :] = (centred * lax.rsqrt(spread + NORM_EPS) * one_gain + bias).astype(BF)
        return carry

    lax.fori_loop(0, values_ref.shape[0] // size, block, 0)


def attend_rows(query, key, value, out, clips, causal):
    rows, keys = query.shape[0] // clips, key.shape[0] // clips
    pairs = query.shape[1] // 128
    lane = lax.broadcasted_iota(jnp.int32, (1, 128), 1)
    halves = [(lane < 64).astype(F32).astype(BF), (lane >= 64).astype(F32).astype(BF)]

    def pair(index, carry):
        at_q = chunk(lax.div(index, pairs), rows)
        at_k = chunk(lax.div(index, pairs), keys)
        lanes = chunk(lax.rem(index, pairs), 128)
        q, k, v = query[at_q, lanes], key[at_k, lanes], value[at_k, lanes]
        total = jnp.zeros((rows, 128), F32)
        for half in halves:
            scores = dot_nt(q * half, k) * SCORE_SCALE
            if causal:
                allowed = lax.broadcasted_iota(jnp.int32, (rows, keys), 0) >= lax.broadcasted_iota(
                    jnp.int32, (rows, keys), 1
                )
                scores = jnp.where(allowed, scores, NEG_FILL)
            exponents = jnp.exp(scores - jnp.max(scores, axis=-1, keepdims=True))
            probs = exponents / jnp.sum(exponents, axis=-1, keepdims=True)
            total = total + dot_nn(probs.astype(BF), v * half)
        out[at_q, lanes] = total.astype(BF)
        return carry

    lax.fori_loop(0, clips * pairs, pair, 0)


def forward_kernel(clips, denominator, special, *refs):
    r = ForwardRefs(*refs)
    z, y, c, x = place()
    me = lax.axis_index("dp") * 2 + x
    line, z_dev, y_dev, x_dev, c_dev = partners()
    books, frames = r.ids.shape[1], r.ids.shape[2]
    rows = clips * frames
    order = transfer_order(books)
    count = len(order)
    outs = (r.w0, r.w1, r.w2, r.w3, r.w4, r.w5, r.w6)
    columns, lanes = r.looked.shape[1], r.stacked.shape[2]
    high_count = r.stacked.shape[1] // columns
    devices = 32

    def device_of(index):
        return (lax.div(index, 2), lax.rem(index, 2))

    barrier = pltpu.get_barrier_semaphore()

    def signal(step, carry):
        pl.semaphore_signal(
            barrier, inc=1, device_id=device_of(lax.rem(me + step, devices)), device_id_type=MESH
        )
        return carry

    lax.fori_loop(1, devices, signal, 0)
    pl.semaphore_wait(barrier, devices - 1)

    def copy(src, dst, item, slot, target):
        return pltpu.make_async_remote_copy(
            src_ref=src,
            dst_ref=dst,
            send_sem=r.send_sem.at[item, slot],
            recv_sem=r.recv_sem.at[item, slot],
            device_id=target,
            device_id_type=MESH,
        )

    def whole(unit):
        group, index = UNITS[unit]
        return outs[group].at[index]

    own = [
        pltpu.make_async_copy(r.layer.at[unit], whole(unit).at[z, y, c, x], r.local_sem.at[unit])
        for unit in range(len(UNITS))
    ]
    own.append(
        pltpu.make_async_copy(r.head_own, r.head.at[:, z, y, c], r.local_sem.at[len(UNITS)])
    )

    def first(item):
        kind, unit = order[item]
        if kind == "h":
            src, dst = r.head_own.at[unit], r.head.at[unit, z, y, c]
        else:
            src, dst = r.layer.at[unit], whole(unit).at[z, y, c, x]
        return [copy(src, dst, item, slot, target) for slot, target in enumerate(z_dev)]

    def second(item):
        kind, unit = order[item]
        block = r.head.at[unit, :, y, c] if kind == "h" else whole(unit).at[:, y, c, x]
        parts = [
            copy(block, block, item, 3, x_dev if kind == "b" else y_dev),
            copy(block, block, item, 6, c_dev),
        ]
        if kind != "h":
            parts.append(copy(block, block, item, 4, y_dev if kind == "b" else x_dev))
        return parts

    def third(item):
        kind, unit = order[item]
        if kind == "h":
            block = r.head.at[unit, :, 1 - y, c]
        elif kind == "b":
            block = whole(unit).at[:, y, c, 1 - x]
        else:
            block = whole(unit).at[:, 1 - y, c, x]
        parts = [copy(block, block, item, 7, c_dev)]
        if kind != "h":
            parts.append(copy(block, block, item, 5, y_dev if kind == "b" else x_dev))
        return parts

    def fourth(item):
        kind, unit = order[item]
        if kind == "h":
            return []
        block = whole(unit).at[:, 1 - y, c] if kind == "b" else whole(unit).at[:, :, c, 1 - x]
        return [copy(block, block, item, 8, c_dev)]

    ticks = [0]

    def pump():
        tick = ticks[0]
        ticks[0] += 1
        if tick < count:
            for part in first(tick):
                part.start()
        item = tick - GATHER_LATE[0]
        if 0 <= item < count:
            for part in first(item):
                part.wait_recv()
            for part in second(item):
                part.start()
        item = tick - GATHER_LATE[1]
        if 0 <= item < count:
            second(item)[0].wait_recv()
            for part in third(item):
                part.start()
        item = tick - GATHER_LATE[2]
        if 0 <= item < count:
            for part in second(item)[2:] + third(item)[1:]:
                part.wait_recv()
            for part in fourth(item):
                part.start()
        item = tick - GATHER_LATE[3]
        if 0 <= item < count:
            for part in [second(item)[1], third(item)[0]] + fourth(item):
                part.wait_recv()
        advance_loads()

    item_of = {entry: item for item, entry in enumerate(order)}

    def ticks_for(kind, unit):
        return item_of[kind, unit] + GATHER_LATE[3] + 1

    def unit_kind(unit):
        return "b" if unit % 4 == 3 else "a"

    taken, loading = [0], [0]
    weight_slots = r.weight.shape[0]
    sequence = [(unit_kind(unit), unit) for unit in range(len(UNITS))]
    sequence += [("h", k) for k in range(books)]

    def weight_copy(index):
        kind, unit = sequence[index]
        slot = index % weight_slots
        if kind == "h":
            src, dst = r.head.at[unit], r.weight.at[slot].reshape(r.head.shape[1:])
        else:
            src, dst = whole(unit), r.weight.at[slot].reshape(whole(unit).shape)
        return pltpu.make_async_copy(src, dst, r.weight_sem.at[slot])

    def advance_loads():
        while (
            loading[0] < min(len(sequence), taken[0] + weight_slots)
            and ticks_for(*sequence[loading[0]]) <= ticks[0]
        ):
            weight_copy(loading[0]).start()
            loading[0] += 1

    def next_weight():
        index = taken[0]
        while loading[0] <= index:
            pump()
        weight_copy(index).wait()
        taken[0] += 1
        return r.weight.at[index % weight_slots]

    stores = []

    def store(src, dst):
        piece = pltpu.make_async_copy(src, dst, r.store_sem.at[len(stores)])
        piece.start()
        stores.append(piece)

    def small(block, slot, target):
        return pltpu.make_async_remote_copy(
            src_ref=block,
            dst_ref=block,
            send_sem=r.small_send.at[slot],
            recv_sem=r.small_recv.at[slot],
            device_id=target,
            device_id_type=MESH,
        )

    for piece in own:
        piece.start()
    r.ids_all[z, y, c] = r.ids[...]
    r.norms_all[z, y, c, x] = r.norms[...]
    small_stages = (
        [small(r.ids_all.at[z, y, c], k, z_dev[k]) for k in range(3)]
        + [small(r.norms_all.at[z, y, c, x], 3 + k, z_dev[k]) for k in range(3)],
        [small(r.ids_all.at[:, y, c], 6, y_dev), small(r.norms_all.at[:, y, c, x], 7, y_dev)],
        [small(r.ids_all.at[:, :, c], 8, c_dev), small(r.norms_all.at[:, :, c, x], 9, c_dev)],
        [small(r.norms_all.at[:, :, :, x], 10, x_dev)],
    )
    for number, stage in enumerate(small_stages):
        for part in stage:
            part.start()
        if number == 0:
            for piece in own:
                piece.wait()
            pump()
            pump()
            for book in range(books):
                for high in range(high_count):
                    r.stacked[book, high * columns : (high + 1) * columns, :] = r.table[
                        book, :, high * lanes : (high + 1) * lanes
                    ].astype(BF)
        for part in stage:
            part.wait()
        if number == 2:
            pump()
    for group in range(8):
        parts = [
            r.norms_all[group // 2, group % 2, j // 2, j % 2] for j in range(4)
        ]
        r.norm_rows[:, group * 128 : (group + 1) * 128] = parts[0] + parts[1] + parts[2] + parts[3]
    r.gains[...] = r.norm_rows[0:4, :]

    spread = lax.broadcasted_iota(jnp.int32, (lanes, rows), 0)

    def look_block(step, carry):
        target = lax.rem(me + step, devices)
        dp, member = lax.div(target, 2), lax.rem(target, 2)
        at = (lax.div(dp, 4), lax.rem(lax.div(dp, 2), 2), lax.rem(dp, 2))
        total = jnp.zeros((columns, rows), F32)
        for book in range(books):
            ids = jnp.concatenate(
                [r.ids_all[(*at, clips * member + m, pl.ds(book, 1))] for m in range(clips)], axis=1
            )
            low_ids, high_ids = ids & (lanes - 1), lax.shift_right_logical(ids, 8)
            hot = jnp.where(spread == low_ids, 1.0, 0.0).astype(BF)
            found = dot_nn(r.stacked[book], hot)
            for high in range(high_count):
                total = total + jnp.where(
                    high_ids == high, found[high * columns : (high + 1) * columns], 0.0
                )
        r.looked[step] = total
        return carry

    def look_copy(step):
        return pltpu.make_async_remote_copy(
            src_ref=r.looked.at[step],
            dst_ref=r.landed.at[me],
            send_sem=r.look_send.at[step],
            recv_sem=r.look_recv.at[step],
            device_id=device_of(lax.rem(me + step, devices)),
            device_id_type=MESH,
        )

    def look_and_send(step, carry):
        look_block(step, carry)
        look_copy(step).start()
        return carry

    for part in range(4):
        lax.fori_loop(1 + 8 * part, min(9 + 8 * part, devices), look_and_send, 0)
        pump()
    look_block(0, 0)
    r.landed[me] = r.looked[0]

    code = lax.broadcasted_iota(jnp.int32, (128, r.teach.shape[2]), 0)
    teach_count = r.teach.shape[1] - 8

    def want(book):
        def block(index, carry):
            here = code + index * 128
            total = jnp.zeros(here.shape, F32)
            for i in range(teach_count):
                total = total + jnp.where(here == r.teach[book, i : i + 1, :], 1.0, 0.0)
            hit = jnp.where(here == r.teach[book, teach_count : teach_count + 1, :], 1.0, 0.0)
            r.wanted[book, :, chunk(index, 128)] = (total * (1.0 / teach_count) + hit).T
            return carry

        lax.fori_loop(0, r.wanted.shape[2] // 128, block, 0)

    for book in range(books):
        want(book)
        pump()

    def look_wait(step, carry):
        look_copy(step).wait_recv()
        return carry

    lax.fori_loop(1, devices, look_wait, 0)

    def place_rows(index, carry):
        cols = chunk(index, 128)
        block = jnp.concatenate([r.landed[index * 4 + j] for j in range(4)], axis=0).T
        angles = r.angles[:, cols]
        r.xs[0, :, cols] = block + jnp.concatenate([angles] * clips, axis=0)
        return carry

    lax.fori_loop(0, r.xs.shape[2] // 128, place_rows, 0)

    def norm(index, low_ref):
        norm_rows_low(
            r.xs.at[index],
            r.norm_rows.at[index : index + 1],
            r.norm_rows.at[4 + index : 5 + index],
            low_ref,
        )

    def product(left_ref, w, out_ref):
        def part(n, carry):
            cols = chunk(n, 256)
            out_ref[:, cols] = dot_nn(left_ref[...], w[:, cols]).astype(BF)
            return carry

        lax.fori_loop(0, 4, part, 0)

    def residual(left_ref, w, before, after):
        def part(n, carry):
            cols = chunk(n, 256)
            r.xs[after, :, cols] = r.xs[before, :, cols] + dot_nn(left_ref[...], w[:, cols])
            return carry

        lax.fori_loop(0, 4, part, 0)

    store(r.xs.at[0], r.x0)
    norm(0, r.hs.at[0])
    store(r.hs.at[0], r.h1)
    for k in range(3):
        product(r.hs.at[0], next_weight(), r.qkv.at[k])
        store(r.qkv.at[k], (r.q1, r.k1, r.v1)[k])
    pump()
    attend_rows(r.qkv.at[0], r.qkv.at[1], r.qkv.at[2], r.mixed.at[0], clips, True)
    store(r.mixed.at[0], r.o1)
    residual(r.mixed.at[0], next_weight(), 0, 1)
    store(r.xs.at[1], r.x1)
    norm(1, r.hs.at[1])
    store(r.hs.at[1], r.h2)
    product(r.hs.at[1], next_weight(), r.query2)
    store(r.query2, r.q2)
    for k in range(2):
        product(r.text, next_weight(), r.kv2.at[k])
        store(r.kv2.at[k], (r.k2, r.v2)[k])
    pump()
    attend_rows(r.query2, r.kv2.at[0], r.kv2.at[1], r.mixed.at[1], clips, False)
    store(r.mixed.at[1], r.o2)
    residual(r.mixed.at[1], next_weight(), 1, 2)
    store(r.xs.at[2], r.x2)
    norm(2, r.hs.at[2])
    store(r.hs.at[2], r.h3)
    pieces = r.uppers.shape[0]
    for j in range(pieces):
        w = next_weight()

        def part(n, carry):
            cols = chunk(n, 256)
            upper = dot_nn(r.hs[2], w[:, cols])
            r.uppers[j, :, cols] = upper
            r.acts[j, :, cols] = (upper * (0.5 * (1.0 + lax.erf(upper * math.sqrt(0.5))))).astype(BF)
            return carry

        lax.fori_loop(0, 4, part, 0)
        store(r.uppers.at[j], r.upper.at[j])
        store(r.acts.at[j], r.act.at[j])
    for j in range(pieces):
        w = next_weight()

        def part(n, carry):
            cols = chunk(n, 256)
            before = r.xs[2, :, cols] if j == 0 else r.xs[3, :, cols]
            r.xs[3, :, cols] = before + dot_nt(r.acts[j], w[cols, :])
            return carry

        lax.fori_loop(0, 4, part, 0)
    store(r.xs.at[3], r.x3)
    norm(3, r.final)
    half = r.pair.shape[1]
    r.pair[x] = dot_nn(r.pick[...], r.final[...]).astype(BF)

    def exchange(ref, slot):
        return pltpu.make_async_remote_copy(
            src_ref=ref.at[x],
            dst_ref=ref.at[x],
            send_sem=r.pair_send.at[slot],
            recv_sem=r.pair_recv.at[slot],
            device_id=x_dev,
            device_id_type=MESH,
        )

    trade = exchange(r.pair, 0)
    trade.start()
    trade.wait()
    pair_count = 2 * half
    stat_lane = lax.broadcasted_iota(jnp.int32, (pair_count, 128), 1)
    stats = jnp.zeros((pair_count, 128), F32)
    for k in range(books):
        w = next_weight()

        def part(n, carry):
            cols = chunk(n, 256)
            pair = jnp.concatenate([r.pair[0], r.pair[1]], axis=0)
            r.logits[k, :, cols] = dot_nn(pair, w[:, cols])
            return carry

        lax.fori_loop(0, 4, part, 0)
        highest = jnp.max(r.logits[k], axis=-1, keepdims=True)
        exp_sum = jnp.sum(jnp.exp(r.logits[k] - highest), axis=-1, keepdims=True)
        stats = jnp.where(stat_lane == k, highest, stats)
        stats = jnp.where(stat_lane == books + k, exp_sum, stats)
    r.stats[x] = stats
    trade = exchange(r.stats, 1)
    trade.start()
    store(r.pair.at[0], r.pair_rows.at[0])
    store(r.pair.at[1], r.pair_rows.at[1])
    trade.wait()
    weight_col = r.row_info[:, books : books + 1]
    owned = r.row_info[:, books + 1 : books + 2]
    loss_col = jnp.zeros((pair_count, 1), F32)
    for k in range(books):
        valid = r.row_info[:, k : k + 1]
        tops = [r.stats[m][:, k : k + 1] for m in range(2)]
        sums = [r.stats[m][:, books + k : books + k + 1] for m in range(2)]
        top = jnp.maximum(tops[0], tops[1])
        log_total = top + jnp.log(sums[0] * jnp.exp(tops[0] - top) + sums[1] * jnp.exp(tops[1] - top))
        loss_col = loss_col + owned * weight_col * (valid + 1.0) * log_total
        scaled = weight_col * (1.0 / denominator)

        def part(n, total):
            cols = chunk(n, 256)
            logits, wanted = r.logits[k, :, cols], r.wanted[k, :, cols]
            r.logit_grads[k, :, cols] = (
                scaled * ((valid + 1.0) * jnp.exp(logits - log_total) - wanted)
            ).astype(BF)
            return total + jnp.sum(wanted * logits, axis=-1, keepdims=True)

        picked = lax.fori_loop(0, 4, part, jnp.zeros((pair_count, 1), F32))
        loss_col = loss_col - weight_col * picked
        store(r.logit_grads.at[k], r.grad_logits.at[k])
    r.loss[...] = jnp.broadcast_to(jnp.sum(loss_col, axis=0, keepdims=True), r.loss.shape)

    def look_done(step, carry):
        look_copy(step).wait_send()
        return carry

    lax.fori_loop(1, devices, look_done, 0)
    for item in range(count):
        for part in first(item) + second(item) + third(item) + fourth(item):
            part.wait_send()
    for piece in stores:
        piece.wait()


def forward_fast(clips, denominator, special, operands):
    named = ForwardRefs(*operands, *(None,) * (len(ForwardRefs._fields) - len(operands)))
    books, frames = named.ids.shape[1:]
    rows, width = clips * frames, named.layer.shape[2]
    text_rows, pair_count = named.text.shape[0], named.teach.shape[2]
    codes, columns = named.head_own.shape[2], named.table.shape[1]
    lanes = 256
    high_count = named.table.shape[2] // lanes
    count = books + len(UNITS)
    pieces = GROUPS[-1]
    vmem, dma = pltpu.VMEM, pltpu.SemaphoreType.DMA
    any_spec, vmem_spec = pl.BlockSpec(memory_space=pl.ANY), pl.BlockSpec(memory_space=vmem)

    def shaped(shape, dtype=BF):
        return jax.ShapeDtypeStruct(shape, dtype)

    in_vmem = (
        shaped((4, 2, 2) + named.ids.shape, jnp.int32),
        shaped((4, width), F32),
        shaped((8, 128), F32),
    )
    in_hbm = (
        (shaped((books, 4, 2, 2) + named.head_own.shape[1:]),)
        + tuple(shaped((size, 4, 2, 2, 2) + named.layer.shape[1:]) for size in GROUPS)
        + (shaped((books, pair_count, codes)), shaped((2, pair_count // 2, width)))
        + (shaped((rows, width), F32),) * 4
        + (shaped((rows, width)),) * 8
        + (shaped((text_rows, width)),) * 2
        + (shaped((rows, width)), shaped((pieces, rows, width), F32), shaped((pieces, rows, width)))
    )
    results = pl.pallas_call(
        functools.partial(forward_kernel, clips, denominator, special),
        out_shape=in_vmem + in_hbm,
        in_specs=[vmem_spec] * len(operands),
        out_specs=(vmem_spec,) * len(in_vmem) + (any_spec,) * len(in_hbm),
        scratch_shapes=[
            vmem((4, 2, 2, 2, 8, 128), F32),
            vmem((8, width), F32),
            vmem((books, high_count * columns, lanes), BF),
            vmem((32, columns, rows), F32),
            vmem((32, columns, rows), F32),
            vmem((4, rows, width), F32),
            vmem((3, rows, width), BF),
            vmem((3, rows, width), BF),
            vmem((2, rows, width), BF),
            vmem((rows, width), BF),
            vmem((2, text_rows, width), BF),
            vmem((pieces, rows, width), F32),
            vmem((pieces, rows, width), BF),
            vmem((rows, width), BF),
            vmem((2, pair_count // 2, width), BF),
            vmem((books, pair_count, codes), F32),
            vmem((books, pair_count, codes), F32),
            vmem((books, pair_count, codes), BF),
            vmem((2, pair_count, 128), F32),
            vmem((3, width, width), BF),
            dma((count, 9)),
            dma((count, 9)),
            dma((len(UNITS) + 1,)),
            dma((11,)),
            dma((11,)),
            dma((32,)),
            dma((32,)),
            dma((3,)),
            dma((40,)),
            dma((2,)),
            dma((2,)),
        ],
        compiler_params=pltpu.CompilerParams(
            collective_id=1, has_side_effects=True, vmem_limit_bytes=58 * 2**20
        ),
    )(*operands)
    return ForwardRefs(
        *operands,
        *results,
        *(None,) * (len(ForwardRefs._fields) - len(operands) - len(results)),
    )


def low(values):
    return values.astype(BF)


def ein(formula, left, right):
    return jnp.einsum(formula, left, right, preferred_element_type=F32)


def norm_stats(values):
    average = jnp.mean(values, axis=-1, keepdims=True)
    centred = values - average
    spread = jnp.mean(centred * centred, axis=-1, keepdims=True)
    scale = lax.rsqrt(spread + NORM_EPS)
    return centred * scale, scale


def norm_forward(values, gain, bias):
    hat, scale = norm_stats(values)
    return hat * (1.0 + gain) + bias


def norm_backward(values, gain, cotangent):
    hat, scale = norm_stats(values)
    scaled = cotangent * (1.0 + gain)
    mean_one = jnp.mean(scaled, axis=-1, keepdims=True)
    mean_two = jnp.mean(scaled * hat, axis=-1, keepdims=True)
    return (
        (scaled - mean_one - hat * mean_two) * scale,
        jnp.sum(cotangent * hat, axis=0),
        jnp.sum(cotangent, axis=0),
    )


def sinusoid(frames, model_width):
    half_width = model_width // 2
    freq_rates = jnp.exp(
        jnp.arange(half_width, dtype=F32) * (-math.log(10000.0) / (half_width - 1))
    )
    angles = jnp.arange(frames, dtype=F32)[:, None] * freq_rates[None, :]
    return jnp.concatenate([jnp.sin(angles), jnp.cos(angles)], axis=1)


def delay_ids(codes, offsets, special):
    frames = codes.shape[2]
    frame = jnp.arange(frames, dtype=jnp.int32)[None, None, :]
    inputs = jnp.full_like(codes, special)
    targets = jnp.full_like(codes, special)
    padded = jnp.pad(codes, ((0, 0), (0, 0), (4, 0)), constant_values=special)
    for shift in range(4):
        is_shift = (offsets == shift)[:, :, None]
        targets = jnp.where(is_shift, padded[:, :, 4 - shift : 4 - shift + frames], targets)
        inputs = jnp.where(is_shift, padded[:, :, 3 - shift : 3 - shift + frames], inputs)
    return inputs, targets


def split_heads(matrix, clips):
    return matrix.reshape(clips, matrix.shape[0] // clips, HEADS, -1)


def raw_scores(queries, keyset, causal):
    scores = ein("bqhe,bkhe->bhqk", queries, keyset) * SCORE_SCALE
    if causal:
        length = scores.shape[2]
        allowed = jnp.arange(length)[:, None] >= jnp.arange(length)[None, :]
        scores = jnp.where(allowed[None, None], scores, NEG_FILL)
    return scores


def attend_forward(queries, keyset, valset, clips, causal):
    queries, keyset, valset = (split_heads(m, clips) for m in (queries, keyset, valset))
    scores = raw_scores(queries, keyset, causal)
    highest = jnp.max(scores, axis=-1, keepdims=True)
    exponents = jnp.exp(scores - highest)
    denominator = jnp.sum(exponents, axis=-1, keepdims=True)
    probs = exponents / denominator
    mixed = ein("bhqk,bkhe->bqhe", low(probs), valset)
    return low(mixed).reshape(mixed.shape[0] * mixed.shape[1], -1), probs


def attend_backward(queries, keyset, valset, probs, grad_mixed, clips):
    queries, keyset, valset, grad_mixed = (
        split_heads(m, clips) for m in (queries, keyset, valset, grad_mixed)
    )
    grad_probs = ein("bqhe,bkhe->bhqk", grad_mixed, valset)
    grad_values = low(ein("bhqk,bqhe->bkhe", low(probs), grad_mixed))
    grad_scores = low(
        probs * (grad_probs - jnp.sum(probs * grad_probs, axis=-1, keepdims=True))
    )
    grad_queries = low(ein("bhqk,bkhe->bqhe", grad_scores, keyset) * SCORE_SCALE)
    grad_keys = low(ein("bhqk,bqhe->bkhe", grad_scores, queries) * SCORE_SCALE)
    return tuple(
        m.reshape(m.shape[0] * m.shape[1], -1) for m in (grad_queries, grad_keys, grad_values)
    )


def normal_cdf(values):
    return 0.5 * (1.0 + lax.erf(values * math.sqrt(0.5)))


def adam_step(weight, first_moment, second_moment, gradient, factor, corr_one, corr_two):
    clipped = gradient * factor
    first_next = BETA_ONE * first_moment + (1.0 - BETA_ONE) * clipped
    second_next = BETA_TWO * second_moment + (1.0 - BETA_TWO) * clipped * clipped
    update = (
        first_next / corr_one / (jnp.sqrt(second_next / corr_two) + ADAM_EPS) + DECAY_RATE * weight
    )
    return (weight - LEARN_RATE * update, first_next, second_next)


def columns_apart(matrix, pieces):
    count, rows, width = matrix.shape
    parts = matrix.reshape(count, rows, pieces, width // pieces).transpose(0, 2, 1, 3)
    return parts.reshape(count * pieces, rows, width // pieces)


def columns_together(parts, pieces):
    total, rows, width = parts.shape
    matrix = parts.reshape(total // pieces, pieces, rows, width).transpose(0, 2, 1, 3)
    return matrix.reshape(total // pieces, rows, pieces * width)


def local(
    fast,
    audio_codes,
    delay_offsets,
    clip_lengths,
    loss_positions,
    teacher_ids,
    text_states,
    step_count,
    in_proj,
    in_proj_mean,
    in_proj_sq,
    out_proj,
    out_proj_mean,
    out_proj_sq,
    ffn_proj,
    ffn_proj_mean,
    ffn_proj_sq,
    embed_table,
    embed_table_mean,
    embed_table_sq,
    head_table,
    head_table_mean,
    head_table_sq,
    norm_gain,
    norm_gain_mean,
    norm_gain_sq,
    norm_bias,
    norm_bias_mean,
    norm_bias_sq,
):
    clips = text_states.shape[0]
    vocab_count = lax.axis_size("vocab")
    device_count = lax.axis_size("dp") * vocab_count
    vocab_index = lax.axis_index("vocab")
    book_count = head_table.shape[0]
    pos_count = loss_positions.shape[1]
    frames = audio_codes.shape[2]
    table_rows = embed_table.shape[1]
    special = table_rows - 1
    half_vocab = head_table.shape[2]
    vocab_base = vocab_index * half_vocab
    model_width = text_states.shape[2]
    rows = clips * frames
    ffn_pieces = ffn_proj.shape[2] // model_width
    denominator = float(clips * device_count * pos_count * book_count)

    inputs, targets = delay_ids(audio_codes, delay_offsets, special)
    own_first = vocab_index * clips
    own_inputs = lax.dynamic_slice_in_dim(inputs, own_first, clips, 0)
    own_positions = lax.dynamic_slice_in_dim(loss_positions, own_first, clips, 0)

    layer_local = jnp.concatenate(
        [
            low(in_proj[0:3]),
            low(out_proj[0:1]),
            low(in_proj[3:6]),
            low(out_proj[1:2]),
            columns_apart(low(ffn_proj), ffn_pieces),
        ],
        axis=0,
    )
    head_local = low(head_table)
    norms_local = low(jnp.concatenate([norm_gain, norm_bias], axis=0))
    target_at = jnp.take_along_axis(targets, loss_positions[:, None, :], axis=2)
    pair_count = target_at.shape[0] * pos_count
    target_at = target_at.transpose(1, 0, 2).reshape(book_count, pair_count)
    valid = (target_at != special).astype(F32)
    row_weight = (loss_positions < clip_lengths[:, None]).astype(F32).reshape(pair_count)
    flat_positions = (own_positions + jnp.arange(clips, dtype=jnp.int32)[:, None] * frames).reshape(-1)
    pick = flat_positions[:, None] == jnp.arange(rows, dtype=jnp.int32)[None, :]
    text = text_states.reshape(-1, model_width)
    angles = sinusoid(frames, model_width)
    if fast:
        device_index = lax.axis_index("dp") * vocab_count + vocab_index
        norm_width = norm_gain.shape[1]
        norms_placed = lax.dynamic_update_slice(
            jnp.zeros((8, 128), F32),
            norms_local.astype(F32),
            (0, lax.rem(device_index, 128 // norm_width) * norm_width),
        )
        table_t = jnp.swapaxes(embed_table, 1, 2)
        table_t = jnp.pad(table_t, ((0, 0), (0, 0), (0, -table_rows % 256)))
        teach = jnp.concatenate(
            [
                teacher_ids.transpose(1, 3, 0, 2).reshape(book_count, -1, pair_count) - vocab_base,
                jnp.where(target_at == special, -1, target_at - vocab_base)[:, None, :],
                jnp.full((book_count, 7, pair_count), -1, jnp.int32),
            ],
            axis=1,
        )
        owned = (jnp.arange(pair_count) // (clips * pos_count) == vocab_index).astype(F32)
        row_info = jnp.concatenate([valid, row_weight[None], owned[None]], axis=0).T
        row_info = jnp.pad(row_info, ((0, 0), (0, 128 - row_info.shape[1])))
        kept = forward_fast(
            clips,
            denominator,
            special,
            (
                inputs,
                norms_placed,
                table_t,
                layer_local,
                head_local,
                angles,
                text,
                pick.astype(BF),
                teach,
                row_info,
            ),
        )
        block_ids = (
            kept.ids_all.reshape(device_count, clips, book_count, frames)
            .transpose(0, 2, 1, 3)
            .reshape(device_count, book_count, rows)
        )
        loss_sum = kept.loss[0, 0]

        def joined(part):
            return part.reshape(part.shape[0], -1, part.shape[-1])

        layer_shard, head_shard, norm_grads, start_grad = backward_fast(
            clips,
            (
                kept.grad_logits,
                kept.pair_rows.reshape(pair_count, model_width),
                pick.T.astype(BF),
                kept.x0,
                kept.x1,
                kept.x2,
                kept.x3,
                kept.h1,
                kept.h2,
                kept.h3,
                kept.q1,
                kept.k1,
                kept.v1,
                kept.o1,
                kept.q2,
                kept.k2,
                kept.v2,
                kept.o2,
                kept.upper,
                kept.act,
                text,
                kept.gains,
                joined(kept.head),
                joined(kept.w0),
                joined(kept.w1),
                joined(kept.w2),
                joined(kept.w3),
                joined(kept.w4),
                joined(kept.w5),
                joined(kept.w6),
            ),
        )
        parted = start_grad.reshape(device_count, -1, rows)
        parted = lax.all_to_all(parted, BOTH, 0, 0, tiled=True)
        embed_shard = jnp.swapaxes(spread_rows(block_ids, parted, table_rows), 1, 2)
    else:
        norms = lax.all_gather(norms_local, BOTH, axis=1, tiled=True).astype(F32)
        table = lax.all_gather(low(embed_table), BOTH, axis=2, tiled=True)
        embedded = jnp.zeros((rows, model_width), F32)
        for book in range(book_count):
            embedded = embedded + jnp.take(
                table[book], own_inputs[:, book].reshape(-1), axis=0
            ).astype(F32)
        layer_all = lax.all_gather(layer_local, BOTH, axis=1, tiled=True)
        starts = [sum(GROUPS[:g]) for g in range(len(GROUPS))]
        layer_parts = [layer_all[s : s + g] for s, g in zip(starts, GROUPS)]
        head_all = lax.all_gather(head_local, "dp", axis=1, tiled=True)
        w_self, w_self_out, w_query, w_text, w_cross_out, w_up, w_down = layer_parts
        gains, biases = norms[:4], norms[4:]

        start = embedded + jnp.tile(angles, (clips, 1))
        normed_self = low(norm_forward(start, gains[0], biases[0]))
        proj = low(ein("rd,kde->kre", normed_self, w_self))
        self_out, self_probs = attend_forward(proj[0], proj[1], proj[2], clips, True)
        after_self = start + ein("rd,de->re", self_out, w_self_out[0])
        normed_cross = low(norm_forward(after_self, gains[1], biases[1]))
        cross_query = low(ein("rd,de->re", normed_cross, w_query[0]))
        cross_text = low(ein("td,kde->kte", text, w_text))
        cross_out, cross_probs = attend_forward(cross_query, cross_text[0], cross_text[1], clips, False)
        after_cross = after_self + ein("rd,de->re", cross_out, w_cross_out[0])
        normed_ffn = low(norm_forward(after_cross, gains[2], biases[2]))
        upper = ein("rd,jdf->jrf", normed_ffn, w_up)
        cdf = normal_cdf(upper)
        active = low(upper * cdf)
        after_ffn = after_cross + ein("jrf,jdf->rd", active, w_down)
        final_norm = low(norm_forward(after_ffn, gains[3], biases[3]))
        chosen = low(ein("pr,rd->pd", pick.astype(BF), final_norm))

        pair_rows = lax.all_gather(chosen, "vocab", axis=0, tiled=True)
        teach = teacher_ids.transpose(1, 0, 2, 3).reshape(book_count, pair_count, -1)
        local_ids = vocab_base + jnp.arange(half_vocab, dtype=jnp.int32)
        counts = jnp.sum(
            (teach[:, :, :, None] == local_ids[None, None, None, :]).astype(F32), axis=2
        )
        wanted = counts / teach.shape[2] + valid[:, :, None] * (
            target_at[:, :, None] == local_ids[None, None, :]
        ).astype(F32)
        logits = ein("rd,kdv->krv", pair_rows, head_all)
        highest = jnp.max(logits, axis=-1)
        exp_sum = jnp.sum(jnp.exp(logits - highest[:, :, None]), axis=-1)
        stats = lax.all_gather(jnp.stack([highest, exp_sum]), "vocab")
        top_all = jnp.max(stats[:, 0], axis=0)
        sum_all = jnp.sum(stats[:, 1] * jnp.exp(stats[:, 0] - top_all[None]), axis=0)
        log_total = top_all + jnp.log(sum_all)
        row_loss = row_weight[None, :] * (valid + 1.0) * log_total
        own_rows = clips * pos_count
        loss_sum = jnp.sum(
            lax.dynamic_slice_in_dim(row_loss, vocab_index * own_rows, own_rows, 1)
        ) - jnp.sum(row_weight[None, :] * jnp.sum(wanted * logits, axis=-1))
        scaled = (row_weight / denominator)[None, :, None]
        grad_logits = low(
            scaled * ((valid + 1.0)[:, :, None] * jnp.exp(logits - log_total[:, :, None]) - wanted)
        )
        grad_head = ein("rd,krv->kdv", pair_rows, grad_logits)
        grad_rows = ein("krv,kdv->rd", grad_logits, head_all)
        grad_chosen = lax.psum_scatter(low(grad_rows), "vocab", scatter_dimension=0, tiled=True).astype(F32)

        grad_final = jnp.einsum(
            "pr,pd->rd", pick.astype(F32), grad_chosen, precision=lax.Precision.HIGHEST
        )
        grad_ffn_res, gain_three, bias_three = norm_backward(after_ffn, gains[3], grad_final)
        low_ffn = low(grad_ffn_res)
        grad_down = ein("rd,jrf->jdf", low_ffn, active)
        grad_active = ein("rd,jdf->jrf", low_ffn, w_down)
        slope = cdf + upper * jnp.exp(-0.5 * upper * upper) * (1.0 / math.sqrt(2.0 * math.pi))
        grad_upper = low(grad_active * slope)
        grad_up = ein("rd,jrf->jdf", normed_ffn, grad_upper)
        grad_normed = ein("jrf,jdf->rd", grad_upper, w_up)
        grad_inner, gain_two, bias_two = norm_backward(after_cross, gains[2], grad_normed)
        grad_cross_res = grad_ffn_res + grad_inner
        low_cross = low(grad_cross_res)
        grad_cross_out = ein("rd,re->de", cross_out, low_cross)[None]
        grad_mixed = low(ein("re,de->rd", low_cross, w_cross_out[0]))
        grad_query, grad_key, grad_value = attend_backward(
            cross_query, cross_text[0], cross_text[1], cross_probs, grad_mixed, clips
        )
        grad_w_query = ein("rd,re->de", normed_cross, grad_query)[None]
        grad_w_text = ein("td,kte->kde", text, jnp.stack([grad_key, grad_value]))
        grad_normed = ein("re,de->rd", grad_query, w_query[0])
        grad_inner, gain_one, bias_one = norm_backward(after_self, gains[1], grad_normed)
        grad_self_res = grad_cross_res + grad_inner
        low_self = low(grad_self_res)
        grad_self_out = ein("rd,re->de", self_out, low_self)[None]
        grad_mixed = low(ein("re,de->rd", low_self, w_self_out[0]))
        grad_proj = jnp.stack(
            attend_backward(proj[0], proj[1], proj[2], self_probs, grad_mixed, clips)
        )
        grad_w_self = ein("rd,kre->kde", normed_self, grad_proj)
        grad_normed = ein("kre,kde->rd", grad_proj, w_self)
        grad_inner, gain_zero, bias_zero = norm_backward(start, gains[0], grad_normed)
        grad_start = grad_self_res + grad_inner

        layer_grads = (
            grad_w_self, grad_self_out, grad_w_query, grad_w_text, grad_cross_out, grad_up, grad_down
        )
        norm_grads = jnp.stack(
            [gain_zero, gain_one, gain_two, gain_three, bias_zero, bias_one, bias_two, bias_three]
        )
        embed_sum = jnp.stack(
            [
                jax.ops.segment_sum(
                    grad_start, own_inputs[:, book].reshape(-1), num_segments=table_rows
                )
                for book in range(book_count)
            ]
        )
        embed_shard = lax.psum_scatter(embed_sum, BOTH, scatter_dimension=2, tiled=True)
        layer_shard = lax.psum_scatter(
            jnp.concatenate(layer_grads, axis=0), BOTH, scatter_dimension=1, tiled=True
        )
        head_shard = lax.psum_scatter(grad_head, "dp", scatter_dimension=1, tiled=True)
    big_gradients = (
        jnp.concatenate([layer_shard[0:3], layer_shard[4:7]], axis=0),
        jnp.concatenate([layer_shard[3:4], layer_shard[7:8]], axis=0),
        columns_together(layer_shard[8:], ffn_pieces),
        embed_shard,
        head_shard,
    )
    square_sum = jnp.zeros((), F32)
    for shard_grad in big_gradients:
        square_sum = square_sum + jnp.sum(shard_grad * shard_grad)
    if fast:
        scalars = jnp.pad(jnp.stack([square_sum, loss_sum])[None], ((0, 7), (0, model_width - 2)))
        totals = total_over_all(jnp.concatenate([norm_grads, scalars], axis=0))
        norm_total, square_total, loss_total = totals[:8], totals[8, 0], totals[8, 1]
    else:
        norm_total = lax.psum(norm_grads, BOTH)
        square_total, loss_total = lax.psum((square_sum, loss_sum), BOTH)
    square_total = square_total + jnp.sum(norm_total * norm_total)
    norm_width = norm_gain.shape[1]
    norm_shard = lax.dynamic_slice_in_dim(
        norm_total, (lax.axis_index("dp") * vocab_count + vocab_index) * norm_width, norm_width, 1
    )
    gradients = big_gradients + (norm_shard[:4], norm_shard[4:])
    loss_value = loss_total / denominator
    grad_norm = jnp.sqrt(square_total)
    factor = CLIP_LIMIT / jnp.maximum(grad_norm, CLIP_LIMIT)
    steps_float = step_count.astype(F32)
    corr_one = 1.0 - jnp.power(BETA_ONE, steps_float)
    corr_two = 1.0 - jnp.power(BETA_TWO, steps_float)
    masters = (in_proj, out_proj, ffn_proj, embed_table, head_table, norm_gain, norm_bias)
    mean_list = (
        in_proj_mean,
        out_proj_mean,
        ffn_proj_mean,
        embed_table_mean,
        head_table_mean,
        norm_gain_mean,
        norm_bias_mean,
    )
    square_list = (
        in_proj_sq,
        out_proj_sq,
        ffn_proj_sq,
        embed_table_sq,
        head_table_sq,
        norm_gain_sq,
        norm_bias_sq,
    )
    outputs = [loss_value, grad_norm]
    for index in range(7):
        outputs.extend(
            adam_step(
                masters[index],
                mean_list[index],
                square_list[index],
                gradients[index],
                factor,
                corr_one,
                corr_two,
            )
        )
    return tuple(outputs)


def solution(mesh):
    by_row = P(None, BOTH, None)
    by_column = P(None, None, BOTH)
    by_head = P(None, "dp", "vocab")
    by_feature = P(None, BOTH)
    weights = (
        (by_row,) * 9 + (by_column,) * 3 + (by_head,) * 3 + (by_feature,) * 6
    )
    placed = (
        P("dp", None, None),
        P("dp", None),
        P("dp"),
        P("dp", None),
        P("dp", None, None, None),
        P(BOTH, None, None),
        P(),
    ) + weights
    fast = dict(mesh.shape) == {"dp": 16, "vocab": 2}
    return jax.shard_map(
        functools.partial(local, fast),
        mesh=mesh,
        in_specs=placed,
        out_specs=(P(), P()) + weights,
        check_vma=False,
    )
```

time: 857 us -> 554 us (0.65)
  blocking collectives: 143 us -> 0 us
  matrix products: 108 us -> 0 us
  local copies, waits for them, and re-layouts: 72.9 us -> 13.4 us
  Pallas kernels: 430 us -> 487 us
  other arithmetic: 61.5 us -> 33.9 us
  between operations: 26.4 us -> 9.52 us
    all_gather x4 -> x0, blocking collectives: 104 us -> none  [the longest x1 68.9 us: local(): lax.all_gather(low(jnp.concatenate([norm_gain, norm_bias], axis=0)), BOTH...]
    dot_general x35 -> x0, matrix products: 100 us -> none  [the longest x34 97.5 us: ein(): return jnp.einsum(formula, left, right, preferred_element_type=F32)]
    pallas_call x3, Pallas kernels: 417 us -> 474 us  [the longest x1 242 us: forward_fast(): pl.pallas_call(functools.partial(forward_kernel, clips, denominator, spec...]
    psum x1 -> x0, blocking collectives: 39.6 us -> none  [local(): square_total, loss_total = lax.psum((square_sum, loss_sum), BOTH)]
    reduce_sum x9 -> x0, other arithmetic: 24.2 us -> none  [the longest x1 20.3 us: local(): jnp.sum((teach[:, :, :, None] == local_ids[None, None, None, :]).astype(F...]
    another operation x16 -> x1, local copies, waits for them, and re-layouts: 20.5 us -> 0.09 us  [local(): row_info = jnp.concatenate([valid, row_weight[None], owned[None]], axis=0).T]
    reshape x10 -> x2, local copies, waits for them, and re-layouts: 17.1 us -> 0.2 us  [the longest x1 0.13 us: local(): block_ids = kept.ids_all.reshape(device_count, clips, book_count, frames)...]
    unnamed x290 -> x72, local copies, waits for them, and re-layouts: 16.7 us -> 4.18 us
  transfers between devices with their start and end apart: 4 -> 1, of which waited for: 1 -> 1; matrix products, arithmetic and copies ran while one was open for 7% -> 1% of each run, Pallas kernels for 47% -> 0%
where the time goes in v2:
time: 554 us; the launch traced here: 552 us
  Pallas kernels  487 us (88%)
  other arithmetic  33.9 us (6%)
  local copies, waits for them, and re-layouts  13.4 us (2%)
  between operations  9.52 us (2%)
    pallas_call x1, Pallas kernels, forward_fast(): pl.pallas_call(functools.partial(forward_kernel, clips, denominator, spec...  242 us
    pallas_call x1, Pallas kernels, backward_fast(): pl.pallas_call(functools.partial(backward_kernel, clips), out_shape=(jax....  214 us
    pallas_call x1, Pallas kernels, total_over_all(): pl.pallas_call(total_kernel, out_shape=jax.ShapeDtypeStruct(value.shape,...  18 us
    pallas_call x1, Pallas kernels, spread_rows(): pl.pallas_call(spread_kernel, grid=(blocks,), out_shape=jax.ShapeDtypeStr...  12.9 us
  transfers between devices with their start and end apart: 1, of which 1 were waited for; matrix products, arithmetic and copies ran while one was open for 1% of the time, Pallas kernels for 0%

profile of v2, /device:TPU:0, one launch (start us, length us, event | category | flops | bytes accessed | tf_op | source)
XLA Modules:
  0.0 552.3 jit_solution(12484523110741989125)
XLA Ops:
  0.7 0.7 bitcast_or_fusion
  1.4 0.8 dynamic-slice_add_fusion
  2.3 0.7 fusion.10.refs_7_
  3.0 0.6 fusion.9.refs_2_
  3.6 0.7 broadcast_compare_fusion.4
  4.3 0.7 convert.22
  5.0 0.7 convert.21
  5.7 1.3 convert.23
  7.2 0.7 fusion.26
  8.4 0.9 convert_element_type.47.refs_4_
  9.3 0.9 fusion.8
  10.2 0.7 select_select_fusion
  11.2 1.2 gather_fusion
  12.7 1.0 subtract_bitcast_fusion
  14.3 0.6 pad_convert_fusion.refs_9_
  14.9 1.1 pad.19.refs_2_
  16.1 0.9 pad_maximum_fusion.2.refs_5_
  17.1 0.7 add_add_fusion.refs_8_
  17.9 242.5 %shard_map.443 = (s32[4,2,2,4,4,128]{5,4,3,2,1,0:T(4,128)}, f32[4,1024]{1,0:T(4,128)}, f32[8,128]{1,0:T(8,128)}, bf16[4,4,2,2,64,1024]{5,4,3,2,1,0:T(8,128)(2,1)...) custom-call(s32[4,4,128]{2,1,0:T(4,128)} %get-tuple-element.125.refs, ...), custom_call_target="tpu_custom_call" | custom-call | tf_op jit(solution)/shard_map/pallas_call | solution.py:1426
  260.4 213.7 %shard_map.444 = (f32[16,32,1024]{2,1,0:T(8,128)}, f32[4,2,32,1024]{3,2,1,0:T(8,128)}, f32[8,1024]{1,0:T(8,128)}, bf16[1024,256]{1,0:T(8,128)(2,1)}, bf16[20,4,2,2,32,1024]{5,4,3,2,1,0:T(8,128)(2,1)}) custom-call(bf16[4,128,1024]{2,1,0:T(8,128)(2,1)} %get-tuple-element.57.refs_0_, bf16[128,1024]{1,0:T(8,128)(2,1)} %bitcast.72, ...), custom_call_target="tpu_custom_call" | custom-call | tf_op jit(solution)/shard_map/pallas_call | solution.py:778
  474.1 4.8 all-to-all-start
  478.9 1.2 slice.94
  481.0 1.0 fusion.24
  482.0 0.7 multiply_reduce_fusion.4
  482.7 1.2 fusion.25
  483.9 0.7 copy-done.6
  484.6 0.8 multiply_reduce_fusion.3
  486.7 2.1 multiply_reduce_fusion.2
  489.5 0.9 multiply_reduce_fusion.1
  490.3 3.6 all-to-all-done.rows_ref
  493.9 12.9 %shard_map.445 = f32[4,32,2049]{2,1,0:T(8,128)S(1)} custom-call(s32[32,4,256]{2,1,0:T(4,128)S(1)} %reshape.226.ids_ref, bf16[32,32,256]{2,1,0:T(8,128)(2,1)S(1)} %all-to-all-done.rows_ref), custom_call_target="tpu_custom_call" | custom-call | tf_op jit(solution)/shard_map/pallas_call | solution.py:157
  506.8 0.9 multiply_reduce_fusion
  509.0 0.7 maximum_bitcast_fusion
  509.8 1.4 select_maximum_fusion.value_ref
  511.1 18.0 %shard_map.446 = f32[16,1024]{1,0:T(8,128)} custom-call(f32[16,1024]{1,0:T(8,128)} %select_maximum_fusion.value_ref), custom_call_target="tpu_custom_call" | custom-call | tf_op jit(solution)/shard_map/pallas_call | solution.py:102
  529.1 1.3 fusion.28
  530.5 1.4 fusion.27
  533.2 1.3 slice_multiply_fusion
  534.6 1.4 broadcast_multiply_fusion
  537.5 1.8 multiply_subtract_fusion.3
  539.4 1.0 multiply_subtract_fusion.4
  540.4 0.6 copy-done.10
  541.0 2.3 multiply_subtract_fusion
  543.3 0.7 copy-done.13
  544.0 2.2 multiply_subtract_fusion.2
  546.3 0.7 copy-done.15
  547.0 2.3 multiply_subtract_fusion.1
  549.4 0.6 multiply_subtract_fusion.5
  (98 shorter events, 3.2 us)
Async XLA Ops:
  0.7 6.3 %copy-start.16 = (f32[2,32,1024]{2,1,0:T(8,128)S(1)}, f32[2,32,1024]{2,1,0:T(8,128)}, u32[]{:S(2)}) copy-start(f32[2,32,1024]{2,1,0:T(8,128)} %param.38) | copy-start | bytes 786436
  5.7 1.5 copy-start.2
  7.1 1.3 copy-start.4
  8.4 1.8 copy-start.26
  8.4 4.1 copy-start.25
  8.4 4.1 copy-start.33
  10.2 4.7 copy-start
  14.9 1.1 copy-start.20
  16.1 1.7 copy-start.9
  17.1 0.8 copy-start.24
  474.1 6.0 %copy-start.23 = (s32[4,2,2,4,4,128]{5,4,3,2,1,0:T(4,128)S(1)}, s32[4,2,2,4,4,128]{5,4,3,2,1,0:T(4,128)}, u32[]{:S(2)}) copy-start(s32[4,2,2,4,4,128]{5,4,3,2,1,0:T(4,128)} %get-tuple-element.87) | copy-start | bytes 393220
  474.1 19.8 %all-to-all-start = ((bf16[32,32,256]{2,1,0:T(8,128)(2,1)}), bf16[32,32,256]{2,1,0:T(8,128)(2,1)S(1)}, u32[]{:S(2)}, u32[]{:S(2)}) async-start(bf16[32,32,256]{2,1,0:T(8,128)(2,1)} %bitcast.70), calls=%async_computation | async-start | bytes 1048576 | tf_op jit(solution)/shard_map/all_to_all | solution.py:1753
  483.9 0.7 copy-start.6
  483.9 5.6 %copy-start.1 = (f32[4,2,32,1024]{3,2,1,0:T(8,128)S(1)}, f32[4,2,32,1024]{3,2,1,0:T(8,128)}, u32[]{:S(2)}) copy-start(f32[4,2,32,1024]{3,2,1,0:T(8,128)} %get-tuple-element.89) | copy-start | bytes 3145732
  534.6 2.4 copy-start.19
  536.0 1.0 copy-start.7
  536.0 1.3 copy-start.8
  536.0 1.5 copy-start.18
  537.5 1.8 copy-start.17
  537.5 1.8 copy-start.21
  537.5 1.8 copy-start.22
  537.5 2.9 copy-start.11
  539.3 1.6 copy-start.10
  541.0 2.4 copy-start.3
  541.0 2.4 copy-start.12
  541.0 3.1 copy-start.13
  544.0 2.2 copy-start.5
  544.0 2.3 copy-start.14
  544.0 3.0 copy-start.15
  547.0 2.3 copy-start.27
  547.0 2.3 copy-start.28
  547.0 2.3 copy-start.29
  547.0 2.4 copy-start.30
  547.0 2.4 copy-start.31
  547.0 2.4 copy-start.32

commit v3 on v2

--- a/solution.py
+++ b/solution.py
@@ -23,6 +23,7 @@
 MESH = pl.DeviceIdType.MESH
 BF = jnp.bfloat16
 F32 = jnp.float32
+DEVICES = 32
 GROUPS = (3, 1, 1, 2, 1, 4, 4)
 UNITS = tuple((group, index) for group, size in enumerate(GROUPS) for index in range(size))
 
@@ -48,124 +49,31 @@
     )
 
 
-def greet(targets):
+def device_of(index):
+    return (lax.div(index, 2), lax.rem(index, 2))
+
+
+def greet_all(me):
     barrier = pltpu.get_barrier_semaphore()
-    for target in targets:
-        pl.semaphore_signal(barrier, inc=1, device_id=target, device_id_type=MESH)
-    pl.semaphore_wait(barrier, len(targets))
+
+    def signal(step, carry):
+        pl.semaphore_signal(
+            barrier, inc=1, device_id=device_of(lax.rem(me + step, DEVICES)), device_id_type=MESH
+        )
+        return carry
+
+    lax.fori_loop(1, DEVICES, signal, 0)
+    pl.semaphore_wait(barrier, DEVICES - 1)
 
 
 def transfer_order(heads):
     order, head = [], 0
     for unit in range(len(UNITS)):
-        order.append(("b" if unit % 4 == 3 else "a", unit))
+        order.append(("a", unit))
         if unit % 4 == 1 and head < heads:
             order.append(("h", head))
             head += 1
     return tuple(order)
-
-
-def total_kernel(value_ref, out_ref, landed, send_sem, recv_sem):
-    z, y, c, x = place()
-    line, z_dev, y_dev, x_dev, c_dev = partners()
-    greet(z_dev + [y_dev, x_dev, c_dev])
-
-    def copy(src, dst, slot, target):
-        return pltpu.make_async_remote_copy(
-            src_ref=src,
-            dst_ref=dst,
-            send_sem=send_sem.at[slot],
-            recv_sem=recv_sem.at[slot],
-            device_id=target,
-            device_id_type=MESH,
-        )
-
-    landed[z] = value_ref[...]
-    parts = [copy(value_ref, landed.at[z], k, z_dev[k]) for k in range(3)]
-    for part in parts:
-        part.start()
-    for part in parts:
-        part.wait()
-    landed[4] = landed[0] + landed[1] + landed[2] + landed[3]
-    for step, target in enumerate((y_dev, x_dev, c_dev)):
-        part = copy(landed.at[4 + 2 * step], landed.at[5 + 2 * step], 3 + step, target)
-        part.start()
-        part.wait()
-        summed = landed[4 + 2 * step] + landed[5 + 2 * step]
-        if step == 2:
-            out_ref[...] = summed
-        else:
-            landed[6 + 2 * step] = summed
-
-
-def total_over_all(value):
-    return pl.pallas_call(
-        total_kernel,
-        out_shape=jax.ShapeDtypeStruct(value.shape, F32),
-        in_specs=[pl.BlockSpec(memory_space=pltpu.VMEM)],
-        out_specs=pl.BlockSpec(memory_space=pltpu.VMEM),
-        scratch_shapes=[
-            pltpu.VMEM((10,) + value.shape, F32),
-            pltpu.SemaphoreType.DMA((6,)),
-            pltpu.SemaphoreType.DMA((6,)),
-        ],
-        compiler_params=pltpu.CompilerParams(collective_id=4, has_side_effects=True),
-    )(value)
-
-
-def spread_kernel(ids_ref, rows_ref, out_ref, total):
-    books, columns, rows = out_ref.shape
-    width = rows_ref.shape[2]
-    lanes = total.shape[2]
-    high_count = total.shape[1] // columns
-    step = pl.program_id(0)
-
-    @pl.when(step == 0)
-    def _():
-        total[...] = jnp.zeros_like(total)
-
-    values = rows_ref[0].astype(F32)
-    spread = lax.broadcasted_iota(jnp.int32, (lanes, width), 0)
-    for book in range(books):
-        ids = ids_ref[0, book : book + 1, :]
-        low = ids % lanes
-        high_ids = ids // lanes
-        hot = jnp.where(spread == low, 1.0, 0.0).astype(BF)
-        parted = jnp.concatenate(
-            [jnp.where(high_ids == high, values, 0.0) for high in range(high_count)], axis=0
-        ).astype(BF)
-        total[book] += lax.dot_general(
-            parted, hot, (((1,), (1,)), ((), ())), preferred_element_type=F32
-        )
-
-    @pl.when(step == pl.num_programs(0) - 1)
-    def _():
-        for book in range(books):
-            for high in range(high_count):
-                first = high * lanes
-                last = min(rows, first + lanes)
-                out_ref[book, :, first:last] = total[
-                    book, high * columns : (high + 1) * columns, : last - first
-                ]
-
-
-def spread_rows(ids, values, rows):
-    blocks, books, width = ids.shape
-    columns = values.shape[1]
-    lanes = 256
-    high_count = -(-rows // lanes)
-    return pl.pallas_call(
-        spread_kernel,
-        grid=(blocks,),
-        out_shape=jax.ShapeDtypeStruct((books, columns, rows), F32),
-        in_specs=[
-            pl.BlockSpec((1, books, width), lambda i: (i, 0, 0)),
-            pl.BlockSpec((1, columns, width), lambda i: (i, 0, 0)),
-        ],
-        out_specs=pl.BlockSpec((books, columns, rows), lambda i: (0, 0, 0)),
-        scratch_shapes=[pltpu.VMEM((books, high_count * columns, lanes), F32)],
-        compiler_params=pltpu.CompilerParams(vmem_limit_bytes=40 * 2**20),
-    )(ids, values)
 
 
 PAIR, RES3, FFN, MIX2, CROSS, TEXT, MIX1, SELF = range(8)
@@ -173,27 +81,28 @@
 RES2, QUERY2, KEY2, VALUE2, RES1, QUERY1, KEY1, VALUE1 = range(12, 20)
 PLAN = (
     ("h", 0, PAIR, LOGIT + 0),
+    ("h", 1, PAIR, LOGIT + 1),
+    ("h", 2, PAIR, LOGIT + 2),
+    ("h", 3, PAIR, LOGIT + 3),
     ("a", 12, RES3, ACT + 0),
     ("a", 13, RES3, ACT + 1),
-    ("h", 1, PAIR, LOGIT + 1),
+    ("a", 14, RES3, ACT + 2),
+    ("a", 15, RES3, ACT + 3),
     ("a", 8, FFN, UP + 0),
-    ("a", 14, RES3, ACT + 2),
-    ("b", 9, FFN, UP + 1),
-    ("a", 15, RES3, ACT + 3),
-    ("a", 10, FFN, UP + 2),
-    ("h", 2, PAIR, LOGIT + 2),
-    ("b", 11, FFN, UP + 3),
     ("a", 7, MIX2, RES2),
     ("a", 4, CROSS, QUERY2),
-    ("b", 5, TEXT, KEY2),
+    ("a", 5, TEXT, KEY2),
     ("a", 6, TEXT, VALUE2),
-    ("h", 3, PAIR, LOGIT + 3),
     ("a", 3, MIX1, RES1),
+    ("a", 9, FFN, UP + 1),
     ("a", 0, SELF, QUERY1),
-    ("b", 1, SELF, KEY1),
+    ("a", 1, SELF, KEY1),
     ("a", 2, SELF, VALUE1),
+    ("a", 10, FFN, UP + 2),
+    ("a", 11, FFN, UP + 3),
 )
 LATE = (2, 4, 6, 8)
+HEAD_LATE = (2, 10, 12, 13)
 
 
 def dot_nn(left, right):
@@ -244,7 +153,7 @@
     bias_out[...] = bias_sum
 
 
-def attend_back_rows(query, key, value, grad, query_out, key_out, value_out, clips, causal):
+def attend_back_rows(query, key, value, grad, query_out, key_out, value_out, clips, causal, share):
     rows, keys = query.shape[0] // clips, key.shape[0] // clips
     pairs = query.shape[1] // 128
     lane = lax.broadcasted_iota(jnp.int32, (1, 128), 1)
@@ -279,7 +188,8 @@
         value_out[at_k, lanes] = dv.astype(BF)
         return carry
 
-    lax.fori_loop(0, clips * pairs, pair, 0)
+    first, count = share[0] * clips * pairs // share[1], clips * pairs // share[1]
+    lax.fori_loop(first, first + count, pair, 0)
 
 
 class BackwardRefs(NamedTuple):
@@ -313,16 +223,23 @@
     w4: Any
     w5: Any
     w6: Any
-    layer_out: Any
+    ids_all: Any
+    loss: Any
+    in_out: Any
+    out_out: Any
+    ffn_out: Any
     head_out: Any
+    embed_out: Any
     norm_out: Any
-    start_out: Any
+    total_out: Any
     core_in: Any
-    first_in: Any
-    second_in: Any
+    diagonal_in: Any
+    side_in: Any
     line_in: Any
+    head_line: Any
+    head_send: Any
     head_y: Any
-    head_line: Any
+    head_held: Any
     core_slot: Any
     send_slot: Any
     held: Any
@@ -347,9 +264,17 @@
     pair_in: Any
     pick_in: Any
     gain_in: Any
-    pair_grad: Any
     pair_send: Any
     pair_land: Any
+    head_total: Any
+    norm_grads: Any
+    starts: Any
+    starts_in: Any
+    norms_in: Any
+    spread: Any
+    squares: Any
+    totals: Any
+    totals_in: Any
     send_sem: Any
     recv_sem: Any
     weight_sem: Any
@@ -357,11 +282,14 @@
     core_sem: Any
     upper_sem: Any
     pair_sem: Any
+    far_send: Any
+    far_recv: Any
 
 
 def backward_kernel(clips, *refs):
     r = BackwardRefs(*refs)
     z, y, c, x = place()
+    me = lax.axis_index("dp") * 2 + x
     line, z_dev, y_dev, x_dev, c_dev = partners()
     items = PLAN
     count = len(items)
@@ -398,9 +326,10 @@
 
     def weight_copy(index):
         ref, at = sequence[index]
-        return pltpu.make_async_copy(
-            ref.at[at], r.weight.at[index % slots], r.weight_sem.at[index % slots]
-        )
+        slot = r.weight.at[index % slots]
+        if ref is r.head:
+            slot = slot.at[:, 0 : ref.shape[2]]
+        return pltpu.make_async_copy(ref.at[at], slot, r.weight_sem.at[index % slots])
 
     for index in range(slots - 1):
         weight_copy(index).start()
@@ -420,11 +349,11 @@
 
     upper_copy(0).start()
     upper_copy(1).start()
-    greet(z_dev + [y_dev, x_dev, c_dev])
+    greet_all(me)
 
     left = (
         r.left_pair, r.left.at[0], r.left.at[1], r.left.at[2],
-        r.left.at[3], r.left_text, r.left.at[0], r.left.at[1],
+        r.left.at[3], r.left_text, r.left.at[0], r.left.at[2],
     )
     right = [r.logit.at[k] for k in range(pieces)]
     right += [r.acts.at[j] for j in range(pieces)] + [r.ups.at[j] for j in range(pieces)]
@@ -443,37 +372,67 @@
 
     held_slots = r.held.shape[0]
 
+    def head_cols(index):
+        return pl.ds(pl.multiple_of(index * part_size, part_size), part_size)
+
+    part_size = r.head_out.shape[3] // 2
+    half_cols = (pl.ds(0, part_size), pl.ds(part_size, part_size))
+
+    def used(ref, item):
+        return ref.at[:, :, :, :, half_cols[0]] if items[item][0] == "h" else ref
+
     def to_core(item):
-        return copy(r.send_slot.at[item % 2], r.core_in.at[item], item, 0, c_dev)
+        slot = r.send_slot.at[item % 2]
+        return copy(used(slot, item), used(r.core_in.at[item], item), item, 0, c_dev)
 
     def core_load(item):
+        slot = r.core_slot.at[item % 2]
         return pltpu.make_async_copy(
-            r.core_in.at[item], r.core_slot.at[item % 2], r.core_sem.at[item % 2]
-        )
+            used(r.core_in.at[item], item), used(slot, item), r.core_sem.at[item % 2]
+        )
+
+    def held_of(item):
+        kind, unit = items[item][:2]
+        return r.head_held.at[unit] if kind == "h" else r.held.at[item % held_slots]
 
     def first(item):
         kind, unit = items[item][:2]
-        held = r.held.at[item % held_slots]
-        if kind == "a":
-            return copy(held.at[:, :, 1 - x], r.first_in.at[unit], item, 1, x_dev)
-        target = r.head_y if kind == "h" else r.first_in
-        return copy(held.at[:, 1 - y], target.at[unit], item, 1, y_dev)
+        held = held_of(item)
+        if kind == "h":
+            return [
+                copy(
+                    held.at[other],
+                    r.head_line.at[unit, slot],
+                    item,
+                    1 + slot,
+                    z_dev[slot],
+                )
+                for slot, other in enumerate(line)
+            ]
+        diagonal = held.at[:, 1 - y, 1 - x]
+        return [
+            copy(diagonal.at[:, :, half_cols[n]], r.diagonal_in.at[unit, n], item, 1 + n, target)
+            for n, target in enumerate((x_dev, y_dev))
+        ]
 
     def second(item):
         kind, unit = items[item][:2]
         if kind == "h":
-            return None
-        if kind == "a":
-            return copy(r.first_in.at[unit, :, 1 - y], r.second_in.at[unit], item, 2, y_dev)
-        return copy(r.first_in.at[unit, :, 1 - x], r.second_in.at[unit], item, 2, x_dev)
+            return [copy(r.head_send.at[unit], r.head_y.at[unit], item, 4, y_dev)]
+        held = held_of(item)
+        return [
+            copy(held.at[:, 1 - y, x], r.side_in.at[unit, 0], item, 3, y_dev),
+            copy(held.at[:, y, 1 - x], r.side_in.at[unit, 1], item, 4, x_dev),
+        ]
 
     def third(item):
         kind, unit = items[item][:2]
-        ready, landed = (
-            (r.head_y, r.head_line) if kind == "h" else (r.second_in, r.line_in)
-        )
+        if kind == "h":
+            return []
         return [
-            copy(ready.at[unit, other], landed.at[unit, slot], item, 3 + slot, z_dev[slot])
+            copy(
+                r.side_in.at[unit, 0, other], r.line_in.at[unit, slot], item, 5 + slot, z_dev[slot]
+            )
             for slot, other in enumerate(line)
         ]
 
@@ -485,6 +444,9 @@
 
     def wide(value):
         return value.astype(F32)
+
+    def column_parts(item):
+        return 2 if items[item][0] == "h" else 4
 
     def make(item):
         kind, unit, left_name, right_name = items[item]
@@ -498,15 +460,16 @@
             slot[:, :, :, :, cols] = value.reshape(4, 2, 2, 32, 256)
             return carry
 
-        lax.fori_loop(0, 4, columns, 0)
+        lax.fori_loop(0, column_parts(item), columns, 0)
         to_core(item).start()
 
     def join_core(item):
         kind, unit, left_name, right_name = items[item]
         core_load(item).wait()
-        if item >= held_slots:
-            first(item - held_slots).wait_send()
-        held, landed = r.held.at[item % held_slots], r.core_slot.at[item % 2]
+        if item >= held_slots and items[item - held_slots][0] == "a":
+            for part in first(item - held_slots) + second(item - held_slots):
+                part.wait_send()
+        held, landed = held_of(item), r.core_slot.at[item % 2]
 
         def columns(n, carry):
             cols = chunk(n, 256)
@@ -515,54 +478,79 @@
             held[:, :, :, :, cols] = value.astype(BF)
             return carry
 
-        lax.fori_loop(0, 4, columns, 0)
-        first(item).start()
+        lax.fori_loop(0, column_parts(item), columns, 0)
+        for part in first(item):
+            part.start()
 
     def join_first(item):
         kind, unit = items[item][:2]
-        first(item).wait_recv()
-        held = r.held.at[item % held_slots]
-        target = r.head_y.at[unit] if kind == "h" else r.first_in.at[unit]
+        held = held_of(item)
+        for part in first(item):
+            part.wait_recv()
+        if kind == "h":
+            for side in range(2):
+                total = wide(held[z, side])
+                for slot in range(3):
+                    total = total + wide(r.head_line[unit, slot, side])
+                r.head_total[side] = total
+            own = r.head_total[y]
+            r.head_out[unit, :, :, head_cols(y)] = own
+            squared = own * own
+            r.squares[:, half_cols[0]] += squared[0] + squared[1]
+            r.head_send[unit] = r.head_total[1 - y].astype(BF)
+        else:
+
+            def planes(k, carry):
+                held[k, 1 - y, x, :, half_cols[0]] = (
+                    wide(held[k, 1 - y, x, :, half_cols[0]]) + wide(r.diagonal_in[unit, 0, k])
+                ).astype(BF)
+                held[k, y, 1 - x, :, half_cols[1]] = (
+                    wide(held[k, y, 1 - x, :, half_cols[1]]) + wide(r.diagonal_in[unit, 1, k])
+                ).astype(BF)
+                return carry
+
+            lax.fori_loop(0, 4, planes, 0)
+        for part in second(item):
+            part.start()
+
+    def join_second(item):
+        kind, unit = items[item][:2]
+        for part in second(item):
+            part.wait_recv()
+        if kind == "h":
+            other = wide(r.head_y[unit])
+            r.head_out[unit, :, :, head_cols(1 - y)] = other
+            squared = other * other
+            r.squares[:, half_cols[0]] += squared[0] + squared[1]
+            return
+        held = held_of(item)
 
         def planes(k, carry):
-            kept = held[k, :, x] if kind == "a" else held[k, y]
-            target[k] = (wide(target[k]) + wide(kept)).astype(BF)
+            total = wide(held[k, y, x]) + wide(r.side_in[unit, 0, k]) + wide(r.side_in[unit, 1, k])
+            r.side_in[unit, 0, k] = total.astype(BF)
             return carry
 
         lax.fori_loop(0, 4, planes, 0)
-        parts = third(item) if kind == "h" else [second(item)]
-        for part in parts:
+        for part in third(item):
             part.start()
 
-    def join_second(item):
+    def finish(item):
         kind, unit = items[item][:2]
         if kind == "h":
             return
-        second(item).wait_recv()
-
-        def planes(k, carry):
-            kept = r.first_in[unit, k, y if kind == "a" else x]
-            r.second_in[unit, k] = (wide(r.second_in[unit, k]) + wide(kept)).astype(BF)
-            return carry
-
-        lax.fori_loop(0, 4, planes, 0)
-        for part in third(item):
-            part.start()
-
-    def finish(item):
-        kind, unit = items[item][:2]
         for part in third(item):
             part.wait_recv()
-        if kind == "h":
-            total = wide(r.head_y[unit, z])
-            for slot in range(3):
-                total = total + wide(r.head_line[unit, slot])
-            r.head_out[unit] = total
+        total = wide(r.side_in[unit, 0, z])
+        for slot in range(3):
+            total = total + wide(r.line_in[unit, slot])
+        r.squares[...] += total * total
+        group, index = UNITS[unit]
+        if group in (1, 4):
+            r.out_out[group // 4] = total
+        elif group < 5:
+            r.in_out[(0, 0, 3, 4)[group] + index] = total
         else:
-            total = wide(r.second_in[unit, z])
-            for slot in range(3):
-                total = total + wide(r.line_in[unit, slot])
-            r.layer_out[unit] = total
+            r.ffn_out[group - 5, :, index * total.shape[1] : (index + 1) * total.shape[1]] = total
 
     ticks = [0]
 
@@ -573,10 +561,11 @@
         if 0 <= item < count:
             to_core(item).wait_recv()
             core_load(item).start()
-        for late, stage in zip(LATE, (join_core, join_first, join_second, finish)):
-            item = tick - late
-            if 0 <= item < count:
-                stage(item)
+        for stage_number, stage in enumerate((join_core, join_first, join_second, finish)):
+            for kind, late in (("h", HEAD_LATE), ("a", LATE)):
+                item = tick - late[stage_number]
+                if 0 <= item < count and items[item][0] == kind:
+                    stage(item)
 
     def unit(right_name):
         item = ticks[0]
@@ -584,41 +573,56 @@
         make(item)
         pump()
 
+    r.squares[...] = jnp.zeros_like(r.squares)
     load_logit.wait()
     load_pair.wait()
     r.left_pair[...] = r.pair_in[...].T
     unit(LOGIT + 0)
+    unit(LOGIT + 1)
 
     def pair_rows_of(k, w):
         def columns(n, carry):
             cols = chunk(n, 256)
-            value = dot_nt(r.logit[k], w[cols, :])
-            r.pair_grad[:, cols] = value if k == 0 else r.pair_grad[:, cols] + value
+            value = dot_nt(r.logit[k], w[cols, 0:part_size])
+            r.grad_h[:, cols] = value if k == 0 else r.grad_h[:, cols] + value
             return carry
 
         lax.fori_loop(0, 4, columns, 0)
 
     for k in range(pieces):
         pair_rows_of(k, next_weight())
-    half = r.pair_send.shape[0]
-    r.pair_send[...] = r.pair_grad[chunk(1 - x, half), :].astype(BF)
-    exchange = pltpu.make_async_remote_copy(
-        src_ref=r.pair_send,
-        dst_ref=r.pair_land,
-        send_sem=r.pair_sem.at[0],
-        recv_sem=r.pair_sem.at[1],
-        device_id=x_dev,
-        device_id_type=MESH,
-    )
-    exchange.start()
+    half = r.pair_send.shape[1]
+    mine = y * 2 + x
+    square = (y * 2 + 1 - x, (1 - y) * 2 + x, (1 - y) * 2 + 1 - x)
+    trade = []
+    for slot, (member, target) in enumerate(
+        zip(square, (x_dev, y_dev, device(z, 1 - y, c, 1 - x)), strict=True)
+    ):
+        r.pair_send[slot] = r.grad_h[chunk(member, half), :].astype(BF)
+        trade.append(
+            pltpu.make_async_remote_copy(
+                src_ref=r.pair_send.at[slot],
+                dst_ref=r.pair_land.at[slot],
+                send_sem=r.pair_sem.at[slot],
+                recv_sem=r.pair_sem.at[3 + slot],
+                device_id=target,
+                device_id_type=MESH,
+            )
+        )
+    for piece in trade:
+        piece.start()
+    unit(LOGIT + 2)
     load_h3.wait()
     r.left[1] = r.rows_in[0].T
     load_pick.wait()
     load_gains.wait()
     load_x3.wait()
     load_act.wait()
-    exchange.wait()
-    chosen = r.pair_grad[chunk(x, half), :].astype(BF).astype(F32) + wide(r.pair_land[...])
+    for piece in trade:
+        piece.wait()
+    chosen = r.grad_h[chunk(mine, half), :]
+    for slot in range(3):
+        chosen = chosen + wide(r.pair_land[slot])
     chosen_top = chosen.astype(BF)
     chosen_rest = (chosen - wide(chosen_top)).astype(BF)
     r.grad_h[...] = dot_nn(r.pick_in[...], chosen_top) + dot_nn(r.pick_in[...], chosen_rest)
@@ -631,11 +635,12 @@
             add,
             r.grad_x,
             low_ref,
-            r.norm_out.at[index : index + 1],
-            r.norm_out.at[4 + index : 5 + index],
+            r.norm_grads.at[index : index + 1],
+            r.norm_grads.at[4 + index : 5 + index],
         )
 
     norm_back(3, None, r.lows.at[0])
+    unit(LOGIT + 3)
     load_x2 = load(r.x2, r.values)
     r.left[0] = r.lows[0].T
     load_o2 = load(r.o2, r.rows_in.at[1])
@@ -675,20 +680,14 @@
     down_back(0)
     unit(ACT + 1)
     up_back(0)
-    unit(LOGIT + 1)
-    unit(UP + 0)
     down_back(1)
     unit(ACT + 2)
     up_back(1)
-    unit(UP + 1)
     down_back(2)
+    up_back(2)
+    down_back(3)
     unit(ACT + 3)
-    up_back(2)
-    unit(UP + 2)
-    down_back(3)
-    unit(LOGIT + 2)
     up_back(3)
-    unit(UP + 3)
     load_x2.wait()
     norm_back(2, r.grad_x, r.lows.at[1])
     load_x1 = load(r.x1, r.values)
@@ -696,7 +695,7 @@
     load_o2.wait()
     r.left[2] = r.rows_in[1].T
     load_o1 = load(r.o1, r.rows_in.at[1])
-    unit(RES2)
+    unit(UP + 0)
     for piece in (load_q2, load_k2, load_v2):
         piece.wait()
 
@@ -710,94 +709,221 @@
 
         lax.fori_loop(0, 4, columns, 0)
 
+    def cross_back(share):
+        attend_back_rows(
+            r.query2, r.kv2.at[0], r.kv2.at[1], r.lows.at[0],
+            r.query2_grad, r.kv2_grad.at[0], r.kv2_grad.at[1], clips, False, share,
+        )
+
     into_mixed(r.lows.at[1])
-    attend_back_rows(
-        r.query2, r.kv2.at[0], r.kv2.at[1], r.lows.at[0],
-        r.query2_grad, r.kv2_grad.at[0], r.kv2_grad.at[1], clips, False,
-    )
+    cross_back((0, 2))
+    unit(RES2)
+    cross_back((1, 2))
     load_h2.wait()
     r.left[3] = r.rows_in[0].T
-    load_text = load(r.text, r.pair_in)
+    load_text = load(r.text, r.pair_in.at[0 : r.text.shape[0]])
+    load_h1 = load(r.h1, r.rows_in.at[0])
     unit(QUERY2)
     load_text.wait()
-    r.left_text[...] = r.pair_in[...].T
-    load_h1 = load(r.h1, r.rows_in.at[0])
-    unit(KEY2)
+    r.left_text[...] = r.pair_in[0 : r.text.shape[0]].T
     into_grad_h(r.query2_grad, next_weight(), True)
-    unit(VALUE2)
     load_x1.wait()
     norm_back(1, r.grad_x, r.acts.at[3])
     load_x0 = load(r.x0, r.values)
-
     load_o1.wait()
     r.left[0] = r.rows_in[1].T
-    unit(LOGIT + 3)
-    unit(RES1)
+    unit(KEY2)
+
+    def self_back(share):
+        attend_back_rows(
+            r.qkv.at[0], r.qkv.at[1], r.qkv.at[2], r.lows.at[0],
+            r.acts.at[0], r.acts.at[1], r.acts.at[2], clips, True, share,
+        )
+
     for piece in (load_q1, load_k1, load_v1):
         piece.wait()
     into_mixed(r.acts.at[3])
-    attend_back_rows(
-        r.qkv.at[0], r.qkv.at[1], r.qkv.at[2], r.lows.at[0],
-        r.acts.at[0], r.acts.at[1], r.acts.at[2], clips, True,
-    )
+    self_back((0, 4))
+    unit(VALUE2)
+    self_back((1, 4))
+    self_back((2, 4))
+    unit(RES1)
+    self_back((3, 4))
+    unit(UP + 1)
     load_h1.wait()
-    r.left[1] = r.rows_in[0].T
+    r.left[2] = r.rows_in[0].T
+    into_grad_h(r.acts.at[0], next_weight(), True)
     unit(QUERY1)
-    into_grad_h(r.acts.at[0], next_weight(), True)
+    into_grad_h(r.acts.at[1], next_weight(), False)
+    into_grad_h(r.acts.at[2], next_weight(), False)
     unit(KEY1)
-    into_grad_h(r.acts.at[1], next_weight(), False)
-    unit(VALUE1)
-    into_grad_h(r.acts.at[2], next_weight(), False)
     load_x0.wait()
     norm_back(0, r.grad_x, r.lows.at[1])
-    r.start_out[...] = r.lows[1].T
-    while ticks[0] < count + LATE[-1]:
+    columns, lanes = r.starts.shape[1], r.spread.shape[2]
+    books, rows = r.embed_out.shape[0], r.starts.shape[2]
+    table_rows = r.embed_out.shape[2]
+    high_count = r.spread.shape[1] // columns
+    for group in range(r.starts.shape[0] // 4):
+        turned = r.lows[1, :, group * 128 : (group + 1) * 128].T
+        r.starts[4 * group : 4 * group + 4] = turned.reshape(4, columns, rows)
+
+    def far(src, dst, step, slot):
+        return pltpu.make_async_remote_copy(
+            src_ref=src,
+            dst_ref=dst,
+            send_sem=r.far_send.at[slot, step],
+            recv_sem=r.far_recv.at[slot, step],
+            device_id=device_of(lax.rem(me + step, DEVICES)),
+            device_id_type=MESH,
+        )
+
+    def start_copy(step):
+        return far(r.starts.at[lax.rem(me + step, DEVICES)], r.starts_in.at[me], step, 0)
+
+    def norm_copy(step):
+        group = lax.div(lax.rem(me + step, DEVICES), 4)
+        return far(r.norm_grads.at[:, chunk(group, 128)], r.norms_in.at[me], step, 1)
+
+    def total_copy(step):
+        return far(r.totals, r.totals_in.at[me], step, 2)
+
+    def each(action):
+        def body(step, carry):
+            action(step)
+            return carry
+
+        lax.fori_loop(1, DEVICES, body, 0)
+
+    def send_far(step):
+        start_copy(step).start()
+        norm_copy(step).start()
+
+    each(send_far)
+    r.starts_in[me] = r.starts[me]
+    r.norms_in[me] = r.norm_grads[:, chunk(lax.div(me, 4), 128)]
+    r.spread[...] = jnp.zeros_like(r.spread)
+    spread_code = lax.broadcasted_iota(jnp.int32, (lanes, rows), 0)
+
+    def spread_block(step, carry):
+        source = lax.rem(me - step + DEVICES, DEVICES)
+        dp, member = lax.div(source, 2), lax.rem(source, 2)
+        at = (lax.div(dp, 4), lax.rem(lax.div(dp, 2), 2), lax.rem(dp, 2))
+        values = wide(r.starts_in[source])
+        for book in range(books):
+            ids = jnp.concatenate(
+                [r.ids_all[(*at, clips * member + m, pl.ds(book, 1))] for m in range(clips)], axis=1
+            )
+            low_ids, high_ids = ids & (lanes - 1), lax.shift_right_logical(ids, 8)
+            hot = jnp.where(spread_code == low_ids, 1.0, 0.0).astype(BF)
+            parted = jnp.concatenate(
+                [jnp.where(high_ids == high, values, 0.0) for high in range(high_count)], axis=0
+            ).astype(BF)
+            r.spread[book] += dot_nt(parted, hot)
+        return carry
+
+    def wait_and_spread(step, carry):
+        start_copy(step).wait_recv()
+        return spread_block(step, carry)
+
+    unit(VALUE1)
+    spread_block(0, 0)
+    unit(UP + 2)
+    lax.fori_loop(1, 9, wait_and_spread, 0)
+    unit(UP + 3)
+    for share in range(1, 4):
+        lax.fori_loop(1 + 8 * share, min(9 + 8 * share, DEVICES), wait_and_spread, 0)
         pump()
+    embed_squares = jnp.zeros((columns, lanes), F32)
+    for book in range(books):
+        for high in range(high_count):
+            left_col = high * lanes
+            width = min(table_rows, left_col + lanes) - left_col
+            block = r.spread[book, high * columns : (high + 1) * columns, :]
+            r.embed_out[book, :, left_col : left_col + width] = block[:, :width]
+            embed_squares = embed_squares + block * block
+    each(lambda step: norm_copy(step).wait_recv())
+    norm_total = r.norms_in[0]
+    for other in range(1, DEVICES):
+        norm_total = norm_total + r.norms_in[other]
+    r.norm_out[...] = norm_total
+    lane = lax.broadcasted_iota(jnp.int32, norm_total.shape, 1)
+    norm_squares = jnp.where(lax.div(lane, columns) == lax.rem(me, 4), norm_total * norm_total, 0.0)
+    while ticks[0] < count + max(LATE[-1], HEAD_LATE[-1]):
+        pump()
+
+    sum_tile = norm_squares
+    for k in range(4):
+        for n in range(8):
+            sum_tile = sum_tile + r.squares[8 * k : 8 * k + 8, 128 * n : 128 * n + 128]
+        for n in range(lanes // 128):
+            sum_tile = sum_tile + embed_squares[8 * k : 8 * k + 8, 128 * n : 128 * n + 128]
+    r.totals[0] = sum_tile
+    r.totals[1] = r.loss[...]
+    each(lambda step: total_copy(step).start())
+    r.totals_in[me] = r.totals[...]
+    each(lambda step: total_copy(step).wait_recv())
+    total = r.totals_in[0]
+    for other in range(1, DEVICES):
+        total = total + r.totals_in[other]
+    r.total_out[...] = total
+
+    def far_done(step):
+        start_copy(step).wait_send()
+        norm_copy(step).wait_send()
+        total_copy(step).wait_send()
+
+    each(far_done)
     for item in range(count):
         if item >= count - 2:
             to_core(item).wait_send()
-        if item >= count - held_slots:
-            first(item).wait_send()
-        if items[item][0] != "h":
-            second(item).wait_send()
-        for part in third(item):
+        parts = third(item)
+        if items[item][0] == "h" or item >= count - held_slots:
+            parts = parts + first(item) + second(item)
+        for part in parts:
             part.wait_send()
 
 
-def backward_fast(clips, operands):
+def backward_fast(clips, table_rows, operands):
     named = BackwardRefs(*operands, *(None,) * (len(BackwardRefs._fields) - len(operands)))
     rows, width = named.x0.shape
     pair_count = named.pair_rows.shape[0]
     text_rows = named.text.shape[0]
-    books = named.head.shape[0]
+    books, codes = named.head.shape[0], named.head.shape[2]
     units, count = len(UNITS), len(PLAN)
     block = (32, width)
+    columns, lanes = width // DEVICES, 256
+    high_count = -(-table_rows // lanes)
     vmem, dma = pltpu.VMEM, pltpu.SemaphoreType.DMA
     any_spec, vmem_spec = pl.BlockSpec(memory_space=pl.ANY), pl.BlockSpec(memory_space=vmem)
-    held_slots = LATE[1] - LATE[0] + 1
+    held_slots = LATE[2] - LATE[0] + 1
     results = pl.pallas_call(
         functools.partial(backward_kernel, clips),
         out_shape=(
-            jax.ShapeDtypeStruct((units,) + block, F32),
+            jax.ShapeDtypeStruct((6,) + block, F32),
+            jax.ShapeDtypeStruct((2,) + block, F32),
+            jax.ShapeDtypeStruct((2, 32, 4 * width), F32),
             jax.ShapeDtypeStruct((books, 2) + block, F32),
-            jax.ShapeDtypeStruct((8, width), F32),
-            jax.ShapeDtypeStruct((width, rows), BF),
+            jax.ShapeDtypeStruct((books, columns, table_rows), F32),
+            jax.ShapeDtypeStruct((8, 128), F32),
+            jax.ShapeDtypeStruct((2, 8, 128), F32),
             jax.ShapeDtypeStruct((count, 4, 2, 2) + block, BF),
         ),
-        in_specs=[any_spec] * len(operands),
-        out_specs=(vmem_spec,) * 4 + (any_spec,),
+        in_specs=[any_spec] * (len(operands) - 2) + [vmem_spec] * 2,
+        out_specs=(vmem_spec,) * 7 + (any_spec,),
         scratch_shapes=[
-            vmem((units, 4, 2) + block, BF),
-            vmem((units, 4) + block, BF),
+            vmem((units, 2, 4, 32, width // 2), BF),
+            vmem((units, 2, 4) + block, BF),
             vmem((units, 3) + block, BF),
-            vmem((books, 4, 2) + block, BF),
-            vmem((books, 3, 2) + block, BF),
+            vmem((books, 3, 2, 2, 32, codes), BF),
+            vmem((books, 2, 32, codes), BF),
+            vmem((books, 2, 32, codes), BF),
+            vmem((books, 4, 2, 2, 32, codes), BF),
             vmem((2, 4, 2, 2) + block, BF),
             vmem((2, 4, 2, 2) + block, BF),
             vmem((held_slots, 4, 2, 2) + block, BF),
             vmem((4, rows, width), BF),
             vmem((4, rows, width), BF),
-            vmem((books, pair_count, width), BF),
+            vmem((books, pair_count, codes), BF),
             vmem((2, rows, width), F32),
             vmem((3, rows, width), BF),
             vmem((rows, width), BF),
@@ -816,23 +942,36 @@
             vmem((pair_count, width), BF),
             vmem(named.pick.shape, BF),
             vmem(named.gains.shape, F32),
-            vmem((pair_count, width), F32),
-            vmem((pair_count // 2, width), BF),
-            vmem((pair_count // 2, width), BF),
-            dma((count, 6)),
-            dma((count, 6)),
+            vmem((3, pair_count // 4, width), BF),
+            vmem((3, pair_count // 4, width), BF),
+            vmem((2, 2, 32, codes), F32),
+            vmem((8, width), F32),
+            vmem((DEVICES, columns, rows), BF),
+            vmem((DEVICES, columns, rows), BF),
+            vmem((DEVICES, 8, 128), F32),
+            vmem((books, high_count * columns, lanes), F32),
+            vmem(block, F32),
+            vmem((2, 8, 128), F32),
+            vmem((DEVICES, 2, 8, 128), F32),
+            dma((count, 8)),
+            dma((count, 8)),
             dma((2,)),
             dma((24,)),
             dma((2,)),
             dma((2,)),
-            dma((2,)),
+            dma((6,)),
+            dma((3, DEVICES)),
+            dma((3, DEVICES)),
         ],
         compiler_params=pltpu.CompilerParams(
             collective_id=2, has_side_effects=True, vmem_limit_bytes=60 * 2**20
         ),
     )(*operands)
-    layer_shard, head_shard, norm_grads, start_grad = results[:4]
-    return layer_shard, head_shard.reshape(books, -1, width), norm_grads, start_grad
+    return BackwardRefs(
+        *operands,
+        *results,
+        *(None,) * (len(BackwardRefs._fields) - len(operands) - len(results)),
+    )
 
 
 class ForwardRefs(NamedTuple):
@@ -877,6 +1016,8 @@
     upper: Any
     act: Any
     norms_all: Any
+    teach_all: Any
+    rows_all: Any
     norm_rows: Any
     stacked: Any
     looked: Any
@@ -896,6 +1037,7 @@
     logit_grads: Any
     stats: Any
     weight: Any
+    head_weight: Any
     send_sem: Any
     recv_sem: Any
     local_sem: Any
@@ -909,7 +1051,8 @@
     pair_recv: Any
 
 
-GATHER_LATE = (2, 4, 6, 7)
+GATHER_LATE = (3, 5, 7, 8)
+HOP_LATE = 1
 
 
 def norm_rows_low(values_ref, gain_ref, bias_ref, low_ref):
@@ -968,21 +1111,9 @@
     outs = (r.w0, r.w1, r.w2, r.w3, r.w4, r.w5, r.w6)
     columns, lanes = r.looked.shape[1], r.stacked.shape[2]
     high_count = r.stacked.shape[1] // columns
-    devices = 32
-
-    def device_of(index):
-        return (lax.div(index, 2), lax.rem(index, 2))
-
-    barrier = pltpu.get_barrier_semaphore()
-
-    def signal(step, carry):
-        pl.semaphore_signal(
-            barrier, inc=1, device_id=device_of(lax.rem(me + step, devices)), device_id_type=MESH
-        )
-        return carry
-
-    lax.fori_loop(1, devices, signal, 0)
-    pl.semaphore_wait(barrier, devices - 1)
+    devices = DEVICES
+
+    greet_all(me)
 
     def copy(src, dst, item, slot, target):
         return pltpu.make_async_remote_copy(
@@ -1002,48 +1133,83 @@
         pltpu.make_async_copy(r.layer.at[unit], whole(unit).at[z, y, c, x], r.local_sem.at[unit])
         for unit in range(len(UNITS))
     ]
+    part_size = r.head_own.shape[2] // 2
+
+    def part_cols(index):
+        return pl.ds(pl.multiple_of(index * part_size, part_size), part_size)
+
     own.append(
-        pltpu.make_async_copy(r.head_own, r.head.at[:, z, y, c], r.local_sem.at[len(UNITS)])
+        pltpu.make_async_copy(
+            r.head_own.at[:, :, part_cols(y)], r.head.at[:, z, y, c], r.local_sem.at[len(UNITS)]
+        )
     )
+    half_cols = (pl.ds(0, r.layer.shape[2] // 2), pl.ds(r.layer.shape[2] // 2, r.layer.shape[2] // 2))
 
     def first(item):
         kind, unit = order[item]
         if kind == "h":
-            src, dst = r.head_own.at[unit], r.head.at[unit, z, y, c]
-        else:
-            src, dst = r.layer.at[unit], whole(unit).at[z, y, c, x]
-        return [copy(src, dst, item, slot, target) for slot, target in enumerate(z_dev)]
+            src = r.head_own.at[unit, :, part_cols(1 - y)]
+            return [copy(src, r.head.at[unit, z, y, c], item, 0, y_dev)]
+        return []
+
+    def hop(item, number, side):
+        unit = order[item][1]
+        step = 1 if side == 0 else -1
+        target = device(lax.rem(z + step + 4, 4), y, c, x)
+        block = whole(unit).at[lax.rem(z - step * (number - 1) + 4, 4), y, c, x]
+        source = r.layer.at[unit] if number == 1 else block
+        part = copy(source, block, item, (0, 1, 2, 11, 12, 13)[3 * side + number - 1], target)
+        if side == 0:
+            return part, (z < 3) & (z - number + 1 >= 0), z - number >= 0
+        return part, (z > 0) & (z + number - 1 <= 3), z + number <= 3
+
+    def hop_start(item, number):
+        for side in range(2):
+            part, sends, lands = hop(item, number, side)
+            pl.when(sends)(part.start)
+
+    def hop_wait(item, number):
+        for side in range(2):
+            part, sends, lands = hop(item, number, side)
+            pl.when(lands)(part.wait_recv)
+
+    def hop_done(item):
+        for number in range(1, 4):
+            for side in range(2):
+                part, sends, lands = hop(item, number, side)
+                pl.when(sends)(part.wait_send)
 
     def second(item):
         kind, unit = order[item]
-        block = r.head.at[unit, :, y, c] if kind == "h" else whole(unit).at[:, y, c, x]
-        parts = [
-            copy(block, block, item, 3, x_dev if kind == "b" else y_dev),
-            copy(block, block, item, 6, c_dev),
+        if kind == "h":
+            block = r.head.at[unit, z, :, c]
+            return [copy(block, block, item, 1 + slot, target) for slot, target in enumerate(z_dev)]
+        block = whole(unit).at[:, y, c, x]
+        return [
+            copy(block, block, item, 3 + slot, target)
+            for slot, target in enumerate((y_dev, x_dev, c_dev))
         ]
-        if kind != "h":
-            parts.append(copy(block, block, item, 4, y_dev if kind == "b" else x_dev))
-        return parts
 
     def third(item):
         kind, unit = order[item]
         if kind == "h":
-            block = r.head.at[unit, :, 1 - y, c]
-        elif kind == "b":
-            block = whole(unit).at[:, y, c, 1 - x]
-        else:
-            block = whole(unit).at[:, 1 - y, c, x]
-        parts = [copy(block, block, item, 7, c_dev)]
-        if kind != "h":
-            parts.append(copy(block, block, item, 5, y_dev if kind == "b" else x_dev))
-        return parts
+            block = r.head.at[unit, :, :, c]
+            return [copy(block, block, item, 4, c_dev)]
+        from_y, from_x = whole(unit).at[:, 1 - y, c, x], whole(unit).at[:, y, c, 1 - x]
+        half_y, half_x = from_y.at[:, :, half_cols[0]], from_x.at[:, :, half_cols[1]]
+        return [
+            copy(half_y, half_y, item, 6, x_dev),
+            copy(half_x, half_x, item, 7, y_dev),
+            copy(from_y, from_y, item, 8, c_dev),
+            copy(from_x, from_x, item, 9, c_dev),
+        ]
 
     def fourth(item):
         kind, unit = order[item]
         if kind == "h":
             return []
-        block = whole(unit).at[:, 1 - y, c] if kind == "b" else whole(unit).at[:, :, c, 1 - x]
-        return [copy(block, block, item, 8, c_dev)]
+        block = whole(unit).at[:, 1 - y, c, 1 - x]
+        return [copy(block, block, item, 10, c_dev)]
 
     ticks = [0]
 
@@ -1053,26 +1219,37 @@
         if tick < count:
             for part in first(tick):
                 part.start()
+            if order[tick][0] == "a":
+                hop_start(tick, 1)
+        for number in (1, 2):
+            item = tick - HOP_LATE * number
+            if 0 <= item < count and order[item][0] == "a":
+                hop_wait(item, number)
+                hop_start(item, number + 1)
         item = tick - GATHER_LATE[0]
         if 0 <= item < count:
             for part in first(item):
                 part.wait_recv()
+            if order[item][0] == "a":
+                hop_wait(item, 3)
             for part in second(item):
                 part.start()
         item = tick - GATHER_LATE[1]
         if 0 <= item < count:
-            second(item)[0].wait_recv()
+            for part in second(item) if order[item][0] == "h" else second(item)[:2]:
+                part.wait_recv()
             for part in third(item):
                 part.start()
         item = tick - GATHER_LATE[2]
-        if 0 <= item < count:
-            for part in second(item)[2:] + third(item)[1:]:
+        if 0 <= item < count and order[item][0] != "h":
+            for part in third(item)[:2]:
                 part.wait_recv()
             for part in fourth(item):
                 part.start()
         item = tick - GATHER_LATE[3]
         if 0 <= item < count:
-            for part in [second(item)[1], third(item)[0]] + fourth(item):
+            late = third(item) if order[item][0] == "h" else second(item)[2:] + third(item)[2:]
+            for part in late + fourth(item):
                 part.wait_recv()
         advance_loads()
 
@@ -1081,38 +1258,38 @@
     def ticks_for(kind, unit):
         return item_of[kind, unit] + GATHER_LATE[3] + 1
 
-    def unit_kind(unit):
-        return "b" if unit % 4 == 3 else "a"
-
-    taken, loading = [0], [0]
+    taken, loading, heads_loading = [0], [0], [0]
     weight_slots = r.weight.shape[0]
-    sequence = [(unit_kind(unit), unit) for unit in range(len(UNITS))]
-    sequence += [("h", k) for k in range(books)]
-
-    def weight_copy(index):
-        kind, unit = sequence[index]
-        slot = index % weight_slots
-        if kind == "h":
-            src, dst = r.head.at[unit], r.weight.at[slot].reshape(r.head.shape[1:])
-        else:
-            src, dst = whole(unit), r.weight.at[slot].reshape(whole(unit).shape)
-        return pltpu.make_async_copy(src, dst, r.weight_sem.at[slot])
+
+    def weight_copy(unit):
+        slot = unit % weight_slots
+        return pltpu.make_async_copy(
+            whole(unit), r.weight.at[slot].reshape(whole(unit).shape), r.weight_sem.at[slot]
+        )
+
+    def head_copy(book):
+        return pltpu.make_async_copy(
+            r.head.at[book], r.head_weight.at[book], r.weight_sem.at[weight_slots + book]
+        )
 
     def advance_loads():
         while (
-            loading[0] < min(len(sequence), taken[0] + weight_slots)
-            and ticks_for(*sequence[loading[0]]) <= ticks[0]
+            loading[0] < min(len(UNITS), taken[0] + weight_slots)
+            and ticks_for("a", loading[0]) <= ticks[0]
         ):
             weight_copy(loading[0]).start()
             loading[0] += 1
+        while heads_loading[0] < books and ticks_for("h", heads_loading[0]) <= ticks[0]:
+            head_copy(heads_loading[0]).start()
+            heads_loading[0] += 1
 
     def next_weight():
-        index = taken[0]
-        while loading[0] <= index:
+        unit = taken[0]
+        while loading[0] <= unit:
             pump()
-        weight_copy(index).wait()
+        weight_copy(unit).wait()
         taken[0] += 1
-        return r.weight.at[index % weight_slots]
+        return r.weight.at[unit % weight_slots]
 
     stores = []
 
@@ -1133,6 +1310,11 @@
 
     for piece in own:
         piece.start()
+    r.teach_all[y] = r.teach[...]
+    r.rows_all[y] = r.row_info[...]
+    small_y = [small(r.teach_all.at[y], 11, y_dev), small(r.rows_all.at[y], 12, y_dev)]
+    for part in small_y:
+        part.start()
     r.ids_all[z, y, c] = r.ids[...]
     r.norms_all[z, y, c, x] = r.norms[...]
     small_stages = (
@@ -1208,20 +1390,27 @@
     look_block(0, 0)
     r.landed[me] = r.looked[0]
 
-    code = lax.broadcasted_iota(jnp.int32, (128, r.teach.shape[2]), 0)
+    for part_in in small_y:
+        part_in.wait()
+    code = lax.broadcasted_iota(jnp.int32, (128, r.teach.shape[2]), 0) + (x * 2 + y) * part_size
     teach_count = r.teach.shape[1] - 8
 
     def want(book):
         def block(index, carry):
             here = code + index * 128
-            total = jnp.zeros(here.shape, F32)
-            for i in range(teach_count):
-                total = total + jnp.where(here == r.teach[book, i : i + 1, :], 1.0, 0.0)
-            hit = jnp.where(here == r.teach[book, teach_count : teach_count + 1, :], 1.0, 0.0)
-            r.wanted[book, :, chunk(index, 128)] = (total * (1.0 / teach_count) + hit).T
+            for side in range(2):
+                total = jnp.zeros(here.shape, F32)
+                for i in range(teach_count):
+                    total = total + jnp.where(here == r.teach_all[side, book, i : i + 1, :], 1.0, 0.0)
+                hit = jnp.where(
+                    here == r.teach_all[side, book, teach_count : teach_count + 1, :], 1.0, 0.0
+                )
+                r.wanted[book, side * 128 : side * 128 + 128, chunk(index, 128)] = (
+                    total * (1.0 / teach_count) + hit
+                ).T
             return carry
 
-        lax.fori_loop(0, r.wanted.shape[2] // 128, block, 0)
+        lax.fori_loop(0, part_size // 128, block, 0)
 
     for book in range(books):
         want(book)
@@ -1318,57 +1507,73 @@
     store(r.xs.at[3], r.x3)
     norm(3, r.final)
     half = r.pair.shape[1]
-    r.pair[x] = dot_nn(r.pick[...], r.final[...]).astype(BF)
-
-    def exchange(ref, slot):
-        return pltpu.make_async_remote_copy(
-            src_ref=ref.at[x],
-            dst_ref=ref.at[x],
-            send_sem=r.pair_send.at[slot],
-            recv_sem=r.pair_recv.at[slot],
-            device_id=x_dev,
-            device_id_type=MESH,
-        )
+    mine = y * 2 + x
+    r.pair[mine] = dot_nn(r.pick[...], r.final[...]).astype(BF)
+
+    square = (x_dev, y_dev, device(z, 1 - y, c, 1 - x))
+
+    def exchange(ref, first_slot):
+        return [
+            pltpu.make_async_remote_copy(
+                src_ref=ref.at[mine],
+                dst_ref=ref.at[mine],
+                send_sem=r.pair_send.at[first_slot + slot],
+                recv_sem=r.pair_recv.at[first_slot + slot],
+                device_id=target,
+                device_id_type=MESH,
+            )
+            for slot, target in enumerate(square)
+        ]
 
     trade = exchange(r.pair, 0)
-    trade.start()
-    trade.wait()
-    pair_count = 2 * half
+    for piece in trade:
+        piece.start()
+    for piece in trade:
+        piece.wait()
+    pair_count = 4 * half
     stat_lane = lax.broadcasted_iota(jnp.int32, (pair_count, 128), 1)
     stats = jnp.zeros((pair_count, 128), F32)
     for k in range(books):
-        w = next_weight()
-
-        def part(n, carry):
+        while heads_loading[0] <= k:
+            pump()
+        head_copy(k).wait()
+
+        def logit_part(n, carry):
             cols = chunk(n, 256)
-            pair = jnp.concatenate([r.pair[0], r.pair[1]], axis=0)
-            r.logits[k, :, cols] = dot_nn(pair, w[:, cols])
+            pair = jnp.concatenate([r.pair[m] for m in range(4)], axis=0)
+            w = r.head_weight[k, :, :, :, :, cols].reshape(-1, 256)
+            r.logits[k, :, cols] = dot_nn(pair, w)
             return carry
 
-        lax.fori_loop(0, 4, part, 0)
+        lax.fori_loop(0, part_size // 256, logit_part, 0)
         highest = jnp.max(r.logits[k], axis=-1, keepdims=True)
         exp_sum = jnp.sum(jnp.exp(r.logits[k] - highest), axis=-1, keepdims=True)
         stats = jnp.where(stat_lane == k, highest, stats)
         stats = jnp.where(stat_lane == books + k, exp_sum, stats)
-    r.stats[x] = stats
-    trade = exchange(r.stats, 1)
-    trade.start()
-    store(r.pair.at[0], r.pair_rows.at[0])
-    store(r.pair.at[1], r.pair_rows.at[1])
-    trade.wait()
-    weight_col = r.row_info[:, books : books + 1]
-    owned = r.row_info[:, books + 1 : books + 2]
+    r.stats[mine] = stats
+    trade = exchange(r.stats, 3)
+    for piece in trade:
+        piece.start()
+    for m in range(4):
+        store(r.pair.at[m], r.pair_rows.at[m])
+    for piece in trade:
+        piece.wait()
+    row_info = jnp.concatenate([r.rows_all[0], r.rows_all[1]], axis=0)
+    weight_col = row_info[:, books : books + 1]
+    member = lax.div(lax.broadcasted_iota(jnp.int32, (pair_count, 1), 0), half)
+    owned = jnp.where(member == mine, 1.0, 0.0)
     loss_col = jnp.zeros((pair_count, 1), F32)
     for k in range(books):
-        valid = r.row_info[:, k : k + 1]
-        tops = [r.stats[m][:, k : k + 1] for m in range(2)]
-        sums = [r.stats[m][:, books + k : books + k + 1] for m in range(2)]
-        top = jnp.maximum(tops[0], tops[1])
-        log_total = top + jnp.log(sums[0] * jnp.exp(tops[0] - top) + sums[1] * jnp.exp(tops[1] - top))
+        valid = row_info[:, k : k + 1]
+        tops = [r.stats[m][:, k : k + 1] for m in range(4)]
+        sums = [r.stats[m][:, books + k : books + k + 1] for m in range(4)]
+        top = jnp.maximum(jnp.maximum(tops[0], tops[1]), jnp.maximum(tops[2], tops[3]))
+        exp_sum = sum(sums[m] * jnp.exp(tops[m] - top) for m in range(4))
+        log_total = top + jnp.log(exp_sum)
         loss_col = loss_col + owned * weight_col * (valid + 1.0) * log_total
         scaled = weight_col * (1.0 / denominator)
 
-        def part(n, total):
+        def grad_part(n, total):
             cols = chunk(n, 256)
             logits, wanted = r.logits[k, :, cols], r.wanted[k, :, cols]
             r.logit_grads[k, :, cols] = (
@@ -1376,7 +1581,7 @@
             ).astype(BF)
             return total + jnp.sum(wanted * logits, axis=-1, keepdims=True)
 
-        picked = lax.fori_loop(0, 4, part, jnp.zeros((pair_count, 1), F32))
+        picked = lax.fori_loop(0, part_size // 256, grad_part, jnp.zeros((pair_count, 1), F32))
         loss_col = loss_col - weight_col * picked
         store(r.logit_grads.at[k], r.grad_logits.at[k])
     r.loss[...] = jnp.broadcast_to(jnp.sum(loss_col, axis=0, keepdims=True), r.loss.shape)
@@ -1389,6 +1594,8 @@
     for item in range(count):
         for part in first(item) + second(item) + third(item) + fourth(item):
             part.wait_send()
+        if order[item][0] == "a":
+            hop_done(item)
     for piece in stores:
         piece.wait()
 
@@ -1397,8 +1604,8 @@
     named = ForwardRefs(*operands, *(None,) * (len(ForwardRefs._fields) - len(operands)))
     books, frames = named.ids.shape[1:]
     rows, width = clips * frames, named.layer.shape[2]
-    text_rows, pair_count = named.text.shape[0], named.teach.shape[2]
-    codes, columns = named.head_own.shape[2], named.table.shape[1]
+    text_rows, pair_count = named.text.shape[0], 2 * named.teach.shape[2]
+    codes, columns = named.head_own.shape[2] // 2, named.table.shape[1]
     lanes = 256
     high_count = named.table.shape[2] // lanes
     count = books + len(UNITS)
@@ -1415,9 +1622,9 @@
         shaped((8, 128), F32),
     )
     in_hbm = (
-        (shaped((books, 4, 2, 2) + named.head_own.shape[1:]),)
+        (shaped((books, 4, 2, 2, named.head_own.shape[1], codes)),)
         + tuple(shaped((size, 4, 2, 2, 2) + named.layer.shape[1:]) for size in GROUPS)
-        + (shaped((books, pair_count, codes)), shaped((2, pair_count // 2, width)))
+        + (shaped((books, pair_count, codes)), shaped((4, pair_count // 4, width)))
         + (shaped((rows, width), F32),) * 4
         + (shaped((rows, width)),) * 8
         + (shaped((text_rows, width)),) * 2
@@ -1430,6 +1637,8 @@
         out_specs=(vmem_spec,) * len(in_vmem) + (any_spec,) * len(in_hbm),
         scratch_shapes=[
             vmem((4, 2, 2, 2, 8, 128), F32),
+            vmem((2,) + named.teach.shape, jnp.int32),
+            vmem((2,) + named.row_info.shape, F32),
             vmem((8, width), F32),
             vmem((books, high_count * columns, lanes), BF),
             vmem((32, columns, rows), F32),
@@ -1443,23 +1652,24 @@
             vmem((pieces, rows, width), F32),
             vmem((pieces, rows, width), BF),
             vmem((rows, width), BF),
-            vmem((2, pair_count // 2, width), BF),
+            vmem((4, pair_count // 4, width), BF),
             vmem((books, pair_count, codes), F32),
             vmem((books, pair_count, codes), F32),
             vmem((books, pair_count, codes), BF),
-            vmem((2, pair_count, 128), F32),
+            vmem((4, pair_count, 128), F32),
             vmem((3, width, width), BF),
-            dma((count, 9)),
-            dma((count, 9)),
+            vmem((books, 4, 2, 2, named.head_own.shape[1], codes), BF),
+            dma((count, 14)),
+            dma((count, 14)),
             dma((len(UNITS) + 1,)),
-            dma((11,)),
-            dma((11,)),
+            dma((13,)),
+            dma((13,)),
             dma((32,)),
             dma((32,)),
-            dma((3,)),
-            dma((40,)),
-            dma((2,)),
-            dma((2,)),
+            dma((3 + books,)),
+            dma((44,)),
+            dma((6,)),
+            dma((6,)),
         ],
         compiler_params=pltpu.CompilerParams(
             collective_id=1, has_side_effects=True, vmem_limit_bytes=58 * 2**20
@@ -1678,14 +1888,13 @@
         table_t = jnp.pad(table_t, ((0, 0), (0, 0), (0, -table_rows % 256)))
         teach = jnp.concatenate(
             [
-                teacher_ids.transpose(1, 3, 0, 2).reshape(book_count, -1, pair_count) - vocab_base,
-                jnp.where(target_at == special, -1, target_at - vocab_base)[:, None, :],
+                teacher_ids.transpose(1, 3, 0, 2).reshape(book_count, -1, pair_count),
+                jnp.where(target_at == special, -1, target_at)[:, None, :],
                 jnp.full((book_count, 7, pair_count), -1, jnp.int32),
             ],
             axis=1,
         )
-        owned = (jnp.arange(pair_count) // (clips * pos_count) == vocab_index).astype(F32)
-        row_info = jnp.concatenate([valid, row_weight[None], owned[None]], axis=0).T
+        row_info = jnp.concatenate([valid, row_weight[None]], axis=0).T
         row_info = jnp.pad(row_info, ((0, 0), (0, 128 - row_info.shape[1])))
         kept = forward_fast(
             clips,
@@ -1704,21 +1913,16 @@
                 row_info,
             ),
         )
-        block_ids = (
-            kept.ids_all.reshape(device_count, clips, book_count, frames)
-            .transpose(0, 2, 1, 3)
-            .reshape(device_count, book_count, rows)
-        )
-        loss_sum = kept.loss[0, 0]
 
         def joined(part):
             return part.reshape(part.shape[0], -1, part.shape[-1])
 
-        layer_shard, head_shard, norm_grads, start_grad = backward_fast(
+        done = backward_fast(
             clips,
+            table_rows,
             (
                 kept.grad_logits,
-                kept.pair_rows.reshape(pair_count, model_width),
+                kept.pair_rows.reshape(-1, model_width),
                 pick.T.astype(BF),
                 kept.x0,
                 kept.x1,
@@ -1747,11 +1951,23 @@
                 joined(kept.w4),
                 joined(kept.w5),
                 joined(kept.w6),
+                kept.ids_all,
+                kept.loss,
             ),
         )
-        parted = start_grad.reshape(device_count, -1, rows)
-        parted = lax.all_to_all(parted, BOTH, 0, 0, tiled=True)
-        embed_shard = jnp.swapaxes(spread_rows(block_ids, parted, table_rows), 1, 2)
+        norm_shard = lax.dynamic_slice_in_dim(
+            done.norm_out, lax.rem(device_index, 128 // norm_width) * norm_width, norm_width, 1
+        )
+        gradients = (
+            done.in_out,
+            done.out_out,
+            done.ffn_out,
+            jnp.swapaxes(done.embed_out, 1, 2),
+            done.head_out.reshape(head_table.shape),
+            norm_shard[:4],
+            norm_shard[4:],
+        )
+        square_total, loss_total = jnp.sum(done.total_out[0]), done.total_out[1, 0, 0]
     else:
         norms = lax.all_gather(norms_local, BOTH, axis=1, tiled=True).astype(F32)
         table = lax.all_gather(low(embed_table), BOTH, axis=2, tiled=True)
@@ -1868,29 +2084,24 @@
             jnp.concatenate(layer_grads, axis=0), BOTH, scatter_dimension=1, tiled=True
         )
         head_shard = lax.psum_scatter(grad_head, "dp", scatter_dimension=1, tiled=True)
-    big_gradients = (
-        jnp.concatenate([layer_shard[0:3], layer_shard[4:7]], axis=0),
-        jnp.concatenate([layer_shard[3:4], layer_shard[7:8]], axis=0),
-        columns_together(layer_shard[8:], ffn_pieces),
-        embed_shard,
-        head_shard,
-    )
-    square_sum = jnp.zeros((), F32)
-    for shard_grad in big_gradients:
-        square_sum = square_sum + jnp.sum(shard_grad * shard_grad)
-    if fast:
-        scalars = jnp.pad(jnp.stack([square_sum, loss_sum])[None], ((0, 7), (0, model_width - 2)))
-        totals = total_over_all(jnp.concatenate([norm_grads, scalars], axis=0))
-        norm_total, square_total, loss_total = totals[:8], totals[8, 0], totals[8, 1]
-    else:
+        big_gradients = (
+            jnp.concatenate([layer_shard[0:3], layer_shard[4:7]], axis=0),
+            jnp.concatenate([layer_shard[3:4], layer_shard[7:8]], axis=0),
+            columns_together(layer_shard[8:], ffn_pieces),
+            embed_shard,
+            head_shard,
+        )
+        square_sum = jnp.zeros((), F32)
+        for shard_grad in big_gradients:
+            square_sum = square_sum + jnp.sum(shard_grad * shard_grad)
         norm_total = lax.psum(norm_grads, BOTH)
         square_total, loss_total = lax.psum((square_sum, loss_sum), BOTH)
-    square_total = square_total + jnp.sum(norm_total * norm_total)
-    norm_width = norm_gain.shape[1]
-    norm_shard = lax.dynamic_slice_in_dim(
-        norm_total, (lax.axis_index("dp") * vocab_count + vocab_index) * norm_width, norm_width, 1
-    )
-    gradients = big_gradients + (norm_shard[:4], norm_shard[4:])
+        square_total = square_total + jnp.sum(norm_total * norm_total)
+        norm_width = norm_gain.shape[1]
+        norm_shard = lax.dynamic_slice_in_dim(
+            norm_total, (lax.axis_index("dp") * vocab_count + vocab_index) * norm_width, norm_width, 1
+        )
+        gradients = big_gradients + (norm_shard[:4], norm_shard[4:])
     loss_value = loss_total / denominator
     grad_norm = jnp.sqrt(square_total)
     factor = CLIP_LIMIT / jnp.maximum(grad_norm, CLIP_LIMIT)

time: 554 us -> 483 us (0.87); the launches traced: 552 us -> 474 us
  Pallas kernels: 487 us -> 435 us
  other arithmetic: 33.9 us -> 21.9 us
    pallas_call x2 -> x0, Pallas kernels: 30.9 us -> none  [the longest x1 18 us: total_over_all(): pl.pallas_call(total_kernel, out_shape=jax.ShapeDtypeStruct(value.shape,...]
    pallas_call x1, Pallas kernels: 242 us -> 224 us  [forward_fast(): pl.pallas_call(functools.partial(forward_kernel, clips, denominator, spec...]
  transfers between devices with their start and end apart: 1 -> 0, of which waited for: 1 -> 0; matrix products, arithmetic and copies ran while one was open for 1% -> 0% of each run, Pallas kernels for 0% -> 0%
where the time goes in v3:
time: 483 us; the launch traced here: 474 us
  Pallas kernels  435 us (90%)
  other arithmetic  21.9 us (5%)
  local copies, waits for them, and re-layouts  10.7 us (2%)
  between operations  5.71 us (1%)
    pallas_call x1, Pallas kernels, forward_fast(): pl.pallas_call(functools.partial(forward_kernel, clips, denominator, spec...  224 us
    pallas_call x1, Pallas kernels, backward_fast(): pl.pallas_call(functools.partial(backward_kernel, clips), out_shape=(jax....  212 us
    sub x6, other arithmetic, adam_step(): return (weight - LEARN_RATE * update, first_next, second_next)  10.2 us

profile of v3, /device:TPU:0, one launch (start us, length us, event | category | flops | bytes accessed | tf_op | source)
XLA Modules:
  0.0 473.8 jit_solution(3078916612777327829)
XLA Ops:
  0.7 0.7 convert.20
  1.4 0.7 convert.21
  2.1 0.2 dynamic_update_slice.3.refs_1_
  2.3 0.0 copy-start.21
  2.3 1.3 convert_element_type.33
  3.6 0.0 copy-start.3
  3.7 1.0 copy-done.3
  5.0 1.0 copy-done.4
  6.0 0.7 select_select_fusion
  6.7 0.1 copy.61
  6.9 0.1 reshape.164
  6.9 1.2 gather_fusion
  8.2 0.1 copy.62
  8.3 0.1 broadcast_compare_fusion.1
  8.4 0.1 convert_element_type.36
  8.4 0.1 broadcast_in_dim_reshape.5
  8.5 0.1 copy.64
  8.7 0.6 pad_convert_fusion.refs_9_
  9.3 0.1 reshape.154
  9.5 0.1 copy.63
  9.6 0.1 pad.22.clone
  9.7 0.7 add_add_fusion.refs_8_
  10.4 0.1 dynamic-slice_add_fusion
  10.5 0.1 eq.48
  10.6 0.7 fusion.10.refs_7_
  11.3 0.9 fusion.8
  12.2 0.8 pad_maximum_fusion.1.refs_5_
  13.1 1.1 pad.15.refs_2_
  14.2 0.5 copy-done.1
  14.7 0.9 convert_element_type.34.refs_4_
  15.6 223.8 %shard_map.443 = (s32[4,2,2,4,4,128]{5,4,3,2,1,0:T(4,128)}, f32[4,1024]{1,0:T(4,128)}, f32[8,128]{1,0:T(8,128)}, bf16[4,4,2,2,64,512]{5,4,3,2,1,0:T(8,128)(2,1)}...) custom-call(s32[4,4,128]{2,1,0:T(4,128)} %get-tuple-element.125.refs, ...), custom_call_target="tpu_custom_call" | custom-call | tf_op jit(solution)/shard_map/pallas_call | solution.py:1633
  239.4 0.7 fusion.9.refs_2_
  240.1 211.7 %shard_map.444 = (f32[6,32,1024]{2,1,0:T(8,128)}, f32[2,32,1024]{2,1,0:T(8,128)}, f32[2,32,4096]{2,1,0:T(8,128)}, f32[4,2,32,1024]{3,2,1,0:T(8,128)}, f32[4,32,2...) custom-call(bf16[4,256,512]{2,1,0:T(8,128)(2,1)} %get-tuple-element.60.refs_0, ...), custom_call_target="tpu_custom_call" | custom-call | tf_op jit(solution)/shard_map/pallas_call | solution.py:899
  451.7 0.8 constant_dynamic-slice_fusion
  452.5 1.3 slice_reduce_fusion
  455.3 0.6 multiply_subtract_fusion.5
  455.9 1.3 broadcast_multiply_fusion
  457.3 2.3 multiply_subtract_fusion.1
  459.7 0.7 copy-done.7
  460.4 2.3 multiply_subtract_fusion
  462.7 0.8 copy-done.11
  463.4 0.3 copy-done.12
  463.8 2.2 multiply_subtract_fusion.2
  466.0 1.0 multiply_subtract_fusion.4
  467.0 0.4 copy-done.14
  467.4 0.2 copy-done.15
  467.6 1.8 multiply_subtract_fusion.3
  469.4 1.2 slice.68
  (74 shorter events, 0.4 us)
Async XLA Ops:
  2.3 1.4 copy-start.21
  3.6 1.1 copy-start.3
  3.6 1.1 copy-start.13
  4.8 1.2 copy-start.26
  4.8 1.2 copy-start.23
  4.8 2.0 copy-start.22
  4.9 3.4 copy-start.31
  4.9 4.5 copy-start.17
  5.0 1.0 copy-start.4
  9.4 3.6 copy-start
  13.1 1.7 copy-start.1
  240.0 215.2 %copy-start.24 = (f32[4,32]{1,0:T(4,128)S(1)}, f32[4,32]{1,0:T(4,128)}, u32[]{:S(2)}) copy-start(f32[4,32]{1,0:T(4,128)} %param.53) | copy-start | bytes 1540
  240.0 215.2 %copy-start.25 = (f32[4,32]{1,0:T(4,128)S(1)}, f32[4,32]{1,0:T(4,128)}, u32[]{:S(2)}) copy-start(f32[4,32]{1,0:T(4,128)} %param.50) | copy-start | bytes 1540
  240.0 215.2 %copy-start.27 = (f32[4,32]{1,0:T(4,128)S(1)}, f32[4,32]{1,0:T(4,128)}, u32[]{:S(2)}) copy-start(f32[4,32]{1,0:T(4,128)} %param.55) | copy-start | bytes 1540
  240.0 215.2 %copy-start.28 = (f32[4,32]{1,0:T(4,128)S(1)}, f32[4,32]{1,0:T(4,128)}, u32[]{:S(2)}) copy-start(f32[4,32]{1,0:T(4,128)} %param.54) | copy-start | bytes 1540
  240.0 215.2 %copy-start.29 = (f32[4,32]{1,0:T(4,128)S(1)}, f32[4,32]{1,0:T(4,128)}, u32[]{:S(2)}) copy-start(f32[4,32]{1,0:T(4,128)} %param.52) | copy-start | bytes 1540
  240.1 215.2 %copy-start.30 = (f32[4,32]{1,0:T(4,128)S(1)}, f32[4,32]{1,0:T(4,128)}, u32[]{:S(2)}) copy-start(f32[4,32]{1,0:T(4,128)} %param.51) | copy-start | bytes 1540
  455.3 2.0 copy-start.8
  455.3 2.0 copy-start.9
  457.3 2.3 copy-start.5
  457.3 2.3 copy-start.6
  457.3 3.0 copy-start.7
  460.4 2.3 copy-start.2
  460.4 2.3 copy-start.10
  460.4 3.1 copy-start.11
  460.4 3.4 copy-start.12
  463.7 2.2 copy-start.18
  463.8 2.2 copy-start.19
  463.8 2.2 copy-start.20
  463.8 3.2 copy-start.16
  466.0 1.4 copy-start.14
  466.0 1.7 copy-start.15

commit v4 on v3

--- a/solution.py
+++ b/solution.py
@@ -271,7 +271,6 @@
     starts: Any
     starts_in: Any
     norms_in: Any
-    spread: Any
     squares: Any
     totals: Any
     totals_in: Any
@@ -759,10 +758,11 @@
     unit(KEY1)
     load_x0.wait()
     norm_back(0, r.grad_x, r.lows.at[1])
-    columns, lanes = r.starts.shape[1], r.spread.shape[2]
+    columns, lanes = r.starts.shape[1], 256
     books, rows = r.embed_out.shape[0], r.starts.shape[2]
     table_rows = r.embed_out.shape[2]
-    high_count = r.spread.shape[1] // columns
+    high_count = -(-table_rows // lanes)
+    spread_rows = lanes
     for group in range(r.starts.shape[0] // 4):
         turned = r.lows[1, :, group * 128 : (group + 1) * 128].T
         r.starts[4 * group : 4 * group + 4] = turned.reshape(4, columns, rows)
@@ -801,7 +801,10 @@
     each(send_far)
     r.starts_in[me] = r.starts[me]
     r.norms_in[me] = r.norm_grads[:, chunk(lax.div(me, 4), 128)]
-    r.spread[...] = jnp.zeros_like(r.spread)
+    def book_cols(book, side):
+        return pl.ds((book % 2) * 512 + side * lanes, lanes)
+
+    r.upper_slot[...] = jnp.zeros_like(r.upper_slot)
     spread_code = lax.broadcasted_iota(jnp.int32, (lanes, rows), 0)
 
     def spread_block(step, carry):
@@ -818,7 +821,9 @@
             parted = jnp.concatenate(
                 [jnp.where(high_ids == high, values, 0.0) for high in range(high_count)], axis=0
             ).astype(BF)
-            r.spread[book] += dot_nt(parted, hot)
+            found = dot_nt(parted, hot)
+            r.upper_slot[book // 2, :, book_cols(book, 0)] += found[:spread_rows]
+            r.upper_slot[book // 2, 0:columns, book_cols(book, 1)] += found[spread_rows:]
         return carry
 
     def wait_and_spread(step, carry):
@@ -838,7 +843,9 @@
         for high in range(high_count):
             left_col = high * lanes
             width = min(table_rows, left_col + lanes) - left_col
-            block = r.spread[book, high * columns : (high + 1) * columns, :]
+            side = high * columns // spread_rows
+            row = high * columns - side * spread_rows
+            block = r.upper_slot[book // 2, row : row + columns, book_cols(book, side)]
             r.embed_out[book, :, left_col : left_col + width] = block[:, :width]
             embed_squares = embed_squares + block * block
     each(lambda step: norm_copy(step).wait_recv())
@@ -891,8 +898,7 @@
     books, codes = named.head.shape[0], named.head.shape[2]
     units, count = len(UNITS), len(PLAN)
     block = (32, width)
-    columns, lanes = width // DEVICES, 256
-    high_count = -(-table_rows // lanes)
+    columns = width // DEVICES
     vmem, dma = pltpu.VMEM, pltpu.SemaphoreType.DMA
     any_spec, vmem_spec = pl.BlockSpec(memory_space=pl.ANY), pl.BlockSpec(memory_space=vmem)
     held_slots = LATE[2] - LATE[0] + 1
@@ -949,7 +955,6 @@
             vmem((DEVICES, columns, rows), BF),
             vmem((DEVICES, columns, rows), BF),
             vmem((DEVICES, 8, 128), F32),
-            vmem((books, high_count * columns, lanes), F32),
             vmem(block, F32),
             vmem((2, 8, 128), F32),
             vmem((DEVICES, 2, 8, 128), F32),
@@ -1051,8 +1056,8 @@
     pair_recv: Any
 
 
-GATHER_LATE = (3, 5, 7, 8)
-HOP_LATE = 1
+GATHER_LATE = (5, 7, 9, 10)
+HOP_LATE = 2
 
 
 def norm_rows_low(values_ref, gain_ref, bias_ref, low_ref):
@@ -1071,7 +1076,7 @@
     lax.fori_loop(0, values_ref.shape[0] // size, block, 0)
 
 
-def attend_rows(query, key, value, out, clips, causal):
+def attend_rows(query, key, value, out, clips, causal, share):
     rows, keys = query.shape[0] // clips, key.shape[0] // clips
     pairs = query.shape[1] // 128
     lane = lax.broadcasted_iota(jnp.int32, (1, 128), 1)
@@ -1096,7 +1101,8 @@
         out[at_q, lanes] = total.astype(BF)
         return carry
 
-    lax.fori_loop(0, clips * pairs, pair, 0)
+    first, count = share[0] * clips * pairs // share[1], clips * pairs // share[1]
+    lax.fori_loop(first, first + count, pair, 0)
 
 
 def forward_kernel(clips, denominator, special, *refs):
@@ -1334,13 +1340,18 @@
             pump()
             for book in range(books):
                 for high in range(high_count):
-                    r.stacked[book, high * columns : (high + 1) * columns, :] = r.table[
-                        book, :, high * lanes : (high + 1) * lanes
+                    left = high * lanes
+                    size = min(r.table.shape[2], left + lanes) - left
+                    if size < lanes:
+                        r.stacked[book, high * columns : (high + 1) * columns, :] = jnp.zeros(
+                            (columns, lanes), BF
+                        )
+                    r.stacked[book, high * columns : (high + 1) * columns, 0:size] = r.table[
+                        book, :, left : left + size
                     ].astype(BF)
         for part in stage:
             part.wait()
-        if number == 2:
-            pump()
+        pump()
     for group in range(8):
         parts = [
             r.norms_all[group // 2, group % 2, j // 2, j % 2] for j in range(4)
@@ -1461,8 +1472,11 @@
     for k in range(3):
         product(r.hs.at[0], next_weight(), r.qkv.at[k])
         store(r.qkv.at[k], (r.q1, r.k1, r.v1)[k])
-    pump()
-    attend_rows(r.qkv.at[0], r.qkv.at[1], r.qkv.at[2], r.mixed.at[0], clips, True)
+    for share in range(4):
+        pump()
+        attend_rows(
+            r.qkv.at[0], r.qkv.at[1], r.qkv.at[2], r.mixed.at[0], clips, True, (share, 4)
+        )
     store(r.mixed.at[0], r.o1)
     residual(r.mixed.at[0], next_weight(), 0, 1)
     store(r.xs.at[1], r.x1)
@@ -1473,8 +1487,11 @@
     for k in range(2):
         product(r.text, next_weight(), r.kv2.at[k])
         store(r.kv2.at[k], (r.k2, r.v2)[k])
-    pump()
-    attend_rows(r.query2, r.kv2.at[0], r.kv2.at[1], r.mixed.at[1], clips, False)
+    for share in range(2):
+        pump()
+        attend_rows(
+            r.query2, r.kv2.at[0], r.kv2.at[1], r.mixed.at[1], clips, False, (share, 2)
+        )
     store(r.mixed.at[1], r.o2)
     residual(r.mixed.at[1], next_weight(), 1, 2)
     store(r.xs.at[2], r.x2)
@@ -1607,7 +1624,7 @@
     text_rows, pair_count = named.text.shape[0], 2 * named.teach.shape[2]
     codes, columns = named.head_own.shape[2] // 2, named.table.shape[1]
     lanes = 256
-    high_count = named.table.shape[2] // lanes
+    high_count = -(-named.table.shape[2] // lanes)
     count = books + len(UNITS)
     pieces = GROUPS[-1]
     vmem, dma = pltpu.VMEM, pltpu.SemaphoreType.DMA
@@ -1682,6 +1699,109 @@
     )
 
 
+def adam_kernel(chunks, *refs):
+    arrays = refs[:20]
+    totals, corrections = refs[20:22]
+    results = refs[22:37]
+    buffers, load_sem, store_sem = refs[37:42], refs[42], refs[43]
+    depth = buffers[0].shape[0]
+    seen = [0] * 5
+    places = []
+    for array, index in chunks:
+        places.append((array, index, seen[array] % depth))
+        seen[array] += 1
+
+    def loads(item):
+        array, index, slot = places[item]
+        return [
+            pltpu.make_async_copy(
+                arrays[5 * kind + array].at[index],
+                buffers[array].at[slot, kind],
+                load_sem.at[item, kind],
+            )
+            for kind in range(4)
+        ]
+
+    def stores(item):
+        array, index, slot = places[item]
+        return [
+            pltpu.make_async_copy(
+                buffers[array].at[slot, 4 + kind],
+                results[3 * array + kind].at[index],
+                store_sem.at[item, kind],
+            )
+            for kind in range(3)
+        ]
+
+    def last_use(item):
+        array, index, slot = places[item]
+        for other in range(item - 1, -1, -1):
+            if places[other][0] == array and places[other][2] == slot:
+                return other
+        return None
+
+    ahead = depth
+    for item in range(ahead):
+        for piece in loads(item):
+            piece.start()
+    norm = jnp.sqrt(
+        jnp.sum(jnp.sum(totals[0], axis=0, keepdims=True), axis=1, keepdims=True)
+    )
+    factor = CLIP_LIMIT / jnp.maximum(norm, CLIP_LIMIT)
+    one, two = corrections[0, 0:1, 0:1], corrections[1, 0:1, 0:1]
+    waited = set()
+    for item in range(len(places)):
+        array, index, slot = places[item]
+        for piece in loads(item):
+            piece.wait()
+        before = last_use(item)
+        if before is not None:
+            waited.add(before)
+            for piece in stores(before):
+                piece.wait()
+        buffer = buffers[array]
+
+        def block(n, carry):
+            rows = chunk(n, 8)
+            weight, first, second, grad = (buffer[slot, kind, rows, :] for kind in range(4))
+            clipped = grad * factor
+            first_next = BETA_ONE * first + (1.0 - BETA_ONE) * clipped
+            second_next = BETA_TWO * second + (1.0 - BETA_TWO) * clipped * clipped
+            update = first_next * one / (jnp.sqrt(second_next * two) + ADAM_EPS)
+            buffer[slot, 4, rows, :] = weight - LEARN_RATE * (update + DECAY_RATE * weight)
+            buffer[slot, 5, rows, :] = first_next
+            buffer[slot, 6, rows, :] = second_next
+            return carry
+
+        lax.fori_loop(0, buffer.shape[2] // 8, block, 0)
+        for piece in stores(item):
+            piece.start()
+        if item + ahead < len(places):
+            for piece in loads(item + ahead):
+                piece.start()
+    for item in range(len(places)):
+        if item not in waited:
+            for piece in stores(item):
+                piece.wait()
+
+
+def adam_fast(weights, firsts, seconds, grads, totals, corrections):
+    chunks = [(array, index) for array in (2, 4, 3, 0, 1) for index in range(weights[array].shape[0])]
+    any_spec, vmem_spec = pl.BlockSpec(memory_space=pl.ANY), pl.BlockSpec(memory_space=pltpu.VMEM)
+    results = pl.pallas_call(
+        functools.partial(adam_kernel, tuple(chunks)),
+        out_shape=tuple(
+            jax.ShapeDtypeStruct(part.shape, F32) for part in weights for kind in range(3)
+        ),
+        in_specs=[any_spec] * 20 + [vmem_spec] * 2,
+        out_specs=(any_spec,) * 15,
+        scratch_shapes=[pltpu.VMEM((4, 7) + part.shape[1:], F32) for part in weights]
+        + [pltpu.SemaphoreType.DMA((len(chunks), 4)), pltpu.SemaphoreType.DMA((len(chunks), 3))],
+        compiler_params=pltpu.CompilerParams(vmem_limit_bytes=56 * 2**20),
+    )(*weights, *firsts, *seconds, *grads, totals, corrections)
+    return [results[3 * array : 3 * array + 3] for array in range(5)]
+
+
 def low(values):
     return values.astype(BF)
 
@@ -1885,7 +2005,6 @@
             (0, lax.rem(device_index, 128 // norm_width) * norm_width),
         )
         table_t = jnp.swapaxes(embed_table, 1, 2)
-        table_t = jnp.pad(table_t, ((0, 0), (0, 0), (0, -table_rows % 256)))
         teach = jnp.concatenate(
             [
                 teacher_ids.transpose(1, 3, 0, 2).reshape(book_count, -1, pair_count),
@@ -1958,15 +2077,14 @@
         norm_shard = lax.dynamic_slice_in_dim(
             done.norm_out, lax.rem(device_index, 128 // norm_width) * norm_width, norm_width, 1
         )
-        gradients = (
+        big_gradients = (
             done.in_out,
             done.out_out,
             done.ffn_out,
-            jnp.swapaxes(done.embed_out, 1, 2),
+            done.embed_out,
             done.head_out.reshape(head_table.shape),
-            norm_shard[:4],
-            norm_shard[4:],
-        )
+        )
+        gradients = big_gradients + (norm_shard[:4], norm_shard[4:])
         square_total, loss_total = jnp.sum(done.total_out[0]), done.total_out[1, 0, 0]
     else:
         norms = lax.all_gather(norms_local, BOTH, axis=1, tiled=True).astype(F32)
@@ -2127,8 +2245,24 @@
         norm_gain_sq,
         norm_bias_sq,
     )
+    if fast:
+        corrections = jnp.broadcast_to(
+            jnp.stack([1.0 / corr_one, 1.0 / corr_two])[:, None, None], (2, 8, 128)
+        )
+        turned = [
+            [jnp.swapaxes(part, 1, 2) if index == 3 else part for index, part in enumerate(parts)]
+            for parts in (masters[:5], mean_list[:5], square_list[:5])
+        ]
+        stepped = adam_fast(*turned, big_gradients, done.total_out, corrections)
+        stepped = [
+            [jnp.swapaxes(part, 1, 2) if index == 3 else part for part in parts]
+            for index, parts in enumerate(stepped)
+        ]
     outputs = [loss_value, grad_norm]
     for index in range(7):
+        if fast and index < 5:
+            outputs.extend(stepped[index])
+            continue
         outputs.extend(
             adam_step(
                 masters[index],

time: 483 us -> 473 us (0.979)
  other arithmetic: 21.9 us -> 11.1 us
  Pallas kernels: 435 us -> 441 us
    pallas_call x0 -> x1, Pallas kernels: none -> 13.2 us  [adam_fast(): pl.pallas_call(functools.partial(adam_kernel, tuple(chunks)), out_shape=t...]
    sub x6 -> x1, other arithmetic: 10.2 us -> 0.62 us  [adam_step(): return (weight - LEARN_RATE * update, first_next, second_next)]
    pallas_call x1, Pallas kernels: 224 us -> 218 us  [forward_fast(): pl.pallas_call(functools.partial(forward_kernel, clips, denominator, spec...]
where the time goes in v4:
time: 473 us; the launch traced here: 464 us
  Pallas kernels  441 us (93%)
  other arithmetic  11.1 us (2%)
  local copies, waits for them, and re-layouts  5.96 us (1%)
  between operations  5.94 us (1%)
    pallas_call x1, Pallas kernels, forward_fast(): pl.pallas_call(functools.partial(forward_kernel, clips, denominator, spec...  218 us
    pallas_call x1, Pallas kernels, backward_fast(): pl.pallas_call(functools.partial(backward_kernel, clips), out_shape=(jax....  209 us
    pallas_call x1, Pallas kernels, adam_fast(): pl.pallas_call(functools.partial(adam_kernel, tuple(chunks)), out_shape=t...  13.2 us

profile of v4, /device:TPU:0, one launch (start us, length us, event | category | flops | bytes accessed | tf_op | source)
XLA Modules:
  0.0 463.8 jit_solution(2512444341502777795)
XLA Ops:
  0.7 0.0 copy-start.1
  0.7 0.8 convert.20
  1.4 0.7 convert.21
  2.1 0.2 dynamic_update_slice.3.refs_1_
  2.4 0.0 copy-start.5
  2.4 1.3 convert_element_type.31
  3.6 0.0 copy-start.3
  3.8 0.0 copy-start.10
  3.8 0.0 copy-start.7
  3.8 0.0 copy-start.6
  3.8 0.0 copy-start.15
  3.8 0.0 copy-start.4
  3.9 0.7 copy-done.3
  4.7 0.0 copy-start
  4.7 0.0 copy-start.2
  4.8 0.7 select_select_fusion
  5.5 0.1 copy.61
  5.7 0.0 copy-done.6
  5.7 0.1 reshape.166
  5.8 1.2 gather_fusion
  7.0 0.1 copy.62
  7.1 0.1 broadcast_compare_fusion.1
  7.2 0.1 convert_element_type.34
  7.3 0.1 broadcast_in_dim_reshape.5
  7.4 0.1 copy.64
  7.5 0.6 pad_convert_fusion.refs_9_
  8.1 0.1 reshape.155
  8.3 0.1 copy.63
  8.4 0.1 pad.19.clone
  8.5 0.7 add_add_fusion.refs_8_
  9.2 0.1 dynamic-slice_add_fusion
  9.3 0.1 eq.48
  9.4 0.7 fusion.3.refs_7_
  10.1 0.9 fusion.1
  11.0 0.8 pad_maximum_fusion.1.refs_5_
  11.9 0.9 convert_element_type.32.refs_4_
  12.7 218.2 %shard_map.443 = (s32[4,2,2,4,4,128]{5,4,3,2,1,0:T(4,128)}, f32[4,1024]{1,0:T(4,128)}, f32[8,128]{1,0:T(8,128)}, bf16[4,4,2,2,64,512]{5,4,3,2,1,0:T(8,128)(2,1)}...) custom-call(s32[4,4,128]{2,1,0:T(4,128)} %get-tuple-element.140.refs, ...), custom_call_target="tpu_custom_call" | custom-call | tf_op jit(solution)/shard_map/pallas_call | solution.py:1650
  231.0 0.7 fusion.2.refs_2_
  231.6 0.0 copy-start.13
  231.6 0.0 copy-start.14
  231.7 209.4 %shard_map.444 = (f32[6,32,1024]{2,1,0:T(8,128)}, f32[2,32,1024]{2,1,0:T(8,128)}, f32[2,32,4096]{2,1,0:T(8,128)}, f32[4,2,32,1024]{3,2,1,0:T(8,128)}, f32[4,32,2...) custom-call(bf16[4,256,512]{2,1,0:T(8,128)(2,1)} %get-tuple-element.75.refs_0, ...), custom_call_target="tpu_custom_call" | custom-call | tf_op jit(solution)/shard_map/pallas_call | solution.py:905
  441.0 0.8 constant_dynamic-slice_fusion
  441.8 1.3 slice_reduce_fusion
  444.6 0.6 multiply_subtract_fusion
  445.3 0.1 pad_maximum_fusion.2
  445.4 0.7 broadcast_in_dim.79.refs_21_
  446.0 13.2 %shard_map.445 = (f32[6,32,1024]{2,1,0:T(8,128)}, f32[6,32,1024]{2,1,0:T(8,128)}, f32[6,32,1024]{2,1,0:T(8,128)}, f32[2,32,1024]{2,1,0:T(8,128)}, f32[2,32,1024]...) custom-call(f32[6,32,1024]{2,1,0:T(8,128)} %refs_0_.1, ...), custom_call_target="tpu_custom_call" | custom-call | tf_op jit(solution)/shard_map/pallas_call | solution.py:1791
  459.2 1.2 slice.68
  (38 shorter events, 0.4 us)
Async XLA Ops:
  0.7 3.1 copy-start.1
  2.4 1.5 copy-start.5
  3.6 1.0 copy-start.3
  3.8 1.0 copy-start.10
  3.8 1.0 copy-start.7
  3.8 1.9 copy-start.6
  3.8 3.3 copy-start.15
  3.8 4.4 copy-start.4
  4.7 7.2 %copy-start = (f32[4,64,1024]{2,1,0:T(8,128)S(1)}, f32[4,64,1024]{2,1,0:T(8,128)}, u32[]{:S(2)}) copy-start(f32[4,64,1024]{2,1,0:T(8,128)} %refs_4_.1) | copy-start | bytes 3145732
  4.7 8.0 %copy-start.2 = (bf16[16,32,1024]{2,1,0:T(8,128)(2,1)}, bf16[16,32,1024]{2,1,0:T(8,128)(2,1)S(1)}, u32[]{:S(2)}) copy-start(bf16[16,32,1024]{2,1,0:T(8,128)(2,1)S(1)} %constant_dynamic-update-slice_fusion.refs_3_) | copy-start | bytes 3145732
  231.6 212.9 %copy-start.8 = (f32[4,32]{1,0:T(4,128)S(1)}, f32[4,32]{1,0:T(4,128)}, u32[]{:S(2)}) copy-start(f32[4,32]{1,0:T(4,128)} %param.53) | copy-start | bytes 1540
  231.6 212.9 %copy-start.9 = (f32[4,32]{1,0:T(4,128)S(1)}, f32[4,32]{1,0:T(4,128)}, u32[]{:S(2)}) copy-start(f32[4,32]{1,0:T(4,128)} %param.50) | copy-start | bytes 1540
  231.6 212.9 %copy-start.11 = (f32[4,32]{1,0:T(4,128)S(1)}, f32[4,32]{1,0:T(4,128)}, u32[]{:S(2)}) copy-start(f32[4,32]{1,0:T(4,128)} %param.55) | copy-start | bytes 1540
  231.6 212.9 %copy-start.12 = (f32[4,32]{1,0:T(4,128)S(1)}, f32[4,32]{1,0:T(4,128)}, u32[]{:S(2)}) copy-start(f32[4,32]{1,0:T(4,128)} %param.54) | copy-start | bytes 1540
  231.6 212.9 %copy-start.13 = (f32[4,32]{1,0:T(4,128)S(1)}, f32[4,32]{1,0:T(4,128)}, u32[]{:S(2)}) copy-start(f32[4,32]{1,0:T(4,128)} %param.52) | copy-start | bytes 1540
  231.6 212.9 %copy-start.14 = (f32[4,32]{1,0:T(4,128)S(1)}, f32[4,32]{1,0:T(4,128)}, u32[]{:S(2)}) copy-start(f32[4,32]{1,0:T(4,128)} %param.51) | copy-start | bytes 1540
